TPU v7x, 256 devices: a whole 4x4x8 slice. The times are simulated.
256 devices in a mesh: ctx: 32 (over z, x), chan: 4 (over y), section: 2 (over core).
Axes of the slice: x: 4, y: 4, z: 8, core: 2. Of those that a mesh axis runs over, the one named last changes fastest.
Arguments:
- signal: bfloat16 [16384, 4096], P(('section', 'ctx'), 'chan'), parts along dimension 0, may hold values from -60 to 60
- gating: bfloat16 [16384, 4096], P(('section', 'ctx'), 'chan'), parts along dimension 0, may hold values from -6 to 6
- filters: float32 [16384, 4096], P(('section', 'ctx'), 'chan'), parts along dimension 0, may hold values from -2 to 2
- skip_gain: float32 [8192], P(('section', 'chan')), parts along dimension 0, may hold values from 0.5 to 1.5
Outputs:
- output: bfloat16 [16384, 4096], P(('section', 'ctx'), 'chan'), parts along dimension 0
- cosine: float32 [16384], P(('section', 'ctx')), parts along dimension 0
There are 2 independent parts, one for each index of `section`. A program takes and returns all parts, laid end to end along the dimension named above; each array names one. Nothing has to cross between parts.
All inputs are finite; a program needn't handle non-finite values.
Results may differ from a plain program's by a relative error of at most 0.011.
Values may be sent and summed in bfloat16 or wider, within the bound.
No kernel may reach another device: no remote copies, remote signals or barrier semaphores. Data moves between devices by JAX's collectives and lax.ppermute only.
A program may use at most 128 MiB of HBM per device.

v0:
```python
import math

import jax
import jax.numpy as jnp
import ml_dtypes
import numpy as np
from jax import lax
from jax.experimental import pallas as pl
from jax.experimental.pallas import tpu as pltpu
from jax.sharding import PartitionSpec as P

EPSILON = 1e-06
VMEM_LIMIT = 56 * 2**20
GROUP = 16


def conv_tables(blocks, span):
    total = blocks * span
    n1 = np.arange(blocks)
    n2 = np.arange(span)
    outer = 2 * np.pi * np.outer(4 * n1 + 1, n1) / (4 * blocks)
    twiddle = 2 * np.pi * np.outer(4 * n1 + 1, n2) / (4 * total)
    inner = 2 * np.pi * np.outer(n2, n2) / span
    eye = np.eye(GROUP)
    fwd_outer = np.concatenate([np.kron(np.cos(outer), eye), np.kron(-np.sin(outer), eye)], axis=0)
    inv_outer = np.concatenate(
        [np.kron(np.cos(outer.T), eye), np.kron(-np.sin(outer.T), eye)], axis=1
    )
    cos, sin = np.cos(inner), np.sin(inner)
    fwd_inner = np.block([[cos, -sin], [sin, cos]])
    inv_inner = np.block([[cos, sin], [-sin, cos]]) / total
    short = [t.astype(ml_dtypes.bfloat16) for t in (fwd_outer, inv_outer, fwd_inner, inv_inner)]
    wide = [np.cos(twiddle).astype(np.float32), np.sin(twiddle).astype(np.float32)]
    return short + wide


def dot(left, right):
    return jnp.dot(left, right, preferred_element_type=jnp.float32)


def prepare_kernel(sig_ref, fil_ref, out_ref, sq_ref):
    count, _, width, span = out_ref.shape
    sig = sig_ref[...]
    out_ref[:, 0] = sig.T.reshape(count, width, span)
    fil = fil_ref[...].astype(jnp.bfloat16)
    out_ref[:, 1] = fil.T.reshape(count, width, span)
    wide = sig.astype(jnp.float32)
    sq_ref[...] = token_sums(wide * wide)


def token_sums(terms):
    tokens, channels = terms.shape
    lanes = min(128, channels)
    part = terms[:, :lanes]
    for start in range(lanes, channels, lanes):
        part = part + terms[:, start : start + lanes]
    return jnp.sum(part.T, axis=0, keepdims=True)


def conv_kernel(in_ref, fo_ref, io_ref, fi_ref, ii_ref, cos_ref, sin_ref, out_ref):
    blocks, _, width, span = in_ref.shape
    rows = blocks * GROUP
    cos = jnp.broadcast_to(cos_ref[...][:, None, :], (blocks, GROUP, span)).reshape(rows, span)
    sin = jnp.broadcast_to(sin_ref[...][:, None, :], (blocks, GROUP, span)).reshape(rows, span)

    def spectrum(operand):
        outer = dot(fo_ref[...], operand)
        re, im = outer[:rows], outer[rows:]
        turned = jnp.concatenate([re * cos + im * sin, im * cos - re * sin], axis=1)
        both = dot(turned.astype(jnp.bfloat16), fi_ref[...])
        return both[:, :span], both[:, span:]

    for start in range(0, width, GROUP):
        sig = in_ref[:, 0, start : start + GROUP, :].reshape(rows, span)
        fil = in_ref[:, 1, start : start + GROUP, :].reshape(rows, span)
        sig_re, sig_im = spectrum(sig)
        fil_re, fil_im = spectrum(fil)
        prod = jnp.concatenate(
            [sig_re * fil_re - sig_im * fil_im, sig_re * fil_im + sig_im * fil_re], axis=1
        )
        back = dot(prod.astype(jnp.bfloat16), ii_ref[...])
        re, im = back[:, :span], back[:, span:]
        turned = jnp.concatenate([re * cos - im * sin, re * sin + im * cos], axis=0)
        conv = dot(io_ref[...], turned.astype(jnp.bfloat16))
        out_ref[:, start : start + GROUP, :] = conv.astype(jnp.bfloat16).reshape(blocks, GROUP, span)


def finish_kernel(conv_ref, sig_ref, gate_ref, skip_ref, out_ref, sums_ref):
    count, width, span = conv_ref.shape
    conv = conv_ref[...].reshape(count * width, span).T.astype(jnp.float32)
    sig = sig_ref[...].astype(jnp.float32)
    mixed = gate_ref[...].astype(jnp.float32) * (conv + skip_ref[...] * sig)
    out_ref[...] = mixed.astype(jnp.bfloat16)
    sums_ref[0:1] = token_sums(sig * mixed)
    sums_ref[1:2] = token_sums(mixed * mixed)


def call(kernel, out_shape, **kwargs):
    return pl.pallas_call(
        kernel,
        out_shape=out_shape,
        compiler_params=pltpu.CompilerParams(vmem_limit_bytes=VMEM_LIMIT),
        **kwargs,
    )


def local(signal, gating, filters, skip_gain):
    count = lax.axis_size("ctx")
    span, channels = signal.shape
    width = channels // count
    bf16, f32 = jnp.bfloat16, jnp.float32
    packed, sig_sq = call(
        prepare_kernel,
        (
            jax.ShapeDtypeStruct((count, 2, width, span), bf16),
            jax.ShapeDtypeStruct((1, span), f32),
        ),
    )(signal, filters)
    received = lax.all_to_all(packed, "ctx", split_axis=0, concat_axis=0, tiled=True)
    conv = call(conv_kernel, jax.ShapeDtypeStruct((count, width, span), bf16))(
        received, *conv_tables(count, span)
    )
    returned = lax.all_to_all(conv, "ctx", split_axis=0, concat_axis=0, tiled=True)
    result, sums = call(
        finish_kernel,
        (jax.ShapeDtypeStruct((span, channels), bf16), jax.ShapeDtypeStruct((2, span), f32)),
    )(returned, signal, gating, skip_gain.reshape(1, channels))
    sig_total = lax.psum(sig_sq[0], "chan")
    inner_total, out_total = lax.psum((sums[0], sums[1]), "chan")
    cosine = inner_total / jnp.sqrt((sig_total + EPSILON) * (out_total + EPSILON))
    return (result, cosine)


def solution(mesh):
    return jax.shard_map(
        local,
        mesh=mesh,
        in_specs=(
            P(("section", "ctx"), "chan"),
            P(("section", "ctx"), "chan"),
            P(("section", "ctx"), "chan"),
            P(("section", "chan")),
        ),
        out_specs=(P(("section", "ctx"), "chan"), P(("section", "ctx"))),
        check_vma=False,
    )
```

profile of v0, /device:TPU:32, one launch (start us, length us, event | category | flops | bytes accessed | tf_op | source)
XLA Modules:
  0.0 87.4 jit_solution(14590875379640918442)
XLA Ops:
  0.6 2.7 %shard_map.113 = (bf16[32,2,32,256]{3,2,1,0:T(8,128)(2,1)}, f32[1,256]{1,0:T(1,128)}) custom-call(bf16[256,1024]{1,0:T(8,128)(2,1)} %sig_ref.3, f32[256,1024]{1,0:T(8,128)} %fil_ref.1), custom_call_target="tpu_custom_call" | custom-call | tf_op jit(solution)/shard_map/pallas_call | solution.py:112
  3.4 38.6 %all_to_all.10.in_ref = bf16[32,2,32,256]{3,2,1,0:T(8,128)(2,1)} all-to-all(bf16[32,2,32,256]{3,2,1,0:T(8,128)(2,1)} %get-tuple-element.6), channel_id=1, replica_groups=mesh['ctx'=32,'chan'=4,'section'=2] {'ctx'}, dimensions={0} | all-to-all | bytes 2097152 | tf_op jit(solution)/shard_map/all_to_all | solution.py:119
  41.9 7.6 %shard_map.114 = bf16[32,32,256]{2,1,0:T(8,128)(2,1)} custom-call(bf16[32,2,32,256]{3,2,1,0:T(8,128)(2,1)} %all_to_all.10.in_ref, bf16[1024,512]{1,0:T(8,128)(2,1)} %constant.14.clone.fo_ref, bf16[512,1024]{1,0:T(8,128)(2,1)} %constant.15.clone.io_ref, bf16[512,512]{1,0:T(8,128)(2,1)} %constant.16.clone.fi_ref, bf16[512,512]{1,0:T(8,128)(2,1)} %constant.17.clone.ii_ref, ...), custom_call_target="tpu_custom_call" | custom-call | tf_op jit(solution)/shard_map/pallas_call | solution.py:120
  49.5 22.7 %all_to_all.11.conv_ref = bf16[32,32,256]{2,1,0:T(8,128)(2,1)} all-to-all(bf16[32,32,256]{2,1,0:T(8,128)(2,1)} %shard_map.114), channel_id=1, replica_groups=mesh['ctx'=32,'chan'=4,'section'=2] {'ctx'}, dimensions={0} | all-to-all | bytes 1048576 | tf_op jit(solution)/shard_map/all_to_all | solution.py:123
  72.2 2.5 %shard_map.115 = (bf16[256,1024]{1,0:T(8,128)(2,1)}, f32[2,256]{1,0:T(2,128)}) custom-call(bf16[32,32,256]{2,1,0:T(8,128)(2,1)} %all_to_all.11.conv_ref, bf16[256,1024]{1,0:T(8,128)(2,1)} %sig_ref.3, bf16[256,1024]{1,0:T(8,128)(2,1)} %gate_ref.1, f32[1,1024]{1,0:T(1,128)} %bitcast.4), custom_call_target="tpu_custom_call" | custom-call | tf_op jit(solution)/shard_map/pallas_call | solution.py:124
  74.7 0.7 fusion
  75.5 0.0 copy-start
  75.5 0.7 copy-done
  76.1 10.7 %all-reduce = (f32[256]{0:T(256)S(1)}, f32[256]{0:T(256)S(1)}, f32[256]{0:T(256)S(1)}) all-reduce(f32[256]{0:T(256)S(1)} %bitcast.6, f32[256]{0:T(256)S(1)} %bitcast.5, f32[256]{0:T(256)S(1)} %bitcast.7), channel_id=1, replica_groups=mesh['ctx'=32,'chan'=4,'section'=2] {'chan'}, use_global_device_ids=true, to_apply=%region_0.0 | all-reduce | flops 768 | bytes 6144 | tf_op jit(solution)/shard_map/psum | solution.py:129
  86.9 0.6 rsqrt_multiply_fusion
Async XLA Ops:
  75.5 0.7 copy-start
where the time goes:
time: 87.8 us; the launch traced here: 87.4 us
  blocking collectives  72 us (82%)
  Pallas kernels  12.9 us (15%)
  local copies, waits for them, and re-layouts  1.42 us (2%)
    all_to_all x1, blocking collectives, local(): lax.all_to_all(packed, 'ctx', split_axis=0, concat_axis=0, tiled=True)  38.6 us
    all_to_all x1, blocking collectives, local(): lax.all_to_all(conv, 'ctx', split_axis=0, concat_axis=0, tiled=True)  22.7 us
    psum x1, blocking collectives, local(): inner_total, out_total = lax.psum((sums[0], sums[1]), 'chan')  10.7 us
    pallas_call x1, Pallas kernels, local(): call(conv_kernel, jax.ShapeDtypeStruct((count, width, span), bf16))  7.59 us
    pallas_call x1, Pallas kernels, local(): call(prepare_kernel, (jax.ShapeDtypeStruct((count, 2, width, span), bf16)...  2.74 us
    pallas_call x1, Pallas kernels, local(): call(finish_kernel, (jax.ShapeDtypeStruct((span, channels), bf16), jax.Sh...  2.52 us

commit v1 on v0

--- a/solution.py
+++ b/solution.py
@@ -10,7 +10,7 @@
 from jax.sharding import PartitionSpec as P
 
 EPSILON = 1e-06
-VMEM_LIMIT = 56 * 2**20
+VMEM_LIMIT = 20 * 2**20
 GROUP = 16
 
 
@@ -38,14 +38,12 @@
     return jnp.dot(left, right, preferred_element_type=jnp.float32)
 
 
-def prepare_kernel(sig_ref, fil_ref, out_ref, sq_ref):
+def prepare_kernel(sig_ref, fil_ref, out_ref):
     count, _, width, span = out_ref.shape
     sig = sig_ref[...]
     out_ref[:, 0] = sig.T.reshape(count, width, span)
     fil = fil_ref[...].astype(jnp.bfloat16)
     out_ref[:, 1] = fil.T.reshape(count, width, span)
-    wide = sig.astype(jnp.float32)
-    sq_ref[...] = token_sums(wide * wide)
 
 
 def token_sums(terms):
@@ -92,7 +90,8 @@
     mixed = gate_ref[...].astype(jnp.float32) * (conv + skip_ref[...] * sig)
     out_ref[...] = mixed.astype(jnp.bfloat16)
     sums_ref[0:1] = token_sums(sig * mixed)
-    sums_ref[1:2] = token_sums(mixed * mixed)
+    sums_ref[1:2] = token_sums(sig * sig)
+    sums_ref[2:3] = token_sums(mixed * mixed)
 
 
 def call(kernel, out_shape, **kwargs):
@@ -109,12 +108,8 @@
     span, channels = signal.shape
     width = channels // count
     bf16, f32 = jnp.bfloat16, jnp.float32
-    packed, sig_sq = call(
-        prepare_kernel,
-        (
-            jax.ShapeDtypeStruct((count, 2, width, span), bf16),
-            jax.ShapeDtypeStruct((1, span), f32),
-        ),
+    packed = call(
+        prepare_kernel, jax.ShapeDtypeStruct((count, 2, width, span), bf16)
     )(signal, filters)
     received = lax.all_to_all(packed, "ctx", split_axis=0, concat_axis=0, tiled=True)
     conv = call(conv_kernel, jax.ShapeDtypeStruct((count, width, span), bf16))(
@@ -123,10 +118,14 @@
     returned = lax.all_to_all(conv, "ctx", split_axis=0, concat_axis=0, tiled=True)
     result, sums = call(
         finish_kernel,
-        (jax.ShapeDtypeStruct((span, channels), bf16), jax.ShapeDtypeStruct((2, span), f32)),
+        (jax.ShapeDtypeStruct((span, channels), bf16), jax.ShapeDtypeStruct((3, span), f32)),
     )(returned, signal, gating, skip_gain.reshape(1, channels))
-    sig_total = lax.psum(sig_sq[0], "chan")
-    inner_total, out_total = lax.psum((sums[0], sums[1]), "chan")
+    parts = lax.axis_size("chan")
+    others = [
+        lax.ppermute(sums, "chan", [(i, (i + hop) % parts) for i in range(parts)])
+        for hop in range(1, parts)
+    ]
+    inner_total, sig_total, out_total = sum(others, sums)
     cosine = inner_total / jnp.sqrt((sig_total + EPSILON) * (out_total + EPSILON))
     return (result, cosine)
 

time: 87.8 us -> 79.4 us (0.904)
  blocking collectives: 72 us -> 60.9 us
  Pallas kernels: 12.9 us -> 6.13 us
  starting transfers between devices: 0 us -> 4.62 us
  waiting for transfers between devices: 0 us -> 3.84 us
  local copies, waits for them, and re-layouts: 1.42 us -> 2.31 us
    psum x1 -> x0, blocking collectives: 10.7 us -> none  [local(): inner_total, out_total = lax.psum((sums[0], sums[1]), 'chan')]
    ppermute x0 -> x3, starting transfers between devices: none -> 4.62 us  [local(): lax.ppermute(sums, 'chan', [(i, (i + hop) % parts) for i in range(parts)])]
    ppermute x0 -> x3, waiting for transfers between devices: none -> 3.84 us  [local(): lax.ppermute(sums, 'chan', [(i, (i + hop) % parts) for i in range(parts)])]
    pallas_call x1, Pallas kernels: 7.59 us -> 4.64 us  [local(): call(conv_kernel, jax.ShapeDtypeStruct((count, width, span), bf16))]
    pallas_call x1, Pallas kernels: 2.74 us -> 0.32 us  [local(): call(prepare_kernel, jax.ShapeDtypeStruct((count, 2, width, span), bf16))]
    unnamed x2 -> x22, local copies, waits for them, and re-layouts: 0.68 us -> 2.31 us
    pallas_call x1, Pallas kernels: 2.52 us -> 1.17 us  [local(): call(finish_kernel, (jax.ShapeDtypeStruct((span, channels), bf16), jax.Sh...]
  transfers between devices with their start and end apart: 0 -> 3, of which waited for: 0 -> 2; matrix products, arithmetic and copies ran while one was open for 0% -> 0% of each run, Pallas kernels for 0% -> 0%
where the time goes in v1:
time: 79.4 us; the launch traced here: 79.1 us
  blocking collectives  60.9 us (77%)
  Pallas kernels  6.13 us (8%)
  starting transfers between devices  4.62 us (6%)
  waiting for transfers between devices  3.84 us (5%)
  local copies, waits for them, and re-layouts  2.31 us (3%)
    all_to_all x1, blocking collectives, local(): lax.all_to_all(packed, 'ctx', split_axis=0, concat_axis=0, tiled=True)  38.4 us
    all_to_all x1, blocking collectives, local(): lax.all_to_all(conv, 'ctx', split_axis=0, concat_axis=0, tiled=True)  22.5 us
    pallas_call x1, Pallas kernels, local(): call(conv_kernel, jax.ShapeDtypeStruct((count, width, span), bf16))  4.64 us
    ppermute x3, starting transfers between devices, local(): lax.ppermute(sums, 'chan', [(i, (i + hop) % parts) for i in range(parts)])  4.62 us
    ppermute x3, waiting for transfers between devices, local(): lax.ppermute(sums, 'chan', [(i, (i + hop) % parts) for i in range(parts)])  3.84 us
    unnamed x22, local copies, waits for them, and re-layouts  2.31 us
  transfers between devices with their start and end apart: 3, of which 2 were waited for; matrix products, arithmetic and copies ran while one was open for 0% of the time, Pallas kernels for 0%

profile of v1, /device:TPU:32, one launch (start us, length us, event | category | flops | bytes accessed | tf_op | source)
XLA Modules:
  0.0 79.1 jit_solution(16306253627430954325)
XLA Ops:
  0.6 0.0 copy-start
  0.6 1.0 %copy-done = bf16[256,1024]{1,0:T(8,128)(2,1)S(1)} copy-done((bf16[256,1024]{1,0:T(8,128)(2,1)S(1)}, bf16[256,1024]{1,0:T(8,128)(2,1)}, u32[]{:S(2)}) %copy-start) | copy-done | bytes 524312
  1.7 0.0 copy-start.2
  1.7 1.2 %copy-done.2 = f32[256,1024]{1,0:T(8,128)S(1)} copy-done((f32[256,1024]{1,0:T(8,128)S(1)}, f32[256,1024]{1,0:T(8,128)}, u32[]{:S(2)}) %copy-start.2) | copy-done | bytes 1048600
  2.9 0.0 copy-start.6
  2.9 0.0 copy-start.7
  2.9 0.0 copy-start.8
  2.9 0.0 copy-start.9
  2.9 0.3 shard_map.113
  3.2 0.0 copy-start.3
  3.3 0.0 copy-start.4
  3.3 38.4 %all_to_all.10.in_ref = bf16[32,2,32,256]{3,2,1,0:T(8,128)(2,1)S(1)} all-to-all(bf16[32,2,32,256]{3,2,1,0:T(8,128)(2,1)S(1)} %shard_map.113), channel_id=1, replica_groups=mesh['ctx'=32,'chan'=4,'section'=2] {'ctx'}, dimensions={0} | all-to-all | bytes 2097152 | tf_op jit(solution)/shard_map/all_to_all | solution.py:114
  41.7 0.0 copy-done.6
  41.7 0.0 copy-done.7
  41.7 0.0 copy-done.8
  41.7 0.0 copy-done.9
  41.7 0.0 copy-done.3
  41.7 0.0 copy-done.4
  41.7 0.0 copy-start.10
  41.7 4.6 %shard_map.114 = bf16[32,32,256]{2,1,0:T(8,128)(2,1)S(1)} custom-call(bf16[32,2,32,256]{3,2,1,0:T(8,128)(2,1)S(1)} %all_to_all.10.in_ref, bf16[1024,512]{1,0:T(8,128)(2,1)S(1)} %copy-done.4, bf16[512,1024]{1,0:T(8,128)(2,1)S(1)} %copy-done.3, bf16[512,512]{1,0:T(8,128)(2,1)S(1)} %copy-done.7, bf16[512,512]{1,0:T(8,128)(2,1)S(1)} %copy-done.6, ...), custom_call_target="tpu_custom_call" | custom-call | tf_op jit(solution)/shard_map/pallas_call | solution.py:115
  46.3 0.0 copy-start.1
  46.4 0.0 copy-start.5
  46.4 22.5 %all_to_all.11.conv_ref = bf16[32,32,256]{2,1,0:T(8,128)(2,1)S(1)} all-to-all(bf16[32,32,256]{2,1,0:T(8,128)(2,1)S(1)} %shard_map.114), channel_id=1, replica_groups=mesh['ctx'=32,'chan'=4,'section'=2] {'ctx'}, dimensions={0} | all-to-all | bytes 1048576 | tf_op jit(solution)/shard_map/all_to_all | solution.py:118
  68.9 0.0 copy-done.10
  68.9 0.0 copy-done.1
  68.9 0.0 copy-done.5
  68.9 1.2 %shard_map.115 = (bf16[256,1024]{1,0:T(8,128)(2,1)}, f32[3,256]{1,0:T(4,128)S(1)}) custom-call(bf16[32,32,256]{2,1,0:T(8,128)(2,1)S(1)} %all_to_all.11.conv_ref, bf16[256,1024]{1,0:T(8,128)(2,1)S(1)} %copy-done.1, bf16[256,1024]{1,0:T(8,128)(2,1)S(1)} %copy-done.5, f32[1,1024]{1,0:T(1,128)S(1)} %bitcast.2), custom_call_target="tpu_custom_call" | custom-call | tf_op jit(solution)/shard_map/pallas_call | solution.py:119
  70.1 3.0 %collective-permute-start.2 = (f32[3,256]{1,0:T(4,128)S(1)}, f32[3,256]{1,0:T(4,128)S(1)}, u32[]{:S(2)}, u32[]{:S(2)}) collective-permute-start(f32[3,256]{1,0:T(4,128)S(1)} %get-tuple-element.5), channel_id=1, source_target_pairs={{0,6},{2,0},{4,2},{6,4},{1,7},{3,1},{5,3},{7,5},{8,14},{10,8},{12,... | collective-permute-start | bytes 9224 | tf_op jit(solution)/shard_map/ppermute | solution.py:125
  73.1 0.6 collective-permute-start.1
  73.7 1.0 %collective-permute-start = (f32[3,256]{1,0:T(4,128)S(1)}, f32[3,256]{1,0:T(4,128)S(1)}, u32[]{:S(2)}, u32[]{:S(2)}) collective-permute-start(f32[3,256]{1,0:T(4,128)S(1)} %get-tuple-element.5), channel_id=1, source_target_pairs={{0,2},{2,4},{4,6},{6,0},{1,3},{3,5},{5,7},{7,1},{8,10},{10,12},{12... | collective-permute-start | bytes 9224 | tf_op jit(solution)/shard_map/ppermute | solution.py:125
  74.7 0.0 collective-permute-done.2
  74.7 3.5 %collective-permute-done.1 = f32[3,256]{1,0:T(4,128)S(1)} collective-permute-done((f32[3,256]{1,0:T(4,128)S(1)}, f32[3,256]{1,0:T(4,128)S(1)}, u32[]{:S(2)}, u32[]{:S(2)}) %collective-permute-start.1) | collective-permute-done | bytes 3104 | tf_op jit(solution)/shard_map/ppermute | solution.py:125
  78.2 0.3 collective-permute-done
  78.5 0.6 slice_multiply_fusion
  (1 shorter events, 0.0 us)
Async XLA Ops:
  0.6 1.0 %copy-start = (bf16[256,1024]{1,0:T(8,128)(2,1)S(1)}, bf16[256,1024]{1,0:T(8,128)(2,1)}, u32[]{:S(2)}) copy-start(bf16[256,1024]{1,0:T(8,128)(2,1)} %sig_ref.3) | copy-start | bytes 1572868
  1.7 1.2 %copy-start.2 = (f32[256,1024]{1,0:T(8,128)S(1)}, f32[256,1024]{1,0:T(8,128)}, u32[]{:S(2)}) copy-start(f32[256,1024]{1,0:T(8,128)} %fil_ref.1) | copy-start | bytes 3145732
  2.9 38.8 %copy-start.6 = (bf16[512,512]{1,0:T(8,128)(2,1)S(1)}, bf16[512,512]{1,0:T(8,128)(2,1)}, u32[]{:S(2)}) copy-start(bf16[512,512]{1,0:T(8,128)(2,1)} %constant.17.clone.ii_ref) | copy-start | bytes 1572868
  2.9 38.8 %copy-start.7 = (bf16[512,512]{1,0:T(8,128)(2,1)S(1)}, bf16[512,512]{1,0:T(8,128)(2,1)}, u32[]{:S(2)}) copy-start(bf16[512,512]{1,0:T(8,128)(2,1)} %constant.16.clone.fi_ref) | copy-start | bytes 1572868
  2.9 38.8 %copy-start.8 = (f32[32,256]{1,0:T(8,128)S(1)}, f32[32,256]{1,0:T(8,128)}, u32[]{:S(2)}) copy-start(f32[32,256]{1,0:T(8,128)} %constant.19.clone.sin_ref) | copy-start | bytes 98308
  2.9 38.8 %copy-start.9 = (f32[32,256]{1,0:T(8,128)S(1)}, f32[32,256]{1,0:T(8,128)}, u32[]{:S(2)}) copy-start(f32[32,256]{1,0:T(8,128)} %constant.18.clone.cos_ref) | copy-start | bytes 98308
  3.2 38.4 %copy-start.3 = (bf16[512,1024]{1,0:T(8,128)(2,1)S(1)}, bf16[512,1024]{1,0:T(8,128)(2,1)}, u32[]{:S(2)}) copy-start(bf16[512,1024]{1,0:T(8,128)(2,1)} %constant.15.clone.io_ref) | copy-start | bytes 3145732
  3.3 38.4 %copy-start.4 = (bf16[1024,512]{1,0:T(8,128)(2,1)S(1)}, bf16[1024,512]{1,0:T(8,128)(2,1)}, u32[]{:S(2)}) copy-start(bf16[1024,512]{1,0:T(8,128)(2,1)} %constant.14.clone.fo_ref) | copy-start | bytes 3145732
  41.7 27.2 %copy-start.10 = (f32[1024]{0:T(1024)S(1)}, f32[1024]{0:T(1024)}, u32[]{:S(2)}) copy-start(f32[1024]{0:T(1024)} %param.13) | copy-start | bytes 12292
  46.3 22.5 %copy-start.1 = (bf16[256,1024]{1,0:T(8,128)(2,1)S(1)}, bf16[256,1024]{1,0:T(8,128)(2,1)}, u32[]{:S(2)}) copy-start(bf16[256,1024]{1,0:T(8,128)(2,1)} %sig_ref.3) | copy-start | bytes 1572868
  46.4 22.5 %copy-start.5 = (bf16[256,1024]{1,0:T(8,128)(2,1)S(1)}, bf16[256,1024]{1,0:T(8,128)(2,1)}, u32[]{:S(2)}) copy-start(bf16[256,1024]{1,0:T(8,128)(2,1)} %gate_ref.1) | copy-start | bytes 1572868
  70.1 4.6 %collective-permute-start.2 = (f32[3,256]{1,0:T(4,128)S(1)}, f32[3,256]{1,0:T(4,128)S(1)}, u32[]{:S(2)}, u32[]{:S(2)}) collective-permute-start(f32[3,256]{1,0:T(4,128)S(1)} %get-tuple-element.5), channel_id=1, source_target_pairs={{0,6},{2,0},{4,2},{6,4},{1,7},{3,1},{5,3},{7,5},{8,14},{10,8},{12,... | collective-permute-start | bytes 9224 | tf_op jit(solution)/shard_map/ppermute | solution.py:125
  73.1 5.1 %collective-permute-start.1 = (f32[3,256]{1,0:T(4,128)S(1)}, f32[3,256]{1,0:T(4,128)S(1)}, u32[]{:S(2)}, u32[]{:S(2)}) collective-permute-start(f32[3,256]{1,0:T(4,128)S(1)} %get-tuple-element.5), channel_id=1, source_target_pairs={{0,4},{2,6},{4,0},{6,2},{1,5},{3,7},{5,1},{7,3},{8,12},{10,14},{12... | collective-permute-start | bytes 9224 | tf_op jit(solution)/shard_map/ppermute | solution.py:125
  73.7 4.8 %collective-permute-start = (f32[3,256]{1,0:T(4,128)S(1)}, f32[3,256]{1,0:T(4,128)S(1)}, u32[]{:S(2)}, u32[]{:S(2)}) collective-permute-start(f32[3,256]{1,0:T(4,128)S(1)} %get-tuple-element.5), channel_id=1, source_target_pairs={{0,2},{2,4},{4,6},{6,0},{1,3},{3,5},{5,7},{7,1},{8,10},{10,12},{12... | collective-permute-start | bytes 9224 | tf_op jit(solution)/shard_map/ppermute | solution.py:125

commit v2 on v1

v2 whole, which is shorter than its diff:
```python
import math

import jax
import jax.numpy as jnp
import ml_dtypes
import numpy as np
from jax import lax
from jax.experimental import pallas as pl
from jax.experimental.pallas import tpu as pltpu
from jax.sharding import PartitionSpec as P

EPSILON = 1e-06
VMEM_LIMIT = 20 * 2**20
LANES = 128
GROUP = 8
TILES = 4


def conv_tables(blocks, span):
    total = blocks * span
    n1 = np.arange(blocks)
    n2 = np.arange(span)
    outer = 2 * np.pi * np.outer(4 * n1 + 1, n1) / (4 * blocks)
    twiddle = 2 * np.pi * np.outer(4 * n1 + 1, n2) / (4 * total)
    inner = 2 * np.pi * np.outer(n2, n2) / span
    eye = np.eye(GROUP)
    fwd_outer = np.concatenate([np.kron(np.cos(outer), eye), np.kron(-np.sin(outer), eye)], axis=0)
    inv_outer = np.concatenate(
        [np.kron(np.cos(outer.T), eye), np.kron(-np.sin(outer.T), eye)], axis=1
    )
    cos, sin = np.cos(inner), np.sin(inner)
    fwd_inner = np.block([[cos, -sin], [sin, cos]])
    inv_inner = np.block([[cos, sin], [-sin, cos]]) / total
    short = [t.astype(ml_dtypes.bfloat16) for t in (fwd_outer, inv_outer, fwd_inner, inv_inner)]
    wide = [np.cos(twiddle).astype(np.float32), np.sin(twiddle).astype(np.float32)]
    return short + wide


def dot(left, right):
    return jnp.dot(left, right, preferred_element_type=jnp.float32)


def tile_copies(hbm_ref, buf_ref, sem_ref):
    width = hbm_ref.shape[1] // TILES
    spans = [pl.ds(tile * width, width) for tile in range(TILES)]
    return [
        pltpu.make_async_copy(hbm_ref.at[:, span], buf_ref.at[:, span], sem_ref.at[tile])
        for tile, span in enumerate(spans)
    ]


def prepare_kernel(sig_ref, fil_ref, out_ref):
    devices, _, groups, rows, lanes = out_ref.shape
    parts = rows // GROUP
    span, channels = sig_ref.shape
    width, some = channels // TILES, devices // TILES
    for tile in range(TILES):
        for array, ref in enumerate((sig_ref, fil_ref)):
            block = ref[:, tile * width : (tile + 1) * width].astype(jnp.float32)
            turned = block.T.reshape(width // GROUP, GROUP, span)
            turned = jnp.concatenate(
                [turned[:, :, part * lanes : (part + 1) * lanes] for part in range(parts)], axis=1
            )
            out_ref[tile * some : (tile + 1) * some, array] = turned.astype(jnp.bfloat16).reshape(
                some, groups, rows, lanes
            )


def conv_kernel(in_ref, fo_ref, io_ref, fi_ref, ii_ref, cos_ref, sin_ref, out_ref):
    devices, _, groups, rows, lanes = in_ref.shape
    blocks = devices * rows // GROUP
    size = blocks * GROUP

    def turn(re, im, sign):
        cos, sin = (
            jnp.broadcast_to(ref[...][:, None, :], (blocks, GROUP, lanes)).reshape(size, lanes)
            for ref in (cos_ref, sin_ref)
        )
        if sign > 0:
            return re * cos - im * sin, re * sin + im * cos
        return re * cos + im * sin, im * cos - re * sin

    def spectrum(outer):
        turned = jnp.concatenate(turn(outer[:size], outer[size:], -1), axis=1)
        both = dot(turned.astype(jnp.bfloat16), fi_ref[...])
        return both[:, :lanes], both[:, lanes:]

    def product(group):
        pair = [in_ref[:, array, group].reshape(size, lanes) for array in range(2)]
        outer = dot(fo_ref[...], jnp.concatenate(pair, axis=1))
        sig_re, sig_im = spectrum(outer[:, :lanes])
        fil_re, fil_im = spectrum(outer[:, lanes:])
        prod = jnp.concatenate(
            [sig_re * fil_re - sig_im * fil_im, sig_re * fil_im + sig_im * fil_re], axis=1
        )
        back = dot(prod.astype(jnp.bfloat16), ii_ref[...])
        return jnp.concatenate(turn(back[:, :lanes], back[:, lanes:], 1), axis=0).astype(jnp.bfloat16)

    for group in range(0, groups, 2):
        pair = jnp.concatenate([product(group), product(group + 1)], axis=1)
        conv = dot(io_ref[...], pair).astype(jnp.bfloat16)
        for half in range(2):
            out_ref[:, group + half] = conv[:, half * lanes : (half + 1) * lanes].reshape(
                devices, rows, lanes
            )


def token_sums(terms):
    tokens, channels = terms.shape
    part = terms[:, :LANES]
    for start in range(LANES, channels, LANES):
        part = part + terms[:, start : start + LANES]
    return part


def finish_kernel(conv_ref, sig_ref, gate_ref, skip_ref, out_ref, sums_ref, out_buf, out_sem):
    devices, groups, rows, lanes = conv_ref.shape
    parts = rows // GROUP
    span, channels = out_buf.shape
    width, some = channels // TILES, devices // TILES
    copies = tile_copies(out_buf, out_ref, out_sem)
    sums = None
    for tile in range(TILES):
        turned = conv_ref[tile * some : (tile + 1) * some].astype(jnp.float32)
        turned = turned.reshape(some * groups, rows, lanes)
        conv = jnp.concatenate(
            [
                turned[:, part * GROUP : (part + 1) * GROUP].reshape(width, lanes).T
                for part in range(parts)
            ],
            axis=0,
        )
        at = slice(tile * width, (tile + 1) * width)
        sig = sig_ref[:, at].astype(jnp.float32)
        mixed = gate_ref[:, at].astype(jnp.float32) * (conv + skip_ref[:, at] * sig)
        out_buf[:, at] = mixed.astype(jnp.bfloat16)
        copies[tile].start()
        terms = [token_sums(sig * mixed), token_sums(sig * sig), token_sums(mixed * mixed)]
        sums = terms if sums is None else [a + b for a, b in zip(sums, terms)]
    for row, total in enumerate(sums):
        sums_ref[row : row + 1] = jnp.sum(total.T, axis=0, keepdims=True)
    for copy in copies:
        copy.wait()


def call(kernel, out_shape, **kwargs):
    return pl.pallas_call(
        kernel,
        out_shape=out_shape,
        compiler_params=pltpu.CompilerParams(vmem_limit_bytes=VMEM_LIMIT),
        **kwargs,
    )


def local(signal, gating, filters, skip_gain):
    count = lax.axis_size("ctx")
    span, channels = signal.shape
    width = channels // count
    parts = span // LANES
    packed_tail = (width // GROUP, parts * GROUP, LANES)
    bf16, f32 = jnp.bfloat16, jnp.float32
    hbm = pl.BlockSpec(memory_space=pltpu.HBM)
    vmem = pl.BlockSpec(memory_space=pltpu.VMEM)
    tile_sems = pltpu.SemaphoreType.DMA((TILES,))
    packed = call(
        prepare_kernel,
        jax.ShapeDtypeStruct((count, 2) + packed_tail, bf16),
        in_specs=[vmem, vmem],
        out_specs=vmem,
    )(signal, filters.astype(bf16))
    received = lax.all_to_all(packed, "ctx", split_axis=0, concat_axis=0, tiled=True)
    conv = call(conv_kernel, jax.ShapeDtypeStruct((count,) + packed_tail, bf16))(
        received, *conv_tables(count * parts, LANES)
    )
    returned = lax.all_to_all(conv, "ctx", split_axis=0, concat_axis=0, tiled=True)
    result, sums = call(
        finish_kernel,
        (jax.ShapeDtypeStruct((span, channels), bf16), jax.ShapeDtypeStruct((3, span), f32)),
        in_specs=[vmem] * 4,
        out_specs=(hbm, vmem),
        scratch_shapes=[pltpu.VMEM((span, channels), bf16), tile_sems],
    )(returned, signal, gating, skip_gain.reshape(1, channels))
    chans = lax.axis_size("chan")
    others = [
        lax.ppermute(sums, "chan", [(i, (i + hop) % chans) for i in range(chans)])
        for hop in range(1, chans)
    ]
    inner_total, sig_total, out_total = sum(others, sums)
    cosine = inner_total / jnp.sqrt((sig_total + EPSILON) * (out_total + EPSILON))
    return (result, cosine)


def solution(mesh):
    return jax.shard_map(
        local,
        mesh=mesh,
        in_specs=(
            P(("section", "ctx"), "chan"),
            P(("section", "ctx"), "chan"),
            P(("section", "ctx"), "chan"),
            P(("section", "chan")),
        ),
        out_specs=(P(("section", "ctx"), "chan"), P(("section", "ctx"))),
        check_vma=False,
    )
```

time: 79.4 us -> 77.5 us (0.976)
  local copies, waits for them, and re-layouts: 2.31 us -> 0.06 us
  other arithmetic: 0.58 us -> 1.93 us
  Pallas kernels: 6.13 us -> 5.09 us
    unnamed x22 -> x18, local copies, waits for them, and re-layouts: 2.31 us -> 0.06 us
    convert_element_type x0 -> x1, other arithmetic: none -> 1.35 us  [local(): filters.astype(bf16)]
    pallas_call x2, Pallas kernels: 4.96 us -> 4.08 us  [the longest x1 3.74 us: local(): call(conv_kernel, jax.ShapeDtypeStruct((count,) + packed_tail, bf16))]
where the time goes in v2:
time: 77.5 us; the launch traced here: 77.3 us
  blocking collectives  60.9 us (79%)
  Pallas kernels  5.09 us (7%)
  starting transfers between devices  4.69 us (6%)
  waiting for transfers between devices  3.85 us (5%)
  other arithmetic  1.93 us (2%)
    all_to_all x1, blocking collectives, local(): lax.all_to_all(packed, 'ctx', split_axis=0, concat_axis=0, tiled=True)  38.4 us
    all_to_all x1, blocking collectives, local(): lax.all_to_all(conv, 'ctx', split_axis=0, concat_axis=0, tiled=True)  22.5 us
    ppermute x3, starting transfers between devices, local(): lax.ppermute(sums, 'chan', [(i, (i + hop) % chans) for i in range(chans)])  4.69 us
    ppermute x3, waiting for transfers between devices, local(): lax.ppermute(sums, 'chan', [(i, (i + hop) % chans) for i in range(chans)])  3.85 us
    pallas_call x1, Pallas kernels, local(): call(conv_kernel, jax.ShapeDtypeStruct((count,) + packed_tail, bf16))  3.74 us
  transfers between devices with their start and end apart: 3, of which 2 were waited for; matrix products, arithmetic and copies ran while one was open for 0% of the time, Pallas kernels for 0%

profile of v2, /device:TPU:32, one launch (start us, length us, event | category | flops | bytes accessed | tf_op | source)
XLA Modules:
  0.0 77.3 jit_solution(9867738325295125882)
XLA Ops:
  0.6 0.0 copy-start
  0.6 1.4 %convert_element_type.3.fil_ref = bf16[256,1024]{1,0:T(8,128)(2,1)S(1)} convert(f32[256,1024]{1,0:T(8,128)} %param.12) | non-fusion elementwise | flops 262144 | bytes 1572864 | tf_op jit(solution)/shard_map/convert_element_type | solution.py:170
  2.0 0.0 copy-done
  2.0 0.0 copy-start.4
  2.0 0.0 copy-start.5
  2.0 0.0 copy-start.6
  2.0 0.0 copy-start.7
  2.1 0.3 shard_map.113
  2.4 0.0 copy-start.1
  2.4 0.0 copy-start.2
  2.4 38.4 %all_to_all.10.in_ref = bf16[32,2,4,16,128]{4,3,2,1,0:T(8,128)(2,1)S(1)} all-to-all(bf16[32,2,4,16,128]{4,3,2,1,0:T(8,128)(2,1)S(1)} %shard_map.113), channel_id=1, replica_groups=mesh['ctx'=32,'chan'=4,'section'=2] {'ctx'}, dimensions={0} | all-to-all | bytes 2097152 | tf_op jit(solution)/shard_map/all_to_all | solution.py:171
  40.8 0.0 copy-done.4
  40.8 0.0 copy-done.5
  40.8 0.0 copy-done.6
  40.8 0.0 copy-done.7
  40.8 0.0 copy-done.1
  40.8 0.0 copy-done.2
  40.9 3.7 %shard_map.114 = bf16[32,4,16,128]{3,2,1,0:T(8,128)(2,1)S(1)} custom-call(bf16[32,2,4,16,128]{4,3,2,1,0:T(8,128)(2,1)S(1)} %all_to_all.10.in_ref, bf16[1024,512]{1,0:T(8,128)(2,1)S(1)} %copy-done.2, bf16[512,1024]{1,0:T(8,128)(2,1)S(1)} %copy-done.1, bf16[256,256]{1,0:T(8,128)(2,1)S(1)} %copy-done.5, bf16[256,256]{1,0:T(8,128)(2,1)S(1)} %copy-done.4, ...), custom_call_target="tpu_custom_call" | custom-call | tf_op jit(solution)/shard_map/pallas_call | solution.py:172
  44.6 0.0 copy-start.3
  44.6 0.0 copy-start.8
  44.6 22.5 %all_to_all.11.conv_ref = bf16[32,4,16,128]{3,2,1,0:T(8,128)(2,1)S(1)} all-to-all(bf16[32,4,16,128]{3,2,1,0:T(8,128)(2,1)S(1)} %shard_map.114), channel_id=1, replica_groups=mesh['ctx'=32,'chan'=4,'section'=2] {'ctx'}, dimensions={0} | all-to-all | bytes 1048576 | tf_op jit(solution)/shard_map/all_to_all | solution.py:175
  67.1 0.0 copy-done.3
  67.1 0.0 copy-done.8
  67.1 1.0 %shard_map.115 = (bf16[256,1024]{1,0:T(8,128)(2,1)}, f32[3,256]{1,0:T(4,128)S(1)}) custom-call(bf16[32,4,16,128]{3,2,1,0:T(8,128)(2,1)S(1)} %all_to_all.11.conv_ref, bf16[256,1024]{1,0:T(8,128)(2,1)S(1)} %copy-done, bf16[256,1024]{1,0:T(8,128)(2,1)S(1)} %copy-done.3, f32[1,1024]{1,0:T(1,128)S(1)} %bitcast.2), custom_call_target="tpu_custom_call" | custom-call | tf_op jit(solution)/shard_map/pallas_call | solution.py:176
  68.2 3.1 %collective-permute-start.2 = (f32[3,256]{1,0:T(4,128)S(1)}, f32[3,256]{1,0:T(4,128)S(1)}, u32[]{:S(2)}, u32[]{:S(2)}) collective-permute-start(f32[3,256]{1,0:T(4,128)S(1)} %get-tuple-element.5), channel_id=1, source_target_pairs={{0,6},{2,0},{4,2},{6,4},{1,7},{3,1},{5,3},{7,5},{8,14},{10,8},{12,... | collective-permute-start | bytes 9224 | tf_op jit(solution)/shard_map/ppermute | solution.py:185
  71.3 0.6 collective-permute-start.1
  71.9 1.0 %collective-permute-start = (f32[3,256]{1,0:T(4,128)S(1)}, f32[3,256]{1,0:T(4,128)S(1)}, u32[]{:S(2)}, u32[]{:S(2)}) collective-permute-start(f32[3,256]{1,0:T(4,128)S(1)} %get-tuple-element.5), channel_id=1, source_target_pairs={{0,2},{2,4},{4,6},{6,0},{1,3},{3,5},{5,7},{7,1},{8,10},{10,12},{12... | collective-permute-start | bytes 9224 | tf_op jit(solution)/shard_map/ppermute | solution.py:185
  72.9 0.0 collective-permute-done.2
  72.9 3.5 %collective-permute-done.1 = f32[3,256]{1,0:T(4,128)S(1)} collective-permute-done((f32[3,256]{1,0:T(4,128)S(1)}, f32[3,256]{1,0:T(4,128)S(1)}, u32[]{:S(2)}, u32[]{:S(2)}) %collective-permute-start.1) | collective-permute-done | bytes 3104 | tf_op jit(solution)/shard_map/ppermute | solution.py:185
  76.4 0.3 collective-permute-done
  76.7 0.6 slice_multiply_fusion
  (1 shorter events, 0.0 us)
Async XLA Ops:
  0.6 1.4 %copy-start = (bf16[256,1024]{1,0:T(8,128)(2,1)S(1)}, bf16[256,1024]{1,0:T(8,128)(2,1)}, u32[]{:S(2)}) copy-start(bf16[256,1024]{1,0:T(8,128)(2,1)} %sig_ref.3) | copy-start | bytes 1572868
  2.0 38.8 %copy-start.4 = (bf16[256,256]{1,0:T(8,128)(2,1)S(1)}, bf16[256,256]{1,0:T(8,128)(2,1)}, u32[]{:S(2)}) copy-start(bf16[256,256]{1,0:T(8,128)(2,1)} %constant.17.clone.ii_ref) | copy-start | bytes 393220
  2.0 38.8 %copy-start.5 = (bf16[256,256]{1,0:T(8,128)(2,1)S(1)}, bf16[256,256]{1,0:T(8,128)(2,1)}, u32[]{:S(2)}) copy-start(bf16[256,256]{1,0:T(8,128)(2,1)} %constant.16.clone.fi_ref) | copy-start | bytes 393220
  2.0 38.8 %copy-start.6 = (f32[64,128]{1,0:T(8,128)S(1)}, f32[64,128]{1,0:T(8,128)}, u32[]{:S(2)}) copy-start(f32[64,128]{1,0:T(8,128)} %constant.19.clone.sin_ref) | copy-start | bytes 98308
  2.0 38.8 %copy-start.7 = (f32[64,128]{1,0:T(8,128)S(1)}, f32[64,128]{1,0:T(8,128)}, u32[]{:S(2)}) copy-start(f32[64,128]{1,0:T(8,128)} %constant.18.clone.cos_ref) | copy-start | bytes 98308
  2.4 38.4 %copy-start.1 = (bf16[512,1024]{1,0:T(8,128)(2,1)S(1)}, bf16[512,1024]{1,0:T(8,128)(2,1)}, u32[]{:S(2)}) copy-start(bf16[512,1024]{1,0:T(8,128)(2,1)} %constant.15.clone.io_ref) | copy-start | bytes 3145732
  2.4 38.4 %copy-start.2 = (bf16[1024,512]{1,0:T(8,128)(2,1)S(1)}, bf16[1024,512]{1,0:T(8,128)(2,1)}, u32[]{:S(2)}) copy-start(bf16[1024,512]{1,0:T(8,128)(2,1)} %constant.14.clone.fo_ref) | copy-start | bytes 3145732
  44.6 22.5 %copy-start.3 = (bf16[256,1024]{1,0:T(8,128)(2,1)S(1)}, bf16[256,1024]{1,0:T(8,128)(2,1)}, u32[]{:S(2)}) copy-start(bf16[256,1024]{1,0:T(8,128)(2,1)} %gate_ref.1) | copy-start | bytes 1572868
  44.6 22.5 %copy-start.8 = (f32[1024]{0:T(1024)S(1)}, f32[1024]{0:T(1024)}, u32[]{:S(2)}) copy-start(f32[1024]{0:T(1024)} %param.13) | copy-start | bytes 12292
  68.2 4.7 %collective-permute-start.2 = (f32[3,256]{1,0:T(4,128)S(1)}, f32[3,256]{1,0:T(4,128)S(1)}, u32[]{:S(2)}, u32[]{:S(2)}) collective-permute-start(f32[3,256]{1,0:T(4,128)S(1)} %get-tuple-element.5), channel_id=1, source_target_pairs={{0,6},{2,0},{4,2},{6,4},{1,7},{3,1},{5,3},{7,5},{8,14},{10,8},{12,... | collective-permute-start | bytes 9224 | tf_op jit(solution)/shard_map/ppermute | solution.py:185
  71.3 5.1 %collective-permute-start.1 = (f32[3,256]{1,0:T(4,128)S(1)}, f32[3,256]{1,0:T(4,128)S(1)}, u32[]{:S(2)}, u32[]{:S(2)}) collective-permute-start(f32[3,256]{1,0:T(4,128)S(1)} %get-tuple-element.5), channel_id=1, source_target_pairs={{0,4},{2,6},{4,0},{6,2},{1,5},{3,7},{5,1},{7,3},{8,12},{10,14},{12... | collective-permute-start | bytes 9224 | tf_op jit(solution)/shard_map/ppermute | solution.py:185
  71.9 4.8 %collective-permute-start = (f32[3,256]{1,0:T(4,128)S(1)}, f32[3,256]{1,0:T(4,128)S(1)}, u32[]{:S(2)}, u32[]{:S(2)}) collective-permute-start(f32[3,256]{1,0:T(4,128)S(1)} %get-tuple-element.5), channel_id=1, source_target_pairs={{0,2},{2,4},{4,6},{6,0},{1,3},{3,5},{5,7},{7,1},{8,10},{10,12},{12... | collective-permute-start | bytes 9224 | tf_op jit(solution)/shard_map/ppermute | solution.py:185

commit v3 on v2

--- a/solution.py
+++ b/solution.py
@@ -49,14 +49,18 @@
     ]
 
 
-def prepare_kernel(sig_ref, fil_ref, out_ref):
+def prepare_kernel(sig_ref, fil_ref, out_ref, sq_ref):
     devices, _, groups, rows, lanes = out_ref.shape
     parts = rows // GROUP
     span, channels = sig_ref.shape
     width, some = channels // TILES, devices // TILES
+    squares = None
     for tile in range(TILES):
         for array, ref in enumerate((sig_ref, fil_ref)):
             block = ref[:, tile * width : (tile + 1) * width].astype(jnp.float32)
+            if array == 0:
+                part = token_sums(block * block)
+                squares = part if squares is None else squares + part
             turned = block.T.reshape(width // GROUP, GROUP, span)
             turned = jnp.concatenate(
                 [turned[:, :, part * lanes : (part + 1) * lanes] for part in range(parts)], axis=1
@@ -64,6 +68,7 @@
             out_ref[tile * some : (tile + 1) * some, array] = turned.astype(jnp.bfloat16).reshape(
                 some, groups, rows, lanes
             )
+    sq_ref[...] = jnp.sum(squares.T, axis=0, keepdims=True)
 
 
 def conv_kernel(in_ref, fo_ref, io_ref, fi_ref, ii_ref, cos_ref, sin_ref, out_ref):
@@ -162,12 +167,31 @@
     hbm = pl.BlockSpec(memory_space=pltpu.HBM)
     vmem = pl.BlockSpec(memory_space=pltpu.VMEM)
     tile_sems = pltpu.SemaphoreType.DMA((TILES,))
-    packed = call(
+    packed, sig_sq = call(
         prepare_kernel,
-        jax.ShapeDtypeStruct((count, 2) + packed_tail, bf16),
+        (
+            jax.ShapeDtypeStruct((count, 2) + packed_tail, bf16),
+            jax.ShapeDtypeStruct((1, span), f32),
+        ),
         in_specs=[vmem, vmem],
-        out_specs=vmem,
+        out_specs=(vmem, vmem),
     )(signal, filters.astype(bf16))
+    chans, sections = lax.axis_size("chan"), lax.axis_size("section")
+    last = sections - 1
+
+    def total_first(part):
+        total = part
+        for hop in range(1, chans):
+            total = total + lax.ppermute(
+                part,
+                ("chan", "section"),
+                [(i * sections + last, (i + hop) % chans * sections + last) for i in range(chans)],
+            )
+        return total
+
+    is_last = lax.axis_index("section") == last
+    sig_sq = lax.cond(is_last, total_first, lambda part: part, sig_sq)
+    packed, sig_sq = lax.optimization_barrier((packed, sig_sq))
     received = lax.all_to_all(packed, "ctx", split_axis=0, concat_axis=0, tiled=True)
     conv = call(conv_kernel, jax.ShapeDtypeStruct((count,) + packed_tail, bf16))(
         received, *conv_tables(count * parts, LANES)
@@ -180,12 +204,12 @@
         out_specs=(hbm, vmem),
         scratch_shapes=[pltpu.VMEM((span, channels), bf16), tile_sems],
     )(returned, signal, gating, skip_gain.reshape(1, channels))
-    chans = lax.axis_size("chan")
     others = [
         lax.ppermute(sums, "chan", [(i, (i + hop) % chans) for i in range(chans)])
         for hop in range(1, chans)
     ]
     inner_total, sig_total, out_total = sum(others, sums)
+    sig_total = jnp.where(is_last, sig_sq[0], sig_total)
     cosine = inner_total / jnp.sqrt((sig_total + EPSILON) * (out_total + EPSILON))
     return (result, cosine)
 

time: 77.5 us -> 74.5 us (0.961)
  the two profiles are of different devices: /device:TPU:32 before, /device:TPU:1 now
where the time goes in v3:
time: 74.5 us; the launch traced here: 74.2 us
  blocking collectives  46.3 us (62%)
  starting transfers between devices  14.1 us (19%)
  waiting for transfers between devices  5.88 us (8%)
  Pallas kernels  5.15 us (7%)
  other arithmetic  1.95 us (3%)
  between operations  0.77 us (1%)
    all_to_all x1, blocking collectives, local(): lax.all_to_all(packed, 'ctx', split_axis=0, concat_axis=0, tiled=True)  28.7 us
    all_to_all x1, blocking collectives, local(): lax.all_to_all(conv, 'ctx', split_axis=0, concat_axis=0, tiled=True)  17.6 us
    ppermute x3, starting transfers between devices, total_first(): lax.ppermute(part, ('chan', 'section'), [(i * sections + last, (i + hop)...  10.3 us
    ppermute x3, starting transfers between devices, local(): lax.ppermute(sums, 'chan', [(i, (i + hop) % chans) for i in range(chans)])  3.77 us
    pallas_call x1, Pallas kernels, local(): call(conv_kernel, jax.ShapeDtypeStruct((count,) + packed_tail, bf16))  3.74 us
    ppermute x3, waiting for transfers between devices, local(): lax.ppermute(sums, 'chan', [(i, (i + hop) % chans) for i in range(chans)])  2.98 us
    ppermute x3, waiting for transfers between devices, total_first(): lax.ppermute(part, ('chan', 'section'), [(i * sections + last, (i + hop)...  2.91 us
  transfers between devices with their start and end apart: 6, of which 4 were waited for; matrix products, arithmetic and copies ran while one was open for 0% of the time, Pallas kernels for 0%

profile of v3, /device:TPU:1, one launch (start us, length us, event | category | flops | bytes accessed | tf_op | source)
XLA Modules:
  0.0 74.2 jit_solution(7036337635820467163)
XLA Ops:
  0.6 0.0 copy-start
  0.6 1.4 %convert_element_type.6.fil_ref = bf16[256,1024]{1,0:T(8,128)(2,1)S(1)} convert(f32[256,1024]{1,0:T(8,128)} %param.14) | non-fusion elementwise | flops 262144 | bytes 1572864 | tf_op jit(solution)/shard_map/convert_element_type | solution.py:178
  2.0 0.0 copy-done
  2.0 0.0 copy-start.4
  2.0 0.0 copy-start.5
  2.0 0.0 copy-start.6
  2.0 0.0 copy-start.7
  2.1 0.4 shard_map.113
  2.5 13.3 %conditional.1 = (f32[1,256]{1,0:T(1,128)S(1)}) conditional(s32[]{:T(128)} %convert_element_type.7, f32[1,256]{1,0:T(1,128)S(1)} %get-tuple-element.14, f32[1,256]{1,0:T(1,128)S(1)} %get-tuple-element.14), branch_computations={%region_0.0_spmd, %region_1.0_spmd} | conditional | flops 768 | bytes 17536 | solution.py:193
  2.5 5.5 %collective-permute-start.2 = (f32[1,256]{1,0:T(1,128)S(1)}, f32[1,256]{1,0:T(1,128)S(1)}, u32[]{:S(2)}, u32[]{:S(2)}) collective-permute-start(f32[1,256]{1,0:T(1,128)S(1)} %param.1), channel_id=1, source_target_pairs={{1,7},{3,1},{5,3},{7,5},{9,15},{11,9},{13,11},{15,13},{17,23},{19,... | collective-permute-start | bytes 3080 | tf_op jit(solution)/shard_map/cond/branch_1_fun/ppermute | solution.py:185
  8.0 2.3 %collective-permute-start.1 = (f32[1,256]{1,0:T(1,128)S(1)}, f32[1,256]{1,0:T(1,128)S(1)}, u32[]{:S(2)}, u32[]{:S(2)}) collective-permute-start(f32[1,256]{1,0:T(1,128)S(1)} %param.1), channel_id=1, source_target_pairs={{1,5},{3,7},{5,1},{7,3},{9,13},{11,15},{13,9},{15,11},{17,21},{19,... | collective-permute-start | bytes 3080 | tf_op jit(solution)/shard_map/cond/branch_1_fun/ppermute | solution.py:185
  10.2 2.6 %collective-permute-start = (f32[1,256]{1,0:T(1,128)S(1)}, f32[1,256]{1,0:T(1,128)S(1)}, u32[]{:S(2)}, u32[]{:S(2)}) collective-permute-start(f32[1,256]{1,0:T(1,128)S(1)} %param.1), channel_id=1, source_target_pairs={{1,3},{3,5},{5,7},{7,1},{9,11},{11,13},{13,15},{15,9},{17,19},{19,... | collective-permute-start | bytes 3080 | tf_op jit(solution)/shard_map/cond/branch_1_fun/ppermute | solution.py:185
  12.8 0.0 collective-permute-done.2
  12.8 0.9 %collective-permute-done.1 = f32[1,256]{1,0:T(1,128)S(1)} collective-permute-done((f32[1,256]{1,0:T(1,128)S(1)}, f32[1,256]{1,0:T(1,128)S(1)}, u32[]{:S(2)}, u32[]{:S(2)}) %collective-permute-start.1) | collective-permute-done | bytes 1056 | tf_op jit(solution)/shard_map/cond/branch_1_fun/ppermute | solution.py:185
  13.8 2.0 %collective-permute-done = f32[1,256]{1,0:T(1,128)S(1)} collective-permute-done((f32[1,256]{1,0:T(1,128)S(1)}, f32[1,256]{1,0:T(1,128)S(1)}, u32[]{:S(2)}, u32[]{:S(2)}) %collective-permute-start) | collective-permute-done | bytes 1056 | tf_op jit(solution)/shard_map/cond/branch_1_fun/ppermute | solution.py:185
  15.8 0.0 copy-start.1
  15.8 0.0 copy-start.2
  15.8 28.7 %all_to_all.10.in_ref = bf16[32,2,4,16,128]{4,3,2,1,0:T(8,128)(2,1)S(1)} all-to-all(bf16[32,2,4,16,128]{4,3,2,1,0:T(8,128)(2,1)S(1)} %get-tuple-element.15), channel_id=1, replica_groups=mesh['ctx'=32,'chan'=4,'section'=2] {'ctx'}, dimensions={0} | all-to-all | bytes 2097152 | tf_op jit(solution)/shard_map/all_to_all | solution.py:195
  44.5 0.0 copy-done.4
  44.5 0.0 copy-done.5
  44.5 0.0 copy-done.6
  44.5 0.0 copy-done.7
  44.5 0.0 copy-done.1
  44.5 0.0 copy-done.2
  44.5 3.7 %shard_map.114 = bf16[32,4,16,128]{3,2,1,0:T(8,128)(2,1)S(1)} custom-call(bf16[32,2,4,16,128]{4,3,2,1,0:T(8,128)(2,1)S(1)} %all_to_all.10.in_ref, bf16[1024,512]{1,0:T(8,128)(2,1)S(1)} %copy-done.2, bf16[512,1024]{1,0:T(8,128)(2,1)S(1)} %copy-done.1, bf16[256,256]{1,0:T(8,128)(2,1)S(1)} %copy-done.5, bf16[256,256]{1,0:T(8,128)(2,1)S(1)} %copy-done.4, ...), custom_call_target="tpu_custom_call" | custom-call | tf_op jit(solution)/shard_map/pallas_call | solution.py:196
  48.2 0.0 copy-start.3
  48.3 0.0 copy-start.8
  48.3 17.6 %all_to_all.11.conv_ref = bf16[32,4,16,128]{3,2,1,0:T(8,128)(2,1)S(1)} all-to-all(bf16[32,4,16,128]{3,2,1,0:T(8,128)(2,1)S(1)} %shard_map.114), channel_id=1, replica_groups=mesh['ctx'=32,'chan'=4,'section'=2] {'ctx'}, dimensions={0} | all-to-all | bytes 1048576 | tf_op jit(solution)/shard_map/all_to_all | solution.py:199
  65.8 0.0 copy-done.3
  65.8 0.0 copy-done.8
  65.8 1.0 %shard_map.115 = (bf16[256,1024]{1,0:T(8,128)(2,1)}, f32[3,256]{1,0:T(4,128)S(1)}) custom-call(bf16[32,4,16,128]{3,2,1,0:T(8,128)(2,1)S(1)} %all_to_all.11.conv_ref, bf16[256,1024]{1,0:T(8,128)(2,1)S(1)} %copy-done, bf16[256,1024]{1,0:T(8,128)(2,1)S(1)} %copy-done.3, f32[1,1024]{1,0:T(1,128)S(1)} %bitcast.2), custom_call_target="tpu_custom_call" | custom-call | tf_op jit(solution)/shard_map/pallas_call | solution.py:200
  66.9 2.7 %collective-permute-start.5 = (f32[3,256]{1,0:T(4,128)S(1)}, f32[3,256]{1,0:T(4,128)S(1)}, u32[]{:S(2)}, u32[]{:S(2)}) collective-permute-start(f32[3,256]{1,0:T(4,128)S(1)} %get-tuple-element.17), channel_id=1, source_target_pairs={{0,6},{2,0},{4,2},{6,4},{1,7},{3,1},{5,3},{7,5},{8,14},{10,8},{12,... | collective-permute-start | bytes 9224 | tf_op jit(solution)/shard_map/ppermute | solution.py:208
  69.6 0.3 collective-permute-start.4
  69.9 0.7 collective-permute-start.3
  70.6 0.0 collective-permute-done.5
  70.6 2.9 %collective-permute-done.4 = f32[3,256]{1,0:T(4,128)S(1)} collective-permute-done((f32[3,256]{1,0:T(4,128)S(1)}, f32[3,256]{1,0:T(4,128)S(1)}, u32[]{:S(2)}, u32[]{:S(2)}) %collective-permute-start.4) | collective-permute-done | bytes 3104 | tf_op jit(solution)/shard_map/ppermute | solution.py:208
  73.6 0.1 collective-permute-done.3
  73.6 0.6 slice_multiply_fusion
  (2 shorter events, 0.0 us)
Async XLA Ops:
  0.6 1.4 %copy-start = (bf16[256,1024]{1,0:T(8,128)(2,1)S(1)}, bf16[256,1024]{1,0:T(8,128)(2,1)}, u32[]{:S(2)}) copy-start(bf16[256,1024]{1,0:T(8,128)(2,1)} %sig_ref.3) | copy-start | bytes 1572868
  2.0 42.4 %copy-start.4 = (bf16[256,256]{1,0:T(8,128)(2,1)S(1)}, bf16[256,256]{1,0:T(8,128)(2,1)}, u32[]{:S(2)}) copy-start(bf16[256,256]{1,0:T(8,128)(2,1)} %constant.23.clone.ii_ref) | copy-start | bytes 393220
  2.0 42.4 %copy-start.5 = (bf16[256,256]{1,0:T(8,128)(2,1)S(1)}, bf16[256,256]{1,0:T(8,128)(2,1)}, u32[]{:S(2)}) copy-start(bf16[256,256]{1,0:T(8,128)(2,1)} %constant.22.clone.fi_ref) | copy-start | bytes 393220
  2.0 42.4 %copy-start.6 = (f32[64,128]{1,0:T(8,128)S(1)}, f32[64,128]{1,0:T(8,128)}, u32[]{:S(2)}) copy-start(f32[64,128]{1,0:T(8,128)} %constant.25.clone.sin_ref) | copy-start | bytes 98308
  2.0 42.4 %copy-start.7 = (f32[64,128]{1,0:T(8,128)S(1)}, f32[64,128]{1,0:T(8,128)}, u32[]{:S(2)}) copy-start(f32[64,128]{1,0:T(8,128)} %constant.24.clone.cos_ref) | copy-start | bytes 98308
  2.5 10.4 %collective-permute-start.2 = (f32[1,256]{1,0:T(1,128)S(1)}, f32[1,256]{1,0:T(1,128)S(1)}, u32[]{:S(2)}, u32[]{:S(2)}) collective-permute-start(f32[1,256]{1,0:T(1,128)S(1)} %param.1), channel_id=1, source_target_pairs={{1,7},{3,1},{5,3},{7,5},{9,15},{11,9},{13,11},{15,13},{17,23},{19,... | collective-permute-start | bytes 3080 | tf_op jit(solution)/shard_map/cond/branch_1_fun/ppermute | solution.py:185
  8.0 5.8 %collective-permute-start.1 = (f32[1,256]{1,0:T(1,128)S(1)}, f32[1,256]{1,0:T(1,128)S(1)}, u32[]{:S(2)}, u32[]{:S(2)}) collective-permute-start(f32[1,256]{1,0:T(1,128)S(1)} %param.1), channel_id=1, source_target_pairs={{1,5},{3,7},{5,1},{7,3},{9,13},{11,15},{13,9},{15,11},{17,21},{19,... | collective-permute-start | bytes 3080 | tf_op jit(solution)/shard_map/cond/branch_1_fun/ppermute | solution.py:185
  10.2 5.5 %collective-permute-start = (f32[1,256]{1,0:T(1,128)S(1)}, f32[1,256]{1,0:T(1,128)S(1)}, u32[]{:S(2)}, u32[]{:S(2)}) collective-permute-start(f32[1,256]{1,0:T(1,128)S(1)} %param.1), channel_id=1, source_target_pairs={{1,3},{3,5},{5,7},{7,1},{9,11},{11,13},{13,15},{15,9},{17,19},{19,... | collective-permute-start | bytes 3080 | tf_op jit(solution)/shard_map/cond/branch_1_fun/ppermute | solution.py:185
  15.8 28.7 %copy-start.1 = (bf16[512,1024]{1,0:T(8,128)(2,1)S(1)}, bf16[512,1024]{1,0:T(8,128)(2,1)}, u32[]{:S(2)}) copy-start(bf16[512,1024]{1,0:T(8,128)(2,1)} %constant.21.clone.io_ref) | copy-start | bytes 3145732
  15.8 28.7 %copy-start.2 = (bf16[1024,512]{1,0:T(8,128)(2,1)S(1)}, bf16[1024,512]{1,0:T(8,128)(2,1)}, u32[]{:S(2)}) copy-start(bf16[1024,512]{1,0:T(8,128)(2,1)} %constant.20.clone.fo_ref) | copy-start | bytes 3145732
  48.2 17.6 %copy-start.3 = (bf16[256,1024]{1,0:T(8,128)(2,1)S(1)}, bf16[256,1024]{1,0:T(8,128)(2,1)}, u32[]{:S(2)}) copy-start(bf16[256,1024]{1,0:T(8,128)(2,1)} %gate_ref.1) | copy-start | bytes 1572868
  48.3 17.6 %copy-start.8 = (f32[1024]{0:T(1024)S(1)}, f32[1024]{0:T(1024)}, u32[]{:S(2)}) copy-start(f32[1024]{0:T(1024)} %param.15) | copy-start | bytes 12292
  66.9 3.8 %collective-permute-start.5 = (f32[3,256]{1,0:T(4,128)S(1)}, f32[3,256]{1,0:T(4,128)S(1)}, u32[]{:S(2)}, u32[]{:S(2)}) collective-permute-start(f32[3,256]{1,0:T(4,128)S(1)} %get-tuple-element.17), channel_id=1, source_target_pairs={{0,6},{2,0},{4,2},{6,4},{1,7},{3,1},{5,3},{7,5},{8,14},{10,8},{12,... | collective-permute-start | bytes 9224 | tf_op jit(solution)/shard_map/ppermute | solution.py:208
  69.6 4.0 %collective-permute-start.4 = (f32[3,256]{1,0:T(4,128)S(1)}, f32[3,256]{1,0:T(4,128)S(1)}, u32[]{:S(2)}, u32[]{:S(2)}) collective-permute-start(f32[3,256]{1,0:T(4,128)S(1)} %get-tuple-element.17), channel_id=1, source_target_pairs={{0,4},{2,6},{4,0},{6,2},{1,5},{3,7},{5,1},{7,3},{8,12},{10,14},{12... | collective-permute-start | bytes 9224 | tf_op jit(solution)/shard_map/ppermute | solution.py:208
  69.9 3.7 %collective-permute-start.3 = (f32[3,256]{1,0:T(4,128)S(1)}, f32[3,256]{1,0:T(4,128)S(1)}, u32[]{:S(2)}, u32[]{:S(2)}) collective-permute-start(f32[3,256]{1,0:T(4,128)S(1)} %get-tuple-element.17), channel_id=1, source_target_pairs={{0,2},{2,4},{4,6},{6,0},{1,3},{3,5},{5,7},{7,1},{8,10},{10,12},{12... | collective-permute-start | bytes 9224 | tf_op jit(solution)/shard_map/ppermute | solution.py:208

commit v4 on v3

--- a/solution.py
+++ b/solution.py
@@ -14,26 +14,58 @@
 LANES = 128
 GROUP = 8
 TILES = 4
+RADIX = 4
+COS, SIN, HALF = math.cos(math.pi / 8), math.sin(math.pi / 8), math.sqrt(0.5)
 
 
 def conv_tables(blocks, span):
     total = blocks * span
-    n1 = np.arange(blocks)
-    n2 = np.arange(span)
-    outer = 2 * np.pi * np.outer(4 * n1 + 1, n1) / (4 * blocks)
-    twiddle = 2 * np.pi * np.outer(4 * n1 + 1, n2) / (4 * total)
-    inner = 2 * np.pi * np.outer(n2, n2) / span
-    eye = np.eye(GROUP)
-    fwd_outer = np.concatenate([np.kron(np.cos(outer), eye), np.kron(-np.sin(outer), eye)], axis=0)
-    inv_outer = np.concatenate(
-        [np.kron(np.cos(outer.T), eye), np.kron(-np.sin(outer.T), eye)], axis=1
-    )
-    cos, sin = np.cos(inner), np.sin(inner)
-    fwd_inner = np.block([[cos, -sin], [sin, cos]])
-    inv_inner = np.block([[cos, sin], [-sin, cos]]) / total
+    few = blocks // RADIX
+    m, r = np.arange(few), np.arange(span)
+    k1 = RADIX * np.arange(few)[None, :] + np.arange(RADIX)[:, None]
+    outer = 2 * np.pi * (4 * k1 + 1)[:, :, None] * m / (4 * blocks)
+    twiddle = 2 * np.pi * (4 * k1 + 1).reshape(-1, 1) * r / (4 * total)
+    inner = 2 * np.pi * np.outer(r, r) / span
+
+    def split(cos, sin):
+        return np.block([[cos, -sin], [sin, cos]])
+
+    def spread(angles):
+        eye = np.eye(GROUP)
+        return split(np.kron(np.cos(angles), eye), np.kron(np.sin(angles), eye))
+
+    fwd_outer = np.stack([spread(-angles) for angles in outer])
+    inv_outer = np.stack([spread(angles.T) for angles in outer])
+    fwd_inner = split(np.cos(inner), np.sin(inner))
+    inv_inner = split(np.cos(inner), -np.sin(inner)) / total
     short = [t.astype(ml_dtypes.bfloat16) for t in (fwd_outer, inv_outer, fwd_inner, inv_inner)]
     wide = [np.cos(twiddle).astype(np.float32), np.sin(twiddle).astype(np.float32)]
     return short + wide
+
+
+def quarters(x0, x1, x2, x3):
+    even, odd = HALF * x2, (COS * x1, SIN * x1, COS * x3, SIN * x3)
+    plus, minus = x0 + even, x0 - even
+    c, d = odd[0] + odd[3], odd[1] - odd[2]
+    e, f = odd[1] + odd[2], odd[0] - odd[3]
+    return [
+        (plus + c, -(e + even)),
+        (minus - d, even - f),
+        (plus - c, e - even),
+        (minus + d, f + even),
+    ]
+
+
+def recombined(parts):
+    (r0, i0), (r1, i1), (r2, i2), (r3, i3) = parts
+    a, b, c, d = r0 - r2, r1 - r3, i0 - i2, i1 - i3
+    e, f = r0 + r2, r1 + r3
+    return [
+        e + f,
+        COS * (a - d) - SIN * (b + c),
+        HALF * ((e - f) - ((i0 + i2) - (i1 + i3))),
+        SIN * (a + d) + COS * (b - c),
+    ]
 
 
 def dot(left, right):
@@ -73,41 +105,81 @@
 
 def conv_kernel(in_ref, fo_ref, io_ref, fi_ref, ii_ref, cos_ref, sin_ref, out_ref):
     devices, _, groups, rows, lanes = in_ref.shape
-    blocks = devices * rows // GROUP
-    size = blocks * GROUP
-
-    def turn(re, im, sign):
+    some = devices // RADIX
+    size = some * rows
+    few = size // GROUP
+
+    def turn(re, im, j, sign):
         cos, sin = (
-            jnp.broadcast_to(ref[...][:, None, :], (blocks, GROUP, lanes)).reshape(size, lanes)
+            jnp.broadcast_to(
+                ref[j * few : (j + 1) * few][:, None, :], (few, GROUP, lanes)
+            ).reshape(size, lanes)
             for ref in (cos_ref, sin_ref)
         )
         if sign > 0:
             return re * cos - im * sin, re * sin + im * cos
         return re * cos + im * sin, im * cos - re * sin
 
-    def spectrum(outer):
-        turned = jnp.concatenate(turn(outer[:size], outer[size:], -1), axis=1)
-        both = dot(turned.astype(jnp.bfloat16), fi_ref[...])
-        return both[:, :lanes], both[:, lanes:]
-
-    def product(group):
-        pair = [in_ref[:, array, group].reshape(size, lanes) for array in range(2)]
-        outer = dot(fo_ref[...], jnp.concatenate(pair, axis=1))
-        sig_re, sig_im = spectrum(outer[:, :lanes])
-        fil_re, fil_im = spectrum(outer[:, lanes:])
+    def outer(group):
+        blocks = []
+        for q in range(RADIX):
+            pair = [
+                in_ref[q * some : (q + 1) * some, array, group].reshape(size, lanes)
+                for array in range(2)
+            ]
+            blocks.append(jnp.concatenate(pair, axis=1).astype(jnp.float32))
+        return [
+            dot(fo_ref[j], jnp.concatenate([re, im], axis=0).astype(jnp.bfloat16))
+            for j, (re, im) in enumerate(quarters(*blocks))
+        ]
+
+    def spectra(outers):
+        turned = []
+        for j, part in enumerate(outers):
+            turned.append(
+                [
+                    jnp.concatenate(
+                        turn(part[:size, at : at + lanes], part[size:, at : at + lanes], j, -1), axis=1
+                    ).astype(jnp.bfloat16)
+                    for at in (0, lanes)
+                ]
+            )
+        return [dot(jnp.concatenate(part, axis=0), fi_ref[...]) for part in zip(*turned)]
+
+    def product(sig, fil):
+        sig_re, sig_im = sig[:, :lanes], sig[:, lanes:]
+        fil_re, fil_im = fil[:, :lanes], fil[:, lanes:]
         prod = jnp.concatenate(
             [sig_re * fil_re - sig_im * fil_im, sig_re * fil_im + sig_im * fil_re], axis=1
         )
-        back = dot(prod.astype(jnp.bfloat16), ii_ref[...])
-        return jnp.concatenate(turn(back[:, :lanes], back[:, lanes:], 1), axis=0).astype(jnp.bfloat16)
-
+        return dot(prod.astype(jnp.bfloat16), ii_ref[...])
+
+    def unturned(spread):
+        results = []
+        for j in range(RADIX):
+            back = spread[j * size : (j + 1) * size]
+            back = turn(back[:, :lanes], back[:, lanes:], j, 1)
+            results.append(jnp.concatenate(back, axis=0).astype(jnp.bfloat16))
+        return results
+
+    def finish(group, first, second):
+        parts = []
+        for j, pair in enumerate(zip(first, second)):
+            part = dot(io_ref[j], jnp.concatenate(pair, axis=1))
+            parts.append((part[:size], part[size:]))
+        for q, conv in enumerate(recombined(parts)):
+            conv = conv.astype(jnp.bfloat16)
+            for half in range(2):
+                out_ref[q * some : (q + 1) * some, group + half] = conv[
+                    :, half * lanes : (half + 1) * lanes
+                ].reshape(some, rows, lanes)
+
+    outers = [outer(group) for group in range(groups)]
+    specs = [spectra(part) for part in outers]
+    spreads = [product(*spec) for spec in specs]
+    results = [unturned(spread) for spread in spreads]
     for group in range(0, groups, 2):
-        pair = jnp.concatenate([product(group), product(group + 1)], axis=1)
-        conv = dot(io_ref[...], pair).astype(jnp.bfloat16)
-        for half in range(2):
-            out_ref[:, group + half] = conv[:, half * lanes : (half + 1) * lanes].reshape(
-                devices, rows, lanes
-            )
+        finish(group, results[group], results[group + 1])
 
 
 def token_sums(terms):
@@ -118,12 +190,11 @@
     return part
 
 
-def finish_kernel(conv_ref, sig_ref, gate_ref, skip_ref, out_ref, sums_ref, out_buf, out_sem):
+def finish_kernel(conv_ref, sig_ref, gate_ref, skip_ref, out_ref, sums_ref):
     devices, groups, rows, lanes = conv_ref.shape
     parts = rows // GROUP
-    span, channels = out_buf.shape
+    span, channels = out_ref.shape
     width, some = channels // TILES, devices // TILES
-    copies = tile_copies(out_buf, out_ref, out_sem)
     sums = None
     for tile in range(TILES):
         turned = conv_ref[tile * some : (tile + 1) * some].astype(jnp.float32)
@@ -138,12 +209,17 @@
         at = slice(tile * width, (tile + 1) * width)
         sig = sig_ref[:, at].astype(jnp.float32)
         mixed = gate_ref[:, at].astype(jnp.float32) * (conv + skip_ref[:, at] * sig)
-        out_buf[:, at] = mixed.astype(jnp.bfloat16)
-        copies[tile].start()
+        out_ref[:, at] = mixed.astype(jnp.bfloat16)
         terms = [token_sums(sig * mixed), token_sums(sig * sig), token_sums(mixed * mixed)]
         sums = terms if sums is None else [a + b for a, b in zip(sums, terms)]
     for row, total in enumerate(sums):
         sums_ref[row : row + 1] = jnp.sum(total.T, axis=0, keepdims=True)
+
+
+def deliver_kernel(in_ref, out_ref, sem_ref):
+    copies = tile_copies(in_ref, out_ref, sem_ref)
+    for copy in copies:
+        copy.start()
     for copy in copies:
         copy.wait()
 
@@ -197,13 +273,19 @@
         received, *conv_tables(count * parts, LANES)
     )
     returned = lax.all_to_all(conv, "ctx", split_axis=0, concat_axis=0, tiled=True)
-    result, sums = call(
+    mixed, sums = call(
         finish_kernel,
         (jax.ShapeDtypeStruct((span, channels), bf16), jax.ShapeDtypeStruct((3, span), f32)),
         in_specs=[vmem] * 4,
-        out_specs=(hbm, vmem),
-        scratch_shapes=[pltpu.VMEM((span, channels), bf16), tile_sems],
+        out_specs=(vmem, vmem),
     )(returned, signal, gating, skip_gain.reshape(1, channels))
+    result = call(
+        deliver_kernel,
+        jax.ShapeDtypeStruct((span, channels), bf16),
+        in_specs=[pl.BlockSpec(memory_space=pl.ANY)],
+        out_specs=hbm,
+        scratch_shapes=[tile_sems],
+    )(mixed)
     others = [
         lax.ppermute(sums, "chan", [(i, (i + hop) % chans) for i in range(chans)])
         for hop in range(1, chans)

time: 74.5 us -> 72.8 us (0.977)
  waiting for transfers between devices: 5.88 us -> 5.05 us
  Pallas kernels: 5.15 us -> 4.34 us
    pallas_call x1, Pallas kernels: 3.74 us -> 2.59 us  [local(): call(conv_kernel, jax.ShapeDtypeStruct((count,) + packed_tail, bf16))]
    ppermute x3, waiting for transfers between devices: 2.98 us -> 2.15 us  [local(): lax.ppermute(sums, 'chan', [(i, (i + hop) % chans) for i in range(chans)])]
    pallas_call x0 -> x1, Pallas kernels: none -> 0.82 us  [local(): call(deliver_kernel, jax.ShapeDtypeStruct((span, channels), bf16), in_spe...]
  transfers between devices with their start and end apart: 6 -> 6, of which waited for: 4 -> 4; matrix products, arithmetic and copies ran while one was open for 0% -> 0% of each run, Pallas kernels for 0% -> 1%
where the time goes in v4:
time: 72.8 us; the launch traced here: 72.6 us
  blocking collectives  46.3 us (64%)
  starting transfers between devices  14.1 us (19%)
  waiting for transfers between devices  5.05 us (7%)
  Pallas kernels  4.34 us (6%)
  other arithmetic  1.95 us (3%)
  between operations  0.78 us (1%)
    all_to_all x1, blocking collectives, local(): lax.all_to_all(packed, 'ctx', split_axis=0, concat_axis=0, tiled=True)  28.7 us
    all_to_all x1, blocking collectives, local(): lax.all_to_all(conv, 'ctx', split_axis=0, concat_axis=0, tiled=True)  17.6 us
    ppermute x3, starting transfers between devices, total_first(): lax.ppermute(part, ('chan', 'section'), [(i * sections + last, (i + hop)...  10.3 us
    ppermute x3, starting transfers between devices, local(): lax.ppermute(sums, 'chan', [(i, (i + hop) % chans) for i in range(chans)])  3.77 us
    ppermute x3, waiting for transfers between devices, total_first(): lax.ppermute(part, ('chan', 'section'), [(i * sections + last, (i + hop)...  2.91 us
    pallas_call x1, Pallas kernels, local(): call(conv_kernel, jax.ShapeDtypeStruct((count,) + packed_tail, bf16))  2.59 us
    ppermute x3, waiting for transfers between devices, local(): lax.ppermute(sums, 'chan', [(i, (i + hop) % chans) for i in range(chans)])  2.15 us
  transfers between devices with their start and end apart: 6, of which 4 were waited for; matrix products, arithmetic and copies ran while one was open for 0% of the time, Pallas kernels for 1%

profile of v4, /device:TPU:1, one launch (start us, length us, event | category | flops | bytes accessed | tf_op | source)
XLA Modules:
  0.0 72.6 jit_solution(9382613246413437316)
XLA Ops:
  0.6 0.0 copy-start
  0.6 1.4 %convert_element_type.6.fil_ref = bf16[256,1024]{1,0:T(8,128)(2,1)S(1)} convert(f32[256,1024]{1,0:T(8,128)} %param.14) | non-fusion elementwise | flops 262144 | bytes 1572864 | tf_op jit(solution)/shard_map/convert_element_type | solution.py:254
  2.0 0.0 copy-done
  2.0 0.4 shard_map.113
  2.4 13.3 %conditional.1 = (f32[1,256]{1,0:T(1,128)S(1)}) conditional(s32[]{:T(128)} %convert_element_type.7, f32[1,256]{1,0:T(1,128)S(1)} %get-tuple-element.14, f32[1,256]{1,0:T(1,128)S(1)} %get-tuple-element.14), branch_computations={%region_0.0_spmd, %region_1.0_spmd} | conditional | flops 768 | bytes 17536 | solution.py:269
  2.4 5.5 %collective-permute-start.2 = (f32[1,256]{1,0:T(1,128)S(1)}, f32[1,256]{1,0:T(1,128)S(1)}, u32[]{:S(2)}, u32[]{:S(2)}) collective-permute-start(f32[1,256]{1,0:T(1,128)S(1)} %param.1), channel_id=1, source_target_pairs={{1,7},{3,1},{5,3},{7,5},{9,15},{11,9},{13,11},{15,13},{17,23},{19,... | collective-permute-start | bytes 3080 | tf_op jit(solution)/shard_map/cond/branch_1_fun/ppermute | solution.py:261
  7.9 2.3 %collective-permute-start.1 = (f32[1,256]{1,0:T(1,128)S(1)}, f32[1,256]{1,0:T(1,128)S(1)}, u32[]{:S(2)}, u32[]{:S(2)}) collective-permute-start(f32[1,256]{1,0:T(1,128)S(1)} %param.1), channel_id=1, source_target_pairs={{1,5},{3,7},{5,1},{7,3},{9,13},{11,15},{13,9},{15,11},{17,21},{19,... | collective-permute-start | bytes 3080 | tf_op jit(solution)/shard_map/cond/branch_1_fun/ppermute | solution.py:261
  10.2 2.6 %collective-permute-start = (f32[1,256]{1,0:T(1,128)S(1)}, f32[1,256]{1,0:T(1,128)S(1)}, u32[]{:S(2)}, u32[]{:S(2)}) collective-permute-start(f32[1,256]{1,0:T(1,128)S(1)} %param.1), channel_id=1, source_target_pairs={{1,3},{3,5},{5,7},{7,1},{9,11},{11,13},{13,15},{15,9},{17,19},{19,... | collective-permute-start | bytes 3080 | tf_op jit(solution)/shard_map/cond/branch_1_fun/ppermute | solution.py:261
  12.8 0.0 collective-permute-done.2
  12.8 0.9 %collective-permute-done.1 = f32[1,256]{1,0:T(1,128)S(1)} collective-permute-done((f32[1,256]{1,0:T(1,128)S(1)}, f32[1,256]{1,0:T(1,128)S(1)}, u32[]{:S(2)}, u32[]{:S(2)}) %collective-permute-start.1) | collective-permute-done | bytes 1056 | tf_op jit(solution)/shard_map/cond/branch_1_fun/ppermute | solution.py:261
  13.7 2.0 %collective-permute-done = f32[1,256]{1,0:T(1,128)S(1)} collective-permute-done((f32[1,256]{1,0:T(1,128)S(1)}, f32[1,256]{1,0:T(1,128)S(1)}, u32[]{:S(2)}, u32[]{:S(2)}) %collective-permute-start) | collective-permute-done | bytes 1056 | tf_op jit(solution)/shard_map/cond/branch_1_fun/ppermute | solution.py:261
  15.7 0.0 copy-start.2
  15.7 0.0 copy-start.3
  15.7 0.0 copy-start.4
  15.7 0.0 copy-start.5
  15.7 0.0 copy-start.6
  15.8 0.0 copy-start.7
  15.8 28.7 %all_to_all.10.in_ref = bf16[32,2,4,16,128]{4,3,2,1,0:T(8,128)(2,1)S(1)} all-to-all(bf16[32,2,4,16,128]{4,3,2,1,0:T(8,128)(2,1)S(1)} %get-tuple-element.15), channel_id=1, replica_groups=mesh['ctx'=32,'chan'=4,'section'=2] {'ctx'}, dimensions={0} | all-to-all | bytes 2097152 | tf_op jit(solution)/shard_map/all_to_all | solution.py:271
  44.5 0.0 copy-done.2
  44.5 0.0 copy-done.3
  44.5 0.0 copy-done.4
  44.5 0.0 copy-done.5
  44.5 0.0 copy-done.6
  44.5 0.0 copy-done.7
  44.5 2.6 %shard_map.114 = bf16[32,4,16,128]{3,2,1,0:T(8,128)(2,1)S(1)} custom-call(bf16[32,2,4,16,128]{4,3,2,1,0:T(8,128)(2,1)S(1)} %all_to_all.10.in_ref, bf16[4,256,256]{2,1,0:T(8,128)(2,1)S(1)} %copy-done.3, bf16[4,256,256]{2,1,0:T(8,128)(2,1)S(1)} %copy-done.2, bf16[256,256]{1,0:T(8,128)(2,1)S(1)} %copy-done.5, bf16[256,256]{1,0:T(8,128)(2,1)S(1)} %copy-done.4, ...), custom_call_target="tpu_custom_call" | custom-call | tf_op jit(solution)/shard_map/pallas_call | solution.py:272
  47.1 0.0 copy-start.1
  47.1 0.0 copy-start.8
  47.1 17.6 %all_to_all.11.conv_ref = bf16[32,4,16,128]{3,2,1,0:T(8,128)(2,1)S(1)} all-to-all(bf16[32,4,16,128]{3,2,1,0:T(8,128)(2,1)S(1)} %shard_map.114), channel_id=1, replica_groups=mesh['ctx'=32,'chan'=4,'section'=2] {'ctx'}, dimensions={0} | all-to-all | bytes 1048576 | tf_op jit(solution)/shard_map/all_to_all | solution.py:275
  64.7 0.0 copy-done.1
  64.7 0.0 copy-done.8
  64.7 0.5 shard_map.115
  65.2 2.7 %collective-permute-start.5 = (f32[3,256]{1,0:T(4,128)S(1)}, f32[3,256]{1,0:T(4,128)S(1)}, u32[]{:S(2)}, u32[]{:S(2)}) collective-permute-start(f32[3,256]{1,0:T(4,128)S(1)} %get-tuple-element.17), channel_id=1, source_target_pairs={{0,6},{2,0},{4,2},{6,4},{1,7},{3,1},{5,3},{7,5},{8,14},{10,8},{12,... | collective-permute-start | bytes 9224 | tf_op jit(solution)/shard_map/ppermute | solution.py:290
  68.0 0.4 collective-permute-start.4
  68.3 0.7 collective-permute-start.3
  69.0 0.8 %shard_map.116 = bf16[256,1024]{1,0:T(8,128)(2,1)} custom-call(bf16[256,1024]{1,0:T(8,128)(2,1)S(1)} %get-tuple-element.16.in_ref), custom_call_target="tpu_custom_call" | custom-call | tf_op jit(solution)/shard_map/pallas_call | solution.py:282
  69.8 0.0 collective-permute-done.5
  69.8 2.1 %collective-permute-done.4 = f32[3,256]{1,0:T(4,128)S(1)} collective-permute-done((f32[3,256]{1,0:T(4,128)S(1)}, f32[3,256]{1,0:T(4,128)S(1)}, u32[]{:S(2)}, u32[]{:S(2)}) %collective-permute-start.4) | collective-permute-done | bytes 3104 | tf_op jit(solution)/shard_map/ppermute | solution.py:290
  71.9 0.1 collective-permute-done.3
  72.0 0.6 slice_multiply_fusion
  (2 shorter events, 0.0 us)
Async XLA Ops:
  0.6 1.4 %copy-start = (bf16[256,1024]{1,0:T(8,128)(2,1)S(1)}, bf16[256,1024]{1,0:T(8,128)(2,1)}, u32[]{:S(2)}) copy-start(bf16[256,1024]{1,0:T(8,128)(2,1)} %sig_ref.3) | copy-start | bytes 1572868
  2.4 10.4 %collective-permute-start.2 = (f32[1,256]{1,0:T(1,128)S(1)}, f32[1,256]{1,0:T(1,128)S(1)}, u32[]{:S(2)}, u32[]{:S(2)}) collective-permute-start(f32[1,256]{1,0:T(1,128)S(1)} %param.1), channel_id=1, source_target_pairs={{1,7},{3,1},{5,3},{7,5},{9,15},{11,9},{13,11},{15,13},{17,23},{19,... | collective-permute-start | bytes 3080 | tf_op jit(solution)/shard_map/cond/branch_1_fun/ppermute | solution.py:261
  7.9 5.8 %collective-permute-start.1 = (f32[1,256]{1,0:T(1,128)S(1)}, f32[1,256]{1,0:T(1,128)S(1)}, u32[]{:S(2)}, u32[]{:S(2)}) collective-permute-start(f32[1,256]{1,0:T(1,128)S(1)} %param.1), channel_id=1, source_target_pairs={{1,5},{3,7},{5,1},{7,3},{9,13},{11,15},{13,9},{15,11},{17,21},{19,... | collective-permute-start | bytes 3080 | tf_op jit(solution)/shard_map/cond/branch_1_fun/ppermute | solution.py:261
  10.2 5.5 %collective-permute-start = (f32[1,256]{1,0:T(1,128)S(1)}, f32[1,256]{1,0:T(1,128)S(1)}, u32[]{:S(2)}, u32[]{:S(2)}) collective-permute-start(f32[1,256]{1,0:T(1,128)S(1)} %param.1), channel_id=1, source_target_pairs={{1,3},{3,5},{5,7},{7,1},{9,11},{11,13},{13,15},{15,9},{17,19},{19,... | collective-permute-start | bytes 3080 | tf_op jit(solution)/shard_map/cond/branch_1_fun/ppermute | solution.py:261
  15.7 28.8 %copy-start.2 = (bf16[4,256,256]{2,1,0:T(8,128)(2,1)S(1)}, bf16[4,256,256]{2,1,0:T(8,128)(2,1)}, u32[]{:S(2)}) copy-start(bf16[4,256,256]{2,1,0:T(8,128)(2,1)} %constant.21.clone.io_ref) | copy-start | bytes 1572868
  15.7 28.8 %copy-start.3 = (bf16[4,256,256]{2,1,0:T(8,128)(2,1)S(1)}, bf16[4,256,256]{2,1,0:T(8,128)(2,1)}, u32[]{:S(2)}) copy-start(bf16[4,256,256]{2,1,0:T(8,128)(2,1)} %constant.20.clone.fo_ref) | copy-start | bytes 1572868
  15.7 28.7 %copy-start.4 = (bf16[256,256]{1,0:T(8,128)(2,1)S(1)}, bf16[256,256]{1,0:T(8,128)(2,1)}, u32[]{:S(2)}) copy-start(bf16[256,256]{1,0:T(8,128)(2,1)} %constant.23.clone.ii_ref) | copy-start | bytes 393220
  15.7 28.7 %copy-start.5 = (bf16[256,256]{1,0:T(8,128)(2,1)S(1)}, bf16[256,256]{1,0:T(8,128)(2,1)}, u32[]{:S(2)}) copy-start(bf16[256,256]{1,0:T(8,128)(2,1)} %constant.22.clone.fi_ref) | copy-start | bytes 393220
  15.7 28.7 %copy-start.6 = (f32[64,128]{1,0:T(8,128)S(1)}, f32[64,128]{1,0:T(8,128)}, u32[]{:S(2)}) copy-start(f32[64,128]{1,0:T(8,128)} %constant.25.clone.sin_ref) | copy-start | bytes 98308
  15.8 28.7 %copy-start.7 = (f32[64,128]{1,0:T(8,128)S(1)}, f32[64,128]{1,0:T(8,128)}, u32[]{:S(2)}) copy-start(f32[64,128]{1,0:T(8,128)} %constant.24.clone.cos_ref) | copy-start | bytes 98308
  47.1 17.6 %copy-start.1 = (bf16[256,1024]{1,0:T(8,128)(2,1)S(1)}, bf16[256,1024]{1,0:T(8,128)(2,1)}, u32[]{:S(2)}) copy-start(bf16[256,1024]{1,0:T(8,128)(2,1)} %gate_ref.1) | copy-start | bytes 1572868
  47.1 17.6 %copy-start.8 = (f32[1024]{0:T(1024)S(1)}, f32[1024]{0:T(1024)}, u32[]{:S(2)}) copy-start(f32[1024]{0:T(1024)} %param.15) | copy-start | bytes 12292
  65.2 4.6 %collective-permute-start.5 = (f32[3,256]{1,0:T(4,128)S(1)}, f32[3,256]{1,0:T(4,128)S(1)}, u32[]{:S(2)}, u32[]{:S(2)}) collective-permute-start(f32[3,256]{1,0:T(4,128)S(1)} %get-tuple-element.17), channel_id=1, source_target_pairs={{0,6},{2,0},{4,2},{6,4},{1,7},{3,1},{5,3},{7,5},{8,14},{10,8},{12,... | collective-permute-start | bytes 9224 | tf_op jit(solution)/shard_map/ppermute | solution.py:290
  68.0 4.0 %collective-permute-start.4 = (f32[3,256]{1,0:T(4,128)S(1)}, f32[3,256]{1,0:T(4,128)S(1)}, u32[]{:S(2)}, u32[]{:S(2)}) collective-permute-start(f32[3,256]{1,0:T(4,128)S(1)} %get-tuple-element.17), channel_id=1, source_target_pairs={{0,4},{2,6},{4,0},{6,2},{1,5},{3,7},{5,1},{7,3},{8,12},{10,14},{12... | collective-permute-start | bytes 9224 | tf_op jit(solution)/shard_map/ppermute | solution.py:290
  68.3 3.7 %collective-permute-start.3 = (f32[3,256]{1,0:T(4,128)S(1)}, f32[3,256]{1,0:T(4,128)S(1)}, u32[]{:S(2)}, u32[]{:S(2)}) collective-permute-start(f32[3,256]{1,0:T(4,128)S(1)} %get-tuple-element.17), channel_id=1, source_target_pairs={{0,2},{2,4},{4,6},{6,0},{1,3},{3,5},{5,7},{7,1},{8,10},{10,12},{12... | collective-permute-start | bytes 9224 | tf_op jit(solution)/shard_map/ppermute | solution.py:290

commit v5 on v4

--- a/solution.py
+++ b/solution.py
@@ -286,11 +286,11 @@
         out_specs=hbm,
         scratch_shapes=[tile_sems],
     )(mixed)
-    others = [
-        lax.ppermute(sums, "chan", [(i, (i + hop) % chans) for i in range(chans)])
-        for hop in range(1, chans)
-    ]
-    inner_total, sig_total, out_total = sum(others, sums)
+    reach = 2
+    while reach <= chans:
+        sums = sums + lax.ppermute(sums, "chan", [(i, i ^ (reach - 1)) for i in range(chans)])
+        reach *= 2
+    inner_total, sig_total, out_total = sums
     sig_total = jnp.where(is_last, sig_sq[0], sig_total)
     cosine = inner_total / jnp.sqrt((sig_total + EPSILON) * (out_total + EPSILON))
     return (result, cosine)

time: 72.8 us -> 72.4 us (level)
  waiting for transfers between devices: 5.05 us -> 4.32 us
    ppermute x3 -> x2, waiting for transfers between devices: 2.15 us -> 1.41 us  [local(): lax.ppermute(sums, 'chan', [(i, i ^ reach - 1) for i in range(chans)])]
    ppermute x3 -> x2, starting transfers between devices: 3.77 us -> 4.11 us  [local(): lax.ppermute(sums, 'chan', [(i, i ^ reach - 1) for i in range(chans)])]
  transfers between devices with their start and end apart: 6 -> 5, of which waited for: 4 -> 4; matrix products, arithmetic and copies ran while one was open for 0% -> 0% of each run, Pallas kernels for 1% -> 1%
where the time goes in v5:
time: 72.4 us; the launch traced here: 72.2 us
  blocking collectives  46.3 us (64%)
  starting transfers between devices  14.4 us (20%)
  Pallas kernels  4.34 us (6%)
  waiting for transfers between devices  4.32 us (6%)
  other arithmetic  1.95 us (3%)
  between operations  0.77 us (1%)
    all_to_all x1, blocking collectives, local(): lax.all_to_all(packed, 'ctx', split_axis=0, concat_axis=0, tiled=True)  28.7 us
    all_to_all x1, blocking collectives, local(): lax.all_to_all(conv, 'ctx', split_axis=0, concat_axis=0, tiled=True)  17.6 us
    ppermute x3, starting transfers between devices, total_first(): lax.ppermute(part, ('chan', 'section'), [(i * sections + last, (i + hop)...  10.3 us
    ppermute x2, starting transfers between devices, local(): lax.ppermute(sums, 'chan', [(i, i ^ reach - 1) for i in range(chans)])  4.11 us
    ppermute x3, waiting for transfers between devices, total_first(): lax.ppermute(part, ('chan', 'section'), [(i * sections + last, (i + hop)...  2.91 us
    pallas_call x1, Pallas kernels, local(): call(conv_kernel, jax.ShapeDtypeStruct((count,) + packed_tail, bf16))  2.59 us
  transfers between devices with their start and end apart: 5, of which 4 were waited for; matrix products, arithmetic and copies ran while one was open for 0% of the time, Pallas kernels for 1%

profile of v5, /device:TPU:1, one launch (start us, length us, event | category | flops | bytes accessed | tf_op | source)
XLA Modules:
  0.0 72.2 jit_solution(5309026551948756675)
XLA Ops:
  0.6 0.0 copy-start
  0.6 1.4 %convert_element_type.6.fil_ref = bf16[256,1024]{1,0:T(8,128)(2,1)S(1)} convert(f32[256,1024]{1,0:T(8,128)} %param.14) | non-fusion elementwise | flops 262144 | bytes 1572864 | tf_op jit(solution)/shard_map/convert_element_type | solution.py:254
  2.0 0.0 copy-done
  2.0 0.4 shard_map.113
  2.4 13.3 %conditional.1 = (f32[1,256]{1,0:T(1,128)S(1)}) conditional(s32[]{:T(128)} %convert_element_type.7, f32[1,256]{1,0:T(1,128)S(1)} %get-tuple-element.14, f32[1,256]{1,0:T(1,128)S(1)} %get-tuple-element.14), branch_computations={%region_0.0_spmd, %region_1.0_spmd} | conditional | flops 768 | bytes 17536 | solution.py:269
  2.4 5.5 %collective-permute-start.2 = (f32[1,256]{1,0:T(1,128)S(1)}, f32[1,256]{1,0:T(1,128)S(1)}, u32[]{:S(2)}, u32[]{:S(2)}) collective-permute-start(f32[1,256]{1,0:T(1,128)S(1)} %param.1), channel_id=1, source_target_pairs={{1,7},{3,1},{5,3},{7,5},{9,15},{11,9},{13,11},{15,13},{17,23},{19,... | collective-permute-start | bytes 3080 | tf_op jit(solution)/shard_map/cond/branch_1_fun/ppermute | solution.py:261
  7.9 2.3 %collective-permute-start.1 = (f32[1,256]{1,0:T(1,128)S(1)}, f32[1,256]{1,0:T(1,128)S(1)}, u32[]{:S(2)}, u32[]{:S(2)}) collective-permute-start(f32[1,256]{1,0:T(1,128)S(1)} %param.1), channel_id=1, source_target_pairs={{1,5},{3,7},{5,1},{7,3},{9,13},{11,15},{13,9},{15,11},{17,21},{19,... | collective-permute-start | bytes 3080 | tf_op jit(solution)/shard_map/cond/branch_1_fun/ppermute | solution.py:261
  10.2 2.6 %collective-permute-start = (f32[1,256]{1,0:T(1,128)S(1)}, f32[1,256]{1,0:T(1,128)S(1)}, u32[]{:S(2)}, u32[]{:S(2)}) collective-permute-start(f32[1,256]{1,0:T(1,128)S(1)} %param.1), channel_id=1, source_target_pairs={{1,3},{3,5},{5,7},{7,1},{9,11},{11,13},{13,15},{15,9},{17,19},{19,... | collective-permute-start | bytes 3080 | tf_op jit(solution)/shard_map/cond/branch_1_fun/ppermute | solution.py:261
  12.8 0.0 collective-permute-done.2
  12.8 0.9 %collective-permute-done.1 = f32[1,256]{1,0:T(1,128)S(1)} collective-permute-done((f32[1,256]{1,0:T(1,128)S(1)}, f32[1,256]{1,0:T(1,128)S(1)}, u32[]{:S(2)}, u32[]{:S(2)}) %collective-permute-start.1) | collective-permute-done | bytes 1056 | tf_op jit(solution)/shard_map/cond/branch_1_fun/ppermute | solution.py:261
  13.7 2.0 %collective-permute-done = f32[1,256]{1,0:T(1,128)S(1)} collective-permute-done((f32[1,256]{1,0:T(1,128)S(1)}, f32[1,256]{1,0:T(1,128)S(1)}, u32[]{:S(2)}, u32[]{:S(2)}) %collective-permute-start) | collective-permute-done | bytes 1056 | tf_op jit(solution)/shard_map/cond/branch_1_fun/ppermute | solution.py:261
  15.7 0.0 copy-start.2
  15.7 0.0 copy-start.3
  15.7 0.0 copy-start.4
  15.7 0.0 copy-start.5
  15.7 0.0 copy-start.6
  15.8 0.0 copy-start.7
  15.8 28.7 %all_to_all.10.in_ref = bf16[32,2,4,16,128]{4,3,2,1,0:T(8,128)(2,1)S(1)} all-to-all(bf16[32,2,4,16,128]{4,3,2,1,0:T(8,128)(2,1)S(1)} %get-tuple-element.15), channel_id=1, replica_groups=mesh['ctx'=32,'chan'=4,'section'=2] {'ctx'}, dimensions={0} | all-to-all | bytes 2097152 | tf_op jit(solution)/shard_map/all_to_all | solution.py:271
  44.5 0.0 copy-done.2
  44.5 0.0 copy-done.3
  44.5 0.0 copy-done.4
  44.5 0.0 copy-done.5
  44.5 0.0 copy-done.6
  44.5 0.0 copy-done.7
  44.5 2.6 %shard_map.114 = bf16[32,4,16,128]{3,2,1,0:T(8,128)(2,1)S(1)} custom-call(bf16[32,2,4,16,128]{4,3,2,1,0:T(8,128)(2,1)S(1)} %all_to_all.10.in_ref, bf16[4,256,256]{2,1,0:T(8,128)(2,1)S(1)} %copy-done.3, bf16[4,256,256]{2,1,0:T(8,128)(2,1)S(1)} %copy-done.2, bf16[256,256]{1,0:T(8,128)(2,1)S(1)} %copy-done.5, bf16[256,256]{1,0:T(8,128)(2,1)S(1)} %copy-done.4, ...), custom_call_target="tpu_custom_call" | custom-call | tf_op jit(solution)/shard_map/pallas_call | solution.py:272
  47.1 0.0 copy-start.1
  47.1 0.0 copy-start.8
  47.1 17.6 %all_to_all.11.conv_ref = bf16[32,4,16,128]{3,2,1,0:T(8,128)(2,1)S(1)} all-to-all(bf16[32,4,16,128]{3,2,1,0:T(8,128)(2,1)S(1)} %shard_map.114), channel_id=1, replica_groups=mesh['ctx'=32,'chan'=4,'section'=2] {'ctx'}, dimensions={0} | all-to-all | bytes 1048576 | tf_op jit(solution)/shard_map/all_to_all | solution.py:275
  64.7 0.0 copy-done.1
  64.7 0.0 copy-done.8
  64.7 0.5 shard_map.115
  65.2 1.3 %collective-permute-start.3 = (f32[3,256]{1,0:T(4,128)S(1)}, f32[3,256]{1,0:T(4,128)S(1)}, u32[]{:S(2)}, u32[]{:S(2)}) collective-permute-start(f32[3,256]{1,0:T(4,128)S(1)} %get-tuple-element.17), channel_id=1, source_target_pairs={{0,2},{2,0},{4,6},{6,4},{1,3},{3,1},{5,7},{7,5},{8,10},{10,8},{12,... | collective-permute-start | bytes 9224 | tf_op jit(solution)/shard_map/ppermute | solution.py:291
  66.5 1.2 %collective-permute-done.3 = f32[3,256]{1,0:T(4,128)S(1)} collective-permute-done((f32[3,256]{1,0:T(4,128)S(1)}, f32[3,256]{1,0:T(4,128)S(1)}, u32[]{:S(2)}, u32[]{:S(2)}) %collective-permute-start.3) | collective-permute-done | bytes 3104 | tf_op jit(solution)/shard_map/ppermute | solution.py:291
  67.8 2.8 %collective-permute-start.4 = (f32[3,256]{1,0:T(4,128)S(1)}, f32[3,256]{1,0:T(4,128)S(1)}, u32[]{:S(2)}, u32[]{:S(2)}) collective-permute-start(f32[3,256]{1,0:T(4,128)S(1)} %add.23), channel_id=1, source_target_pairs={{0,6},{2,4},{4,2},{6,0},{1,7},{3,5},{5,3},{7,1},{8,14},{10,12},{12... | collective-permute-start | bytes 9224 | tf_op jit(solution)/shard_map/ppermute | solution.py:291
  70.6 0.8 %shard_map.116 = bf16[256,1024]{1,0:T(8,128)(2,1)} custom-call(bf16[256,1024]{1,0:T(8,128)(2,1)S(1)} %get-tuple-element.16.in_ref), custom_call_target="tpu_custom_call" | custom-call | tf_op jit(solution)/shard_map/pallas_call | solution.py:282
  71.4 0.2 collective-permute-done.4
  71.6 0.6 slice_multiply_fusion
  (3 shorter events, 0.0 us)
Async XLA Ops:
  0.6 1.4 %copy-start = (bf16[256,1024]{1,0:T(8,128)(2,1)S(1)}, bf16[256,1024]{1,0:T(8,128)(2,1)}, u32[]{:S(2)}) copy-start(bf16[256,1024]{1,0:T(8,128)(2,1)} %sig_ref.3) | copy-start | bytes 1572868
  2.4 10.4 %collective-permute-start.2 = (f32[1,256]{1,0:T(1,128)S(1)}, f32[1,256]{1,0:T(1,128)S(1)}, u32[]{:S(2)}, u32[]{:S(2)}) collective-permute-start(f32[1,256]{1,0:T(1,128)S(1)} %param.1), channel_id=1, source_target_pairs={{1,7},{3,1},{5,3},{7,5},{9,15},{11,9},{13,11},{15,13},{17,23},{19,... | collective-permute-start | bytes 3080 | tf_op jit(solution)/shard_map/cond/branch_1_fun/ppermute | solution.py:261
  7.9 5.8 %collective-permute-start.1 = (f32[1,256]{1,0:T(1,128)S(1)}, f32[1,256]{1,0:T(1,128)S(1)}, u32[]{:S(2)}, u32[]{:S(2)}) collective-permute-start(f32[1,256]{1,0:T(1,128)S(1)} %param.1), channel_id=1, source_target_pairs={{1,5},{3,7},{5,1},{7,3},{9,13},{11,15},{13,9},{15,11},{17,21},{19,... | collective-permute-start | bytes 3080 | tf_op jit(solution)/shard_map/cond/branch_1_fun/ppermute | solution.py:261
  10.2 5.5 %collective-permute-start = (f32[1,256]{1,0:T(1,128)S(1)}, f32[1,256]{1,0:T(1,128)S(1)}, u32[]{:S(2)}, u32[]{:S(2)}) collective-permute-start(f32[1,256]{1,0:T(1,128)S(1)} %param.1), channel_id=1, source_target_pairs={{1,3},{3,5},{5,7},{7,1},{9,11},{11,13},{13,15},{15,9},{17,19},{19,... | collective-permute-start | bytes 3080 | tf_op jit(solution)/shard_map/cond/branch_1_fun/ppermute | solution.py:261
  15.7 28.8 %copy-start.2 = (bf16[4,256,256]{2,1,0:T(8,128)(2,1)S(1)}, bf16[4,256,256]{2,1,0:T(8,128)(2,1)}, u32[]{:S(2)}) copy-start(bf16[4,256,256]{2,1,0:T(8,128)(2,1)} %constant.21.clone.io_ref) | copy-start | bytes 1572868
  15.7 28.8 %copy-start.3 = (bf16[4,256,256]{2,1,0:T(8,128)(2,1)S(1)}, bf16[4,256,256]{2,1,0:T(8,128)(2,1)}, u32[]{:S(2)}) copy-start(bf16[4,256,256]{2,1,0:T(8,128)(2,1)} %constant.20.clone.fo_ref) | copy-start | bytes 1572868
  15.7 28.7 %copy-start.4 = (bf16[256,256]{1,0:T(8,128)(2,1)S(1)}, bf16[256,256]{1,0:T(8,128)(2,1)}, u32[]{:S(2)}) copy-start(bf16[256,256]{1,0:T(8,128)(2,1)} %constant.23.clone.ii_ref) | copy-start | bytes 393220
  15.7 28.7 %copy-start.5 = (bf16[256,256]{1,0:T(8,128)(2,1)S(1)}, bf16[256,256]{1,0:T(8,128)(2,1)}, u32[]{:S(2)}) copy-start(bf16[256,256]{1,0:T(8,128)(2,1)} %constant.22.clone.fi_ref) | copy-start | bytes 393220
  15.7 28.7 %copy-start.6 = (f32[64,128]{1,0:T(8,128)S(1)}, f32[64,128]{1,0:T(8,128)}, u32[]{:S(2)}) copy-start(f32[64,128]{1,0:T(8,128)} %constant.25.clone.sin_ref) | copy-start | bytes 98308
  15.8 28.7 %copy-start.7 = (f32[64,128]{1,0:T(8,128)S(1)}, f32[64,128]{1,0:T(8,128)}, u32[]{:S(2)}) copy-start(f32[64,128]{1,0:T(8,128)} %constant.24.clone.cos_ref) | copy-start | bytes 98308
  47.1 17.6 %copy-start.1 = (bf16[256,1024]{1,0:T(8,128)(2,1)S(1)}, bf16[256,1024]{1,0:T(8,128)(2,1)}, u32[]{:S(2)}) copy-start(bf16[256,1024]{1,0:T(8,128)(2,1)} %gate_ref.1) | copy-start | bytes 1572868
  47.1 17.6 %copy-start.8 = (f32[1024]{0:T(1024)S(1)}, f32[1024]{0:T(1024)}, u32[]{:S(2)}) copy-start(f32[1024]{0:T(1024)} %param.15) | copy-start | bytes 12292
  65.2 2.5 %collective-permute-start.3 = (f32[3,256]{1,0:T(4,128)S(1)}, f32[3,256]{1,0:T(4,128)S(1)}, u32[]{:S(2)}, u32[]{:S(2)}) collective-permute-start(f32[3,256]{1,0:T(4,128)S(1)} %get-tuple-element.17), channel_id=1, source_target_pairs={{0,2},{2,0},{4,6},{6,4},{1,3},{3,1},{5,7},{7,5},{8,10},{10,8},{12,... | collective-permute-start | bytes 9224 | tf_op jit(solution)/shard_map/ppermute | solution.py:291
  67.8 3.8 %collective-permute-start.4 = (f32[3,256]{1,0:T(4,128)S(1)}, f32[3,256]{1,0:T(4,128)S(1)}, u32[]{:S(2)}, u32[]{:S(2)}) collective-permute-start(f32[3,256]{1,0:T(4,128)S(1)} %add.23), channel_id=1, source_target_pairs={{0,6},{2,4},{4,2},{6,0},{1,7},{3,5},{5,3},{7,1},{8,14},{10,12},{12... | collective-permute-start | bytes 9224 | tf_op jit(solution)/shard_map/ppermute | solution.py:291

commit v6 on v5

--- a/solution.py
+++ b/solution.py
@@ -18,6 +18,21 @@
 COS, SIN, HALF = math.cos(math.pi / 8), math.sin(math.pi / 8), math.sqrt(0.5)
 
 
+def two_parts(table):
+    high = table.astype(ml_dtypes.bfloat16)
+    low = (table - high.astype(np.float64)).astype(ml_dtypes.bfloat16)
+    return np.concatenate([high, low], axis=-1)
+
+
+def mild_scale(table):
+    scales = 1 + np.arange(1000) / 1000
+    errors = [
+        np.square((scale * table).astype(ml_dtypes.bfloat16).astype(np.float64) / scale - table).mean()
+        for scale in scales
+    ]
+    return scales[int(np.argmin(errors))]
+
+
 def conv_tables(blocks, span):
     total = blocks * span
     few = blocks // RADIX
@@ -34,11 +49,12 @@
         eye = np.eye(GROUP)
         return split(np.kron(np.cos(angles), eye), np.kron(np.sin(angles), eye))
 
-    fwd_outer = np.stack([spread(-angles) for angles in outer])
-    inv_outer = np.stack([spread(angles.T) for angles in outer])
-    fwd_inner = split(np.cos(inner), np.sin(inner))
-    inv_inner = split(np.cos(inner), -np.sin(inner)) / total
-    short = [t.astype(ml_dtypes.bfloat16) for t in (fwd_outer, inv_outer, fwd_inner, inv_inner)]
+    scale = mild_scale(np.cos(inner))
+    fwd_outer = two_parts(np.stack([spread(-angles) for angles in outer]))
+    inv_outer = two_parts(np.stack([spread(angles.T) for angles in outer]) / (total * scale**3))
+    fwd_inner = (scale * split(np.cos(inner), np.sin(inner))).astype(ml_dtypes.bfloat16)
+    inv_inner = (scale * split(np.cos(inner), -np.sin(inner))).astype(ml_dtypes.bfloat16)
+    short = [fwd_outer, inv_outer, fwd_inner, inv_inner]
     wide = [np.cos(twiddle).astype(np.float32), np.sin(twiddle).astype(np.float32)]
     return short + wide
 
@@ -70,6 +86,11 @@
 
 def dot(left, right):
     return jnp.dot(left, right, preferred_element_type=jnp.float32)
+
+
+def outer_dot(table, values):
+    values = values.astype(jnp.bfloat16)
+    return dot(table, jnp.concatenate([values, values], axis=0))
 
 
 def tile_copies(hbm_ref, buf_ref, sem_ref):
@@ -129,7 +150,7 @@
             ]
             blocks.append(jnp.concatenate(pair, axis=1).astype(jnp.float32))
         return [
-            dot(fo_ref[j], jnp.concatenate([re, im], axis=0).astype(jnp.bfloat16))
+            outer_dot(fo_ref[j], jnp.concatenate([re, im], axis=0))
             for j, (re, im) in enumerate(quarters(*blocks))
         ]
 
@@ -165,7 +186,7 @@
     def finish(group, first, second):
         parts = []
         for j, pair in enumerate(zip(first, second)):
-            part = dot(io_ref[j], jnp.concatenate(pair, axis=1))
+            part = outer_dot(io_ref[j], jnp.concatenate(pair, axis=1))
             parts.append((part[:size], part[size:]))
         for q, conv in enumerate(recombined(parts)):
             conv = conv.astype(jnp.bfloat16)
@@ -190,7 +211,7 @@
     return part
 
 
-def finish_kernel(conv_ref, sig_ref, gate_ref, skip_ref, out_ref, sums_ref):
+def finish_kernel(conv_ref, sig_ref, gate_ref, skip_ref, sq_ref, out_ref, sums_ref):
     devices, groups, rows, lanes = conv_ref.shape
     parts = rows // GROUP
     span, channels = out_ref.shape
@@ -210,10 +231,11 @@
         sig = sig_ref[:, at].astype(jnp.float32)
         mixed = gate_ref[:, at].astype(jnp.float32) * (conv + skip_ref[:, at] * sig)
         out_ref[:, at] = mixed.astype(jnp.bfloat16)
-        terms = [token_sums(sig * mixed), token_sums(sig * sig), token_sums(mixed * mixed)]
+        terms = [token_sums(sig * mixed), token_sums(mixed * mixed)]
         sums = terms if sums is None else [a + b for a, b in zip(sums, terms)]
     for row, total in enumerate(sums):
         sums_ref[row : row + 1] = jnp.sum(total.T, axis=0, keepdims=True)
+    sums_ref[2:3] = sq_ref[...]
 
 
 def deliver_kernel(in_ref, out_ref, sem_ref):
@@ -276,9 +298,9 @@
     mixed, sums = call(
         finish_kernel,
         (jax.ShapeDtypeStruct((span, channels), bf16), jax.ShapeDtypeStruct((3, span), f32)),
-        in_specs=[vmem] * 4,
+        in_specs=[vmem] * 5,
         out_specs=(vmem, vmem),
-    )(returned, signal, gating, skip_gain.reshape(1, channels))
+    )(returned, signal, gating, skip_gain.reshape(1, channels), sig_sq)
     result = call(
         deliver_kernel,
         jax.ShapeDtypeStruct((span, channels), bf16),
@@ -290,7 +312,7 @@
     while reach <= chans:
         sums = sums + lax.ppermute(sums, "chan", [(i, i ^ (reach - 1)) for i in range(chans)])
         reach *= 2
-    inner_total, sig_total, out_total = sums
+    inner_total, out_total, sig_total = sums
     sig_total = jnp.where(is_last, sig_sq[0], sig_total)
     cosine = inner_total / jnp.sqrt((sig_total + EPSILON) * (out_total + EPSILON))
     return (result, cosine)

time: 72.4 us -> 73.2 us (1.011)
  Pallas kernels: 4.34 us -> 5.1 us
    pallas_call x1, Pallas kernels: 2.59 us -> 3.38 us  [local(): call(conv_kernel, jax.ShapeDtypeStruct((count,) + packed_tail, bf16))]
where the time goes in v6:
time: 73.2 us; the launch traced here: 72.9 us
  blocking collectives  46.3 us (63%)
  starting transfers between devices  14.4 us (20%)
  Pallas kernels  5.1 us (7%)
  waiting for transfers between devices  4.32 us (6%)
  other arithmetic  1.95 us (3%)
  between operations  0.77 us (1%)
    all_to_all x1, blocking collectives, local(): lax.all_to_all(packed, 'ctx', split_axis=0, concat_axis=0, tiled=True)  28.7 us
    all_to_all x1, blocking collectives, local(): lax.all_to_all(conv, 'ctx', split_axis=0, concat_axis=0, tiled=True)  17.6 us
    ppermute x3, starting transfers between devices, total_first(): lax.ppermute(part, ('chan', 'section'), [(i * sections + last, (i + hop)...  10.3 us
    ppermute x2, starting transfers between devices, local(): lax.ppermute(sums, 'chan', [(i, i ^ reach - 1) for i in range(chans)])  4.11 us
    pallas_call x1, Pallas kernels, local(): call(conv_kernel, jax.ShapeDtypeStruct((count,) + packed_tail, bf16))  3.38 us
    ppermute x3, waiting for transfers between devices, total_first(): lax.ppermute(part, ('chan', 'section'), [(i * sections + last, (i + hop)...  2.91 us
  transfers between devices with their start and end apart: 5, of which 4 were waited for; matrix products, arithmetic and copies ran while one was open for 0% of the time, Pallas kernels for 1%

profile of v6, /device:TPU:1, one launch (start us, length us, event | category | flops | bytes accessed | tf_op | source)
XLA Modules:
  0.0 72.9 jit_solution(15532246272070347790)
XLA Ops:
  0.6 0.0 copy-start
  0.6 1.4 %convert_element_type.6.fil_ref = bf16[256,1024]{1,0:T(8,128)(2,1)S(1)} convert(f32[256,1024]{1,0:T(8,128)} %param.14) | non-fusion elementwise | flops 262144 | bytes 1572864 | tf_op jit(solution)/shard_map/convert_element_type | solution.py:276
  2.0 0.0 copy-done
  2.0 0.0 copy-start.4
  2.0 0.0 copy-start.5
  2.0 0.0 copy-start.6
  2.0 0.0 copy-start.7
  2.1 0.4 shard_map.113
  2.5 13.3 %conditional.1 = (f32[1,256]{1,0:T(1,128)S(1)}) conditional(s32[]{:T(128)} %convert_element_type.7, f32[1,256]{1,0:T(1,128)S(1)} %get-tuple-element.14, f32[1,256]{1,0:T(1,128)S(1)} %get-tuple-element.14), branch_computations={%region_0.0_spmd, %region_1.0_spmd} | conditional | flops 768 | bytes 17536 | solution.py:291
  2.5 5.5 %collective-permute-start.2 = (f32[1,256]{1,0:T(1,128)S(1)}, f32[1,256]{1,0:T(1,128)S(1)}, u32[]{:S(2)}, u32[]{:S(2)}) collective-permute-start(f32[1,256]{1,0:T(1,128)S(1)} %param.1), channel_id=1, source_target_pairs={{1,7},{3,1},{5,3},{7,5},{9,15},{11,9},{13,11},{15,13},{17,23},{19,... | collective-permute-start | bytes 3080 | tf_op jit(solution)/shard_map/cond/branch_1_fun/ppermute | solution.py:283
  8.0 2.3 %collective-permute-start.1 = (f32[1,256]{1,0:T(1,128)S(1)}, f32[1,256]{1,0:T(1,128)S(1)}, u32[]{:S(2)}, u32[]{:S(2)}) collective-permute-start(f32[1,256]{1,0:T(1,128)S(1)} %param.1), channel_id=1, source_target_pairs={{1,5},{3,7},{5,1},{7,3},{9,13},{11,15},{13,9},{15,11},{17,21},{19,... | collective-permute-start | bytes 3080 | tf_op jit(solution)/shard_map/cond/branch_1_fun/ppermute | solution.py:283
  10.2 2.6 %collective-permute-start = (f32[1,256]{1,0:T(1,128)S(1)}, f32[1,256]{1,0:T(1,128)S(1)}, u32[]{:S(2)}, u32[]{:S(2)}) collective-permute-start(f32[1,256]{1,0:T(1,128)S(1)} %param.1), channel_id=1, source_target_pairs={{1,3},{3,5},{5,7},{7,1},{9,11},{11,13},{13,15},{15,9},{17,19},{19,... | collective-permute-start | bytes 3080 | tf_op jit(solution)/shard_map/cond/branch_1_fun/ppermute | solution.py:283
  12.8 0.0 collective-permute-done.2
  12.8 0.9 %collective-permute-done.1 = f32[1,256]{1,0:T(1,128)S(1)} collective-permute-done((f32[1,256]{1,0:T(1,128)S(1)}, f32[1,256]{1,0:T(1,128)S(1)}, u32[]{:S(2)}, u32[]{:S(2)}) %collective-permute-start.1) | collective-permute-done | bytes 1056 | tf_op jit(solution)/shard_map/cond/branch_1_fun/ppermute | solution.py:283
  13.8 2.0 %collective-permute-done = f32[1,256]{1,0:T(1,128)S(1)} collective-permute-done((f32[1,256]{1,0:T(1,128)S(1)}, f32[1,256]{1,0:T(1,128)S(1)}, u32[]{:S(2)}, u32[]{:S(2)}) %collective-permute-start) | collective-permute-done | bytes 1056 | tf_op jit(solution)/shard_map/cond/branch_1_fun/ppermute | solution.py:283
  15.8 0.0 copy-start.1
  15.8 0.0 copy-start.2
  15.8 28.7 %all_to_all.10.in_ref = bf16[32,2,4,16,128]{4,3,2,1,0:T(8,128)(2,1)S(1)} all-to-all(bf16[32,2,4,16,128]{4,3,2,1,0:T(8,128)(2,1)S(1)} %get-tuple-element.15), channel_id=1, replica_groups=mesh['ctx'=32,'chan'=4,'section'=2] {'ctx'}, dimensions={0} | all-to-all | bytes 2097152 | tf_op jit(solution)/shard_map/all_to_all | solution.py:293
  44.5 0.0 copy-done.4
  44.5 0.0 copy-done.5
  44.5 0.0 copy-done.6
  44.5 0.0 copy-done.7
  44.5 0.0 copy-done.1
  44.5 0.0 copy-done.2
  44.5 3.4 %shard_map.114 = bf16[32,4,16,128]{3,2,1,0:T(8,128)(2,1)S(1)} custom-call(bf16[32,2,4,16,128]{4,3,2,1,0:T(8,128)(2,1)S(1)} %all_to_all.10.in_ref, bf16[4,256,512]{2,1,0:T(8,128)(2,1)S(1)} %copy-done.2, bf16[4,256,512]{2,1,0:T(8,128)(2,1)S(1)} %copy-done.1, bf16[256,256]{1,0:T(8,128)(2,1)S(1)} %copy-done.5, bf16[256,256]{1,0:T(8,128)(2,1)S(1)} %copy-done.4, ...), custom_call_target="tpu_custom_call" | custom-call | tf_op jit(solution)/shard_map/pallas_call | solution.py:294
  47.9 0.0 copy-start.3
  47.9 0.0 copy-start.8
  47.9 17.6 %all_to_all.11.conv_ref = bf16[32,4,16,128]{3,2,1,0:T(8,128)(2,1)S(1)} all-to-all(bf16[32,4,16,128]{3,2,1,0:T(8,128)(2,1)S(1)} %shard_map.114), channel_id=1, replica_groups=mesh['ctx'=32,'chan'=4,'section'=2] {'ctx'}, dimensions={0} | all-to-all | bytes 1048576 | tf_op jit(solution)/shard_map/all_to_all | solution.py:297
  65.5 0.0 copy-done.3
  65.5 0.0 copy-done.8
  65.5 0.5 shard_map.115
  66.0 1.3 %collective-permute-start.3 = (f32[3,256]{1,0:T(4,128)S(1)}, f32[3,256]{1,0:T(4,128)S(1)}, u32[]{:S(2)}, u32[]{:S(2)}) collective-permute-start(f32[3,256]{1,0:T(4,128)S(1)} %get-tuple-element.18), channel_id=1, source_target_pairs={{0,2},{2,0},{4,6},{6,4},{1,3},{3,1},{5,7},{7,5},{8,10},{10,8},{12,... | collective-permute-start | bytes 9224 | tf_op jit(solution)/shard_map/ppermute | solution.py:313
  67.3 1.2 %collective-permute-done.3 = f32[3,256]{1,0:T(4,128)S(1)} collective-permute-done((f32[3,256]{1,0:T(4,128)S(1)}, f32[3,256]{1,0:T(4,128)S(1)}, u32[]{:S(2)}, u32[]{:S(2)}) %collective-permute-start.3) | collective-permute-done | bytes 3104 | tf_op jit(solution)/shard_map/ppermute | solution.py:313
  68.5 2.8 %collective-permute-start.4 = (f32[3,256]{1,0:T(4,128)S(1)}, f32[3,256]{1,0:T(4,128)S(1)}, u32[]{:S(2)}, u32[]{:S(2)}) collective-permute-start(f32[3,256]{1,0:T(4,128)S(1)} %add.23), channel_id=1, source_target_pairs={{0,6},{2,4},{4,2},{6,0},{1,7},{3,5},{5,3},{7,1},{8,14},{10,12},{12... | collective-permute-start | bytes 9224 | tf_op jit(solution)/shard_map/ppermute | solution.py:313
  71.3 0.8 %shard_map.116 = bf16[256,1024]{1,0:T(8,128)(2,1)} custom-call(bf16[256,1024]{1,0:T(8,128)(2,1)S(1)} %get-tuple-element.17.in_ref), custom_call_target="tpu_custom_call" | custom-call | tf_op jit(solution)/shard_map/pallas_call | solution.py:304
  72.2 0.2 collective-permute-done.4
  72.3 0.6 slice_multiply_fusion
  (3 shorter events, 0.0 us)
Async XLA Ops:
  0.6 1.4 %copy-start = (bf16[256,1024]{1,0:T(8,128)(2,1)S(1)}, bf16[256,1024]{1,0:T(8,128)(2,1)}, u32[]{:S(2)}) copy-start(bf16[256,1024]{1,0:T(8,128)(2,1)} %sig_ref.3) | copy-start | bytes 1572868
  2.0 42.4 %copy-start.4 = (bf16[256,256]{1,0:T(8,128)(2,1)S(1)}, bf16[256,256]{1,0:T(8,128)(2,1)}, u32[]{:S(2)}) copy-start(bf16[256,256]{1,0:T(8,128)(2,1)} %constant.23.clone.ii_ref) | copy-start | bytes 393220
  2.0 42.4 %copy-start.5 = (bf16[256,256]{1,0:T(8,128)(2,1)S(1)}, bf16[256,256]{1,0:T(8,128)(2,1)}, u32[]{:S(2)}) copy-start(bf16[256,256]{1,0:T(8,128)(2,1)} %constant.22.clone.fi_ref) | copy-start | bytes 393220
  2.0 42.4 %copy-start.6 = (f32[64,128]{1,0:T(8,128)S(1)}, f32[64,128]{1,0:T(8,128)}, u32[]{:S(2)}) copy-start(f32[64,128]{1,0:T(8,128)} %constant.25.clone.sin_ref) | copy-start | bytes 98308
  2.0 42.4 %copy-start.7 = (f32[64,128]{1,0:T(8,128)S(1)}, f32[64,128]{1,0:T(8,128)}, u32[]{:S(2)}) copy-start(f32[64,128]{1,0:T(8,128)} %constant.24.clone.cos_ref) | copy-start | bytes 98308
  2.5 10.4 %collective-permute-start.2 = (f32[1,256]{1,0:T(1,128)S(1)}, f32[1,256]{1,0:T(1,128)S(1)}, u32[]{:S(2)}, u32[]{:S(2)}) collective-permute-start(f32[1,256]{1,0:T(1,128)S(1)} %param.1), channel_id=1, source_target_pairs={{1,7},{3,1},{5,3},{7,5},{9,15},{11,9},{13,11},{15,13},{17,23},{19,... | collective-permute-start | bytes 3080 | tf_op jit(solution)/shard_map/cond/branch_1_fun/ppermute | solution.py:283
  8.0 5.8 %collective-permute-start.1 = (f32[1,256]{1,0:T(1,128)S(1)}, f32[1,256]{1,0:T(1,128)S(1)}, u32[]{:S(2)}, u32[]{:S(2)}) collective-permute-start(f32[1,256]{1,0:T(1,128)S(1)} %param.1), channel_id=1, source_target_pairs={{1,5},{3,7},{5,1},{7,3},{9,13},{11,15},{13,9},{15,11},{17,21},{19,... | collective-permute-start | bytes 3080 | tf_op jit(solution)/shard_map/cond/branch_1_fun/ppermute | solution.py:283
  10.2 5.5 %collective-permute-start = (f32[1,256]{1,0:T(1,128)S(1)}, f32[1,256]{1,0:T(1,128)S(1)}, u32[]{:S(2)}, u32[]{:S(2)}) collective-permute-start(f32[1,256]{1,0:T(1,128)S(1)} %param.1), channel_id=1, source_target_pairs={{1,3},{3,5},{5,7},{7,1},{9,11},{11,13},{13,15},{15,9},{17,19},{19,... | collective-permute-start | bytes 3080 | tf_op jit(solution)/shard_map/cond/branch_1_fun/ppermute | solution.py:283
  15.8 28.7 %copy-start.1 = (bf16[4,256,512]{2,1,0:T(8,128)(2,1)S(1)}, bf16[4,256,512]{2,1,0:T(8,128)(2,1)}, u32[]{:S(2)}) copy-start(bf16[4,256,512]{2,1,0:T(8,128)(2,1)} %constant.21.clone.io_ref) | copy-start | bytes 3145732
  15.8 28.7 %copy-start.2 = (bf16[4,256,512]{2,1,0:T(8,128)(2,1)S(1)}, bf16[4,256,512]{2,1,0:T(8,128)(2,1)}, u32[]{:S(2)}) copy-start(bf16[4,256,512]{2,1,0:T(8,128)(2,1)} %constant.20.clone.fo_ref) | copy-start | bytes 3145732
  47.9 17.6 %copy-start.3 = (bf16[256,1024]{1,0:T(8,128)(2,1)S(1)}, bf16[256,1024]{1,0:T(8,128)(2,1)}, u32[]{:S(2)}) copy-start(bf16[256,1024]{1,0:T(8,128)(2,1)} %gate_ref.1) | copy-start | bytes 1572868
  47.9 17.6 %copy-start.8 = (f32[1024]{0:T(1024)S(1)}, f32[1024]{0:T(1024)}, u32[]{:S(2)}) copy-start(f32[1024]{0:T(1024)} %param.15) | copy-start | bytes 12292
  66.0 2.5 %collective-permute-start.3 = (f32[3,256]{1,0:T(4,128)S(1)}, f32[3,256]{1,0:T(4,128)S(1)}, u32[]{:S(2)}, u32[]{:S(2)}) collective-permute-start(f32[3,256]{1,0:T(4,128)S(1)} %get-tuple-element.18), channel_id=1, source_target_pairs={{0,2},{2,0},{4,6},{6,4},{1,3},{3,1},{5,7},{7,5},{8,10},{10,8},{12,... | collective-permute-start | bytes 9224 | tf_op jit(solution)/shard_map/ppermute | solution.py:313
  68.5 3.8 %collective-permute-start.4 = (f32[3,256]{1,0:T(4,128)S(1)}, f32[3,256]{1,0:T(4,128)S(1)}, u32[]{:S(2)}, u32[]{:S(2)}) collective-permute-start(f32[3,256]{1,0:T(4,128)S(1)} %add.23), channel_id=1, source_target_pairs={{0,6},{2,4},{4,2},{6,0},{1,7},{3,5},{5,3},{7,1},{8,14},{10,12},{12... | collective-permute-start | bytes 9224 | tf_op jit(solution)/shard_map/ppermute | solution.py:313

commit v7 on v6

--- a/solution.py
+++ b/solution.py
@@ -25,7 +25,7 @@
 
 
 def mild_scale(table):
-    scales = 1 + np.arange(1000) / 1000
+    scales = 1 + np.arange(4000) / 4000
     errors = [
         np.square((scale * table).astype(ml_dtypes.bfloat16).astype(np.float64) / scale - table).mean()
         for scale in scales
@@ -49,12 +49,13 @@
         eye = np.eye(GROUP)
         return split(np.kron(np.cos(angles), eye), np.kron(np.sin(angles), eye))
 
-    scale = mild_scale(np.cos(inner))
-    fwd_outer = two_parts(np.stack([spread(-angles) for angles in outer]))
-    inv_outer = two_parts(np.stack([spread(angles.T) for angles in outer]) / (total * scale**3))
-    fwd_inner = (scale * split(np.cos(inner), np.sin(inner))).astype(ml_dtypes.bfloat16)
-    inv_inner = (scale * split(np.cos(inner), -np.sin(inner))).astype(ml_dtypes.bfloat16)
-    short = [fwd_outer, inv_outer, fwd_inner, inv_inner]
+    inner_scale, outer_scale = mild_scale(np.cos(inner)), mild_scale(np.cos(outer))
+    first_scale = (total * inner_scale**3 * outer_scale) ** -0.5
+    fwd_outer = two_parts(first_scale * np.stack([spread(-angles) for angles in outer]))
+    inv_outer = outer_scale * np.stack([spread(angles.T) for angles in outer])
+    fwd_inner = inner_scale * split(np.cos(inner), np.sin(inner))
+    inv_inner = inner_scale * split(np.cos(inner), -np.sin(inner))
+    short = [fwd_outer] + [t.astype(ml_dtypes.bfloat16) for t in (inv_outer, fwd_inner, inv_inner)]
     wide = [np.cos(twiddle).astype(np.float32), np.sin(twiddle).astype(np.float32)]
     return short + wide
 
@@ -186,7 +187,7 @@
     def finish(group, first, second):
         parts = []
         for j, pair in enumerate(zip(first, second)):
-            part = outer_dot(io_ref[j], jnp.concatenate(pair, axis=1))
+            part = dot(io_ref[j], jnp.concatenate(pair, axis=1))
             parts.append((part[:size], part[size:]))
         for q, conv in enumerate(recombined(parts)):
             conv = conv.astype(jnp.bfloat16)

time: 73.2 us -> 72.8 us (level)
  no operation moved by 1% of the time
where the time goes in v7:
time: 72.8 us; the launch traced here: 72.6 us
  blocking collectives  46.3 us (64%)
  starting transfers between devices  14.4 us (20%)
  Pallas kernels  4.72 us (6%)
  waiting for transfers between devices  4.32 us (6%)
  other arithmetic  1.95 us (3%)
  between operations  0.77 us (1%)
    all_to_all x1, blocking collectives, local(): lax.all_to_all(packed, 'ctx', split_axis=0, concat_axis=0, tiled=True)  28.7 us
    all_to_all x1, blocking collectives, local(): lax.all_to_all(conv, 'ctx', split_axis=0, concat_axis=0, tiled=True)  17.6 us
    ppermute x3, starting transfers between devices, total_first(): lax.ppermute(part, ('chan', 'section'), [(i * sections + last, (i + hop)...  10.3 us
    ppermute x2, starting transfers between devices, local(): lax.ppermute(sums, 'chan', [(i, i ^ reach - 1) for i in range(chans)])  4.11 us
    pallas_call x1, Pallas kernels, local(): call(conv_kernel, jax.ShapeDtypeStruct((count,) + packed_tail, bf16))  3.01 us
    ppermute x3, waiting for transfers between devices, total_first(): lax.ppermute(part, ('chan', 'section'), [(i * sections + last, (i + hop)...  2.91 us
  transfers between devices with their start and end apart: 5, of which 4 were waited for; matrix products, arithmetic and copies ran while one was open for 0% of the time, Pallas kernels for 1%

profile of v7, /device:TPU:1, one launch (start us, length us, event | category | flops | bytes accessed | tf_op | source)
XLA Modules:
  0.0 72.6 jit_solution(2721651164044625224)
XLA Ops:
  0.6 0.0 copy-start
  0.6 1.4 %convert_element_type.6.fil_ref = bf16[256,1024]{1,0:T(8,128)(2,1)S(1)} convert(f32[256,1024]{1,0:T(8,128)} %param.14) | non-fusion elementwise | flops 262144 | bytes 1572864 | tf_op jit(solution)/shard_map/convert_element_type | solution.py:277
  2.0 0.0 copy-done
  2.0 0.4 shard_map.113
  2.4 13.3 %conditional.1 = (f32[1,256]{1,0:T(1,128)S(1)}) conditional(s32[]{:T(128)} %convert_element_type.7, f32[1,256]{1,0:T(1,128)S(1)} %get-tuple-element.14, f32[1,256]{1,0:T(1,128)S(1)} %get-tuple-element.14), branch_computations={%region_0.0_spmd, %region_1.0_spmd} | conditional | flops 768 | bytes 17536 | solution.py:292
  2.4 5.5 %collective-permute-start.2 = (f32[1,256]{1,0:T(1,128)S(1)}, f32[1,256]{1,0:T(1,128)S(1)}, u32[]{:S(2)}, u32[]{:S(2)}) collective-permute-start(f32[1,256]{1,0:T(1,128)S(1)} %param.1), channel_id=1, source_target_pairs={{1,7},{3,1},{5,3},{7,5},{9,15},{11,9},{13,11},{15,13},{17,23},{19,... | collective-permute-start | bytes 3080 | tf_op jit(solution)/shard_map/cond/branch_1_fun/ppermute | solution.py:284
  7.9 2.3 %collective-permute-start.1 = (f32[1,256]{1,0:T(1,128)S(1)}, f32[1,256]{1,0:T(1,128)S(1)}, u32[]{:S(2)}, u32[]{:S(2)}) collective-permute-start(f32[1,256]{1,0:T(1,128)S(1)} %param.1), channel_id=1, source_target_pairs={{1,5},{3,7},{5,1},{7,3},{9,13},{11,15},{13,9},{15,11},{17,21},{19,... | collective-permute-start | bytes 3080 | tf_op jit(solution)/shard_map/cond/branch_1_fun/ppermute | solution.py:284
  10.2 2.6 %collective-permute-start = (f32[1,256]{1,0:T(1,128)S(1)}, f32[1,256]{1,0:T(1,128)S(1)}, u32[]{:S(2)}, u32[]{:S(2)}) collective-permute-start(f32[1,256]{1,0:T(1,128)S(1)} %param.1), channel_id=1, source_target_pairs={{1,3},{3,5},{5,7},{7,1},{9,11},{11,13},{13,15},{15,9},{17,19},{19,... | collective-permute-start | bytes 3080 | tf_op jit(solution)/shard_map/cond/branch_1_fun/ppermute | solution.py:284
  12.8 0.0 collective-permute-done.2
  12.8 0.9 %collective-permute-done.1 = f32[1,256]{1,0:T(1,128)S(1)} collective-permute-done((f32[1,256]{1,0:T(1,128)S(1)}, f32[1,256]{1,0:T(1,128)S(1)}, u32[]{:S(2)}, u32[]{:S(2)}) %collective-permute-start.1) | collective-permute-done | bytes 1056 | tf_op jit(solution)/shard_map/cond/branch_1_fun/ppermute | solution.py:284
  13.7 2.0 %collective-permute-done = f32[1,256]{1,0:T(1,128)S(1)} collective-permute-done((f32[1,256]{1,0:T(1,128)S(1)}, f32[1,256]{1,0:T(1,128)S(1)}, u32[]{:S(2)}, u32[]{:S(2)}) %collective-permute-start) | collective-permute-done | bytes 1056 | tf_op jit(solution)/shard_map/cond/branch_1_fun/ppermute | solution.py:284
  15.7 0.0 copy-start.1
  15.7 0.0 copy-start.3
  15.7 0.0 copy-start.4
  15.7 0.0 copy-start.5
  15.7 0.0 copy-start.6
  15.8 0.0 copy-start.7
  15.8 28.7 %all_to_all.10.in_ref = bf16[32,2,4,16,128]{4,3,2,1,0:T(8,128)(2,1)S(1)} all-to-all(bf16[32,2,4,16,128]{4,3,2,1,0:T(8,128)(2,1)S(1)} %get-tuple-element.15), channel_id=1, replica_groups=mesh['ctx'=32,'chan'=4,'section'=2] {'ctx'}, dimensions={0} | all-to-all | bytes 2097152 | tf_op jit(solution)/shard_map/all_to_all | solution.py:294
  44.5 0.0 copy-done.1
  44.5 0.0 copy-done.3
  44.5 0.0 copy-done.4
  44.5 0.0 copy-done.5
  44.5 0.0 copy-done.6
  44.5 0.0 copy-done.7
  44.5 3.0 %shard_map.114 = bf16[32,4,16,128]{3,2,1,0:T(8,128)(2,1)S(1)} custom-call(bf16[32,2,4,16,128]{4,3,2,1,0:T(8,128)(2,1)S(1)} %all_to_all.10.in_ref, bf16[4,256,512]{2,1,0:T(8,128)(2,1)S(1)} %copy-done.1, bf16[4,256,256]{2,1,0:T(8,128)(2,1)S(1)} %copy-done.3, bf16[256,256]{1,0:T(8,128)(2,1)S(1)} %copy-done.5, bf16[256,256]{1,0:T(8,128)(2,1)S(1)} %copy-done.4, ...), custom_call_target="tpu_custom_call" | custom-call | tf_op jit(solution)/shard_map/pallas_call | solution.py:295
  47.5 0.0 copy-start.2
  47.5 0.0 copy-start.8
  47.5 17.6 %all_to_all.11.conv_ref = bf16[32,4,16,128]{3,2,1,0:T(8,128)(2,1)S(1)} all-to-all(bf16[32,4,16,128]{3,2,1,0:T(8,128)(2,1)S(1)} %shard_map.114), channel_id=1, replica_groups=mesh['ctx'=32,'chan'=4,'section'=2] {'ctx'}, dimensions={0} | all-to-all | bytes 1048576 | tf_op jit(solution)/shard_map/all_to_all | solution.py:298
  65.1 0.0 copy-done.2
  65.1 0.0 copy-done.8
  65.1 0.5 shard_map.115
  65.6 1.3 %collective-permute-start.3 = (f32[3,256]{1,0:T(4,128)S(1)}, f32[3,256]{1,0:T(4,128)S(1)}, u32[]{:S(2)}, u32[]{:S(2)}) collective-permute-start(f32[3,256]{1,0:T(4,128)S(1)} %get-tuple-element.18), channel_id=1, source_target_pairs={{0,2},{2,0},{4,6},{6,4},{1,3},{3,1},{5,7},{7,5},{8,10},{10,8},{12,... | collective-permute-start | bytes 9224 | tf_op jit(solution)/shard_map/ppermute | solution.py:314
  66.9 1.2 %collective-permute-done.3 = f32[3,256]{1,0:T(4,128)S(1)} collective-permute-done((f32[3,256]{1,0:T(4,128)S(1)}, f32[3,256]{1,0:T(4,128)S(1)}, u32[]{:S(2)}, u32[]{:S(2)}) %collective-permute-start.3) | collective-permute-done | bytes 3104 | tf_op jit(solution)/shard_map/ppermute | solution.py:314
  68.2 2.8 %collective-permute-start.4 = (f32[3,256]{1,0:T(4,128)S(1)}, f32[3,256]{1,0:T(4,128)S(1)}, u32[]{:S(2)}, u32[]{:S(2)}) collective-permute-start(f32[3,256]{1,0:T(4,128)S(1)} %add.23), channel_id=1, source_target_pairs={{0,6},{2,4},{4,2},{6,0},{1,7},{3,5},{5,3},{7,1},{8,14},{10,12},{12... | collective-permute-start | bytes 9224 | tf_op jit(solution)/shard_map/ppermute | solution.py:314
  71.0 0.8 %shard_map.116 = bf16[256,1024]{1,0:T(8,128)(2,1)} custom-call(bf16[256,1024]{1,0:T(8,128)(2,1)S(1)} %get-tuple-element.17.in_ref), custom_call_target="tpu_custom_call" | custom-call | tf_op jit(solution)/shard_map/pallas_call | solution.py:305
  71.8 0.2 collective-permute-done.4
  72.0 0.6 slice_multiply_fusion
  (3 shorter events, 0.0 us)
Async XLA Ops:
  0.6 1.4 %copy-start = (bf16[256,1024]{1,0:T(8,128)(2,1)S(1)}, bf16[256,1024]{1,0:T(8,128)(2,1)}, u32[]{:S(2)}) copy-start(bf16[256,1024]{1,0:T(8,128)(2,1)} %sig_ref.3) | copy-start | bytes 1572868
  2.4 10.4 %collective-permute-start.2 = (f32[1,256]{1,0:T(1,128)S(1)}, f32[1,256]{1,0:T(1,128)S(1)}, u32[]{:S(2)}, u32[]{:S(2)}) collective-permute-start(f32[1,256]{1,0:T(1,128)S(1)} %param.1), channel_id=1, source_target_pairs={{1,7},{3,1},{5,3},{7,5},{9,15},{11,9},{13,11},{15,13},{17,23},{19,... | collective-permute-start | bytes 3080 | tf_op jit(solution)/shard_map/cond/branch_1_fun/ppermute | solution.py:284
  7.9 5.8 %collective-permute-start.1 = (f32[1,256]{1,0:T(1,128)S(1)}, f32[1,256]{1,0:T(1,128)S(1)}, u32[]{:S(2)}, u32[]{:S(2)}) collective-permute-start(f32[1,256]{1,0:T(1,128)S(1)} %param.1), channel_id=1, source_target_pairs={{1,5},{3,7},{5,1},{7,3},{9,13},{11,15},{13,9},{15,11},{17,21},{19,... | collective-permute-start | bytes 3080 | tf_op jit(solution)/shard_map/cond/branch_1_fun/ppermute | solution.py:284
  10.2 5.5 %collective-permute-start = (f32[1,256]{1,0:T(1,128)S(1)}, f32[1,256]{1,0:T(1,128)S(1)}, u32[]{:S(2)}, u32[]{:S(2)}) collective-permute-start(f32[1,256]{1,0:T(1,128)S(1)} %param.1), channel_id=1, source_target_pairs={{1,3},{3,5},{5,7},{7,1},{9,11},{11,13},{13,15},{15,9},{17,19},{19,... | collective-permute-start | bytes 3080 | tf_op jit(solution)/shard_map/cond/branch_1_fun/ppermute | solution.py:284
  15.7 28.8 %copy-start.1 = (bf16[4,256,512]{2,1,0:T(8,128)(2,1)S(1)}, bf16[4,256,512]{2,1,0:T(8,128)(2,1)}, u32[]{:S(2)}) copy-start(bf16[4,256,512]{2,1,0:T(8,128)(2,1)} %constant.20.clone.fo_ref) | copy-start | bytes 3145732
  15.7 28.8 %copy-start.3 = (bf16[4,256,256]{2,1,0:T(8,128)(2,1)S(1)}, bf16[4,256,256]{2,1,0:T(8,128)(2,1)}, u32[]{:S(2)}) copy-start(bf16[4,256,256]{2,1,0:T(8,128)(2,1)} %constant.21.clone.io_ref) | copy-start | bytes 1572868
  15.7 28.7 %copy-start.4 = (bf16[256,256]{1,0:T(8,128)(2,1)S(1)}, bf16[256,256]{1,0:T(8,128)(2,1)}, u32[]{:S(2)}) copy-start(bf16[256,256]{1,0:T(8,128)(2,1)} %constant.23.clone.ii_ref) | copy-start | bytes 393220
  15.7 28.7 %copy-start.5 = (bf16[256,256]{1,0:T(8,128)(2,1)S(1)}, bf16[256,256]{1,0:T(8,128)(2,1)}, u32[]{:S(2)}) copy-start(bf16[256,256]{1,0:T(8,128)(2,1)} %constant.22.clone.fi_ref) | copy-start | bytes 393220
  15.7 28.7 %copy-start.6 = (f32[64,128]{1,0:T(8,128)S(1)}, f32[64,128]{1,0:T(8,128)}, u32[]{:S(2)}) copy-start(f32[64,128]{1,0:T(8,128)} %constant.25.clone.sin_ref) | copy-start | bytes 98308
  15.8 28.7 %copy-start.7 = (f32[64,128]{1,0:T(8,128)S(1)}, f32[64,128]{1,0:T(8,128)}, u32[]{:S(2)}) copy-start(f32[64,128]{1,0:T(8,128)} %constant.24.clone.cos_ref) | copy-start | bytes 98308
  47.5 17.6 %copy-start.2 = (bf16[256,1024]{1,0:T(8,128)(2,1)S(1)}, bf16[256,1024]{1,0:T(8,128)(2,1)}, u32[]{:S(2)}) copy-start(bf16[256,1024]{1,0:T(8,128)(2,1)} %gate_ref.1) | copy-start | bytes 1572868
  47.5 17.6 %copy-start.8 = (f32[1024]{0:T(1024)S(1)}, f32[1024]{0:T(1024)}, u32[]{:S(2)}) copy-start(f32[1024]{0:T(1024)} %param.15) | copy-start | bytes 12292
  65.6 2.5 %collective-permute-start.3 = (f32[3,256]{1,0:T(4,128)S(1)}, f32[3,256]{1,0:T(4,128)S(1)}, u32[]{:S(2)}, u32[]{:S(2)}) collective-permute-start(f32[3,256]{1,0:T(4,128)S(1)} %get-tuple-element.18), channel_id=1, source_target_pairs={{0,2},{2,0},{4,6},{6,4},{1,3},{3,1},{5,7},{7,5},{8,10},{10,8},{12,... | collective-permute-start | bytes 9224 | tf_op jit(solution)/shard_map/ppermute | solution.py:314
  68.2 3.8 %collective-permute-start.4 = (f32[3,256]{1,0:T(4,128)S(1)}, f32[3,256]{1,0:T(4,128)S(1)}, u32[]{:S(2)}, u32[]{:S(2)}) collective-permute-start(f32[3,256]{1,0:T(4,128)S(1)} %add.23), channel_id=1, source_target_pairs={{0,6},{2,4},{4,2},{6,0},{1,7},{3,5},{5,3},{7,1},{8,14},{10,12},{12... | collective-permute-start | bytes 9224 | tf_op jit(solution)/shard_map/ppermute | solution.py:314

commit v8 on v7

--- a/solution.py
+++ b/solution.py
@@ -21,7 +21,7 @@
 def two_parts(table):
     high = table.astype(ml_dtypes.bfloat16)
     low = (table - high.astype(np.float64)).astype(ml_dtypes.bfloat16)
-    return np.concatenate([high, low], axis=-1)
+    return np.concatenate([high, low], axis=-2)
 
 
 def mild_scale(table):
@@ -90,8 +90,9 @@
 
 
 def outer_dot(table, values):
-    values = values.astype(jnp.bfloat16)
-    return dot(table, jnp.concatenate([values, values], axis=0))
+    both = dot(table, values.astype(jnp.bfloat16))
+    half = both.shape[0] // 2
+    return both[:half] + both[half:]
 
 
 def tile_copies(hbm_ref, buf_ref, sem_ref):

time: 72.8 us -> 72.6 us (level)
  no operation moved by 1% of the time
where the time goes in v8:
time: 72.6 us; the launch traced here: 72.3 us
  blocking collectives  46.3 us (64%)
  starting transfers between devices  14.4 us (20%)
  Pallas kernels  4.5 us (6%)
  waiting for transfers between devices  4.32 us (6%)
  other arithmetic  1.95 us (3%)
  between operations  0.77 us (1%)
    all_to_all x1, blocking collectives, local(): lax.all_to_all(packed, 'ctx', split_axis=0, concat_axis=0, tiled=True)  28.7 us
    all_to_all x1, blocking collectives, local(): lax.all_to_all(conv, 'ctx', split_axis=0, concat_axis=0, tiled=True)  17.6 us
    ppermute x3, starting transfers between devices, total_first(): lax.ppermute(part, ('chan', 'section'), [(i * sections + last, (i + hop)...  10.3 us
    ppermute x2, starting transfers between devices, local(): lax.ppermute(sums, 'chan', [(i, i ^ reach - 1) for i in range(chans)])  4.11 us
    ppermute x3, waiting for transfers between devices, total_first(): lax.ppermute(part, ('chan', 'section'), [(i * sections + last, (i + hop)...  2.91 us
    pallas_call x1, Pallas kernels, local(): call(conv_kernel, jax.ShapeDtypeStruct((count,) + packed_tail, bf16))  2.78 us
  transfers between devices with their start and end apart: 5, of which 4 were waited for; matrix products, arithmetic and copies ran while one was open for 0% of the time, Pallas kernels for 1%

profile of v8, /device:TPU:1, one launch (start us, length us, event | category | flops | bytes accessed | tf_op | source)
XLA Modules:
  0.0 72.3 jit_solution(2834462481233566534)
XLA Ops:
  0.6 0.0 copy-start
  0.6 1.4 %convert_element_type.6.fil_ref = bf16[256,1024]{1,0:T(8,128)(2,1)S(1)} convert(f32[256,1024]{1,0:T(8,128)} %param.14) | non-fusion elementwise | flops 262144 | bytes 1572864 | tf_op jit(solution)/shard_map/convert_element_type | solution.py:278
  2.0 0.0 copy-done
  2.0 0.4 shard_map.113
  2.4 13.3 %conditional.1 = (f32[1,256]{1,0:T(1,128)S(1)}) conditional(s32[]{:T(128)} %convert_element_type.7, f32[1,256]{1,0:T(1,128)S(1)} %get-tuple-element.14, f32[1,256]{1,0:T(1,128)S(1)} %get-tuple-element.14), branch_computations={%region_0.0_spmd, %region_1.0_spmd} | conditional | flops 768 | bytes 17536 | solution.py:293
  2.4 5.5 %collective-permute-start.2 = (f32[1,256]{1,0:T(1,128)S(1)}, f32[1,256]{1,0:T(1,128)S(1)}, u32[]{:S(2)}, u32[]{:S(2)}) collective-permute-start(f32[1,256]{1,0:T(1,128)S(1)} %param.1), channel_id=1, source_target_pairs={{1,7},{3,1},{5,3},{7,5},{9,15},{11,9},{13,11},{15,13},{17,23},{19,... | collective-permute-start | bytes 3080 | tf_op jit(solution)/shard_map/cond/branch_1_fun/ppermute | solution.py:285
  7.9 2.3 %collective-permute-start.1 = (f32[1,256]{1,0:T(1,128)S(1)}, f32[1,256]{1,0:T(1,128)S(1)}, u32[]{:S(2)}, u32[]{:S(2)}) collective-permute-start(f32[1,256]{1,0:T(1,128)S(1)} %param.1), channel_id=1, source_target_pairs={{1,5},{3,7},{5,1},{7,3},{9,13},{11,15},{13,9},{15,11},{17,21},{19,... | collective-permute-start | bytes 3080 | tf_op jit(solution)/shard_map/cond/branch_1_fun/ppermute | solution.py:285
  10.2 2.6 %collective-permute-start = (f32[1,256]{1,0:T(1,128)S(1)}, f32[1,256]{1,0:T(1,128)S(1)}, u32[]{:S(2)}, u32[]{:S(2)}) collective-permute-start(f32[1,256]{1,0:T(1,128)S(1)} %param.1), channel_id=1, source_target_pairs={{1,3},{3,5},{5,7},{7,1},{9,11},{11,13},{13,15},{15,9},{17,19},{19,... | collective-permute-start | bytes 3080 | tf_op jit(solution)/shard_map/cond/branch_1_fun/ppermute | solution.py:285
  12.8 0.0 collective-permute-done.2
  12.8 0.9 %collective-permute-done.1 = f32[1,256]{1,0:T(1,128)S(1)} collective-permute-done((f32[1,256]{1,0:T(1,128)S(1)}, f32[1,256]{1,0:T(1,128)S(1)}, u32[]{:S(2)}, u32[]{:S(2)}) %collective-permute-start.1) | collective-permute-done | bytes 1056 | tf_op jit(solution)/shard_map/cond/branch_1_fun/ppermute | solution.py:285
  13.7 2.0 %collective-permute-done = f32[1,256]{1,0:T(1,128)S(1)} collective-permute-done((f32[1,256]{1,0:T(1,128)S(1)}, f32[1,256]{1,0:T(1,128)S(1)}, u32[]{:S(2)}, u32[]{:S(2)}) %collective-permute-start) | collective-permute-done | bytes 1056 | tf_op jit(solution)/shard_map/cond/branch_1_fun/ppermute | solution.py:285
  15.7 0.0 copy-start.1
  15.7 0.0 copy-start.3
  15.7 0.0 copy-start.4
  15.7 0.0 copy-start.5
  15.7 0.0 copy-start.6
  15.8 0.0 copy-start.7
  15.8 28.7 %all_to_all.10.in_ref = bf16[32,2,4,16,128]{4,3,2,1,0:T(8,128)(2,1)S(1)} all-to-all(bf16[32,2,4,16,128]{4,3,2,1,0:T(8,128)(2,1)S(1)} %get-tuple-element.15), channel_id=1, replica_groups=mesh['ctx'=32,'chan'=4,'section'=2] {'ctx'}, dimensions={0} | all-to-all | bytes 2097152 | tf_op jit(solution)/shard_map/all_to_all | solution.py:295
  44.5 0.0 copy-done.1
  44.5 0.0 copy-done.3
  44.5 0.0 copy-done.4
  44.5 0.0 copy-done.5
  44.5 0.0 copy-done.6
  44.5 0.0 copy-done.7
  44.5 2.8 %shard_map.114 = bf16[32,4,16,128]{3,2,1,0:T(8,128)(2,1)S(1)} custom-call(bf16[32,2,4,16,128]{4,3,2,1,0:T(8,128)(2,1)S(1)} %all_to_all.10.in_ref, bf16[4,512,256]{2,1,0:T(8,128)(2,1)S(1)} %copy-done.1, bf16[4,256,256]{2,1,0:T(8,128)(2,1)S(1)} %copy-done.3, bf16[256,256]{1,0:T(8,128)(2,1)S(1)} %copy-done.5, bf16[256,256]{1,0:T(8,128)(2,1)S(1)} %copy-done.4, ...), custom_call_target="tpu_custom_call" | custom-call | tf_op jit(solution)/shard_map/pallas_call | solution.py:296
  47.3 0.0 copy-start.2
  47.3 0.0 copy-start.8
  47.3 17.6 %all_to_all.11.conv_ref = bf16[32,4,16,128]{3,2,1,0:T(8,128)(2,1)S(1)} all-to-all(bf16[32,4,16,128]{3,2,1,0:T(8,128)(2,1)S(1)} %shard_map.114), channel_id=1, replica_groups=mesh['ctx'=32,'chan'=4,'section'=2] {'ctx'}, dimensions={0} | all-to-all | bytes 1048576 | tf_op jit(solution)/shard_map/all_to_all | solution.py:299
  64.9 0.0 copy-done.2
  64.9 0.0 copy-done.8
  64.9 0.5 shard_map.115
  65.4 1.3 %collective-permute-start.3 = (f32[3,256]{1,0:T(4,128)S(1)}, f32[3,256]{1,0:T(4,128)S(1)}, u32[]{:S(2)}, u32[]{:S(2)}) collective-permute-start(f32[3,256]{1,0:T(4,128)S(1)} %get-tuple-element.18), channel_id=1, source_target_pairs={{0,2},{2,0},{4,6},{6,4},{1,3},{3,1},{5,7},{7,5},{8,10},{10,8},{12,... | collective-permute-start | bytes 9224 | tf_op jit(solution)/shard_map/ppermute | solution.py:315
  66.7 1.2 %collective-permute-done.3 = f32[3,256]{1,0:T(4,128)S(1)} collective-permute-done((f32[3,256]{1,0:T(4,128)S(1)}, f32[3,256]{1,0:T(4,128)S(1)}, u32[]{:S(2)}, u32[]{:S(2)}) %collective-permute-start.3) | collective-permute-done | bytes 3104 | tf_op jit(solution)/shard_map/ppermute | solution.py:315
  67.9 2.8 %collective-permute-start.4 = (f32[3,256]{1,0:T(4,128)S(1)}, f32[3,256]{1,0:T(4,128)S(1)}, u32[]{:S(2)}, u32[]{:S(2)}) collective-permute-start(f32[3,256]{1,0:T(4,128)S(1)} %add.23), channel_id=1, source_target_pairs={{0,6},{2,4},{4,2},{6,0},{1,7},{3,5},{5,3},{7,1},{8,14},{10,12},{12... | collective-permute-start | bytes 9224 | tf_op jit(solution)/shard_map/ppermute | solution.py:315
  70.7 0.8 %shard_map.116 = bf16[256,1024]{1,0:T(8,128)(2,1)} custom-call(bf16[256,1024]{1,0:T(8,128)(2,1)S(1)} %get-tuple-element.17.in_ref), custom_call_target="tpu_custom_call" | custom-call | tf_op jit(solution)/shard_map/pallas_call | solution.py:306
  71.6 0.2 collective-permute-done.4
  71.7 0.6 slice_multiply_fusion
  (3 shorter events, 0.0 us)
Async XLA Ops:
  0.6 1.4 %copy-start = (bf16[256,1024]{1,0:T(8,128)(2,1)S(1)}, bf16[256,1024]{1,0:T(8,128)(2,1)}, u32[]{:S(2)}) copy-start(bf16[256,1024]{1,0:T(8,128)(2,1)} %sig_ref.3) | copy-start | bytes 1572868
  2.4 10.4 %collective-permute-start.2 = (f32[1,256]{1,0:T(1,128)S(1)}, f32[1,256]{1,0:T(1,128)S(1)}, u32[]{:S(2)}, u32[]{:S(2)}) collective-permute-start(f32[1,256]{1,0:T(1,128)S(1)} %param.1), channel_id=1, source_target_pairs={{1,7},{3,1},{5,3},{7,5},{9,15},{11,9},{13,11},{15,13},{17,23},{19,... | collective-permute-start | bytes 3080 | tf_op jit(solution)/shard_map/cond/branch_1_fun/ppermute | solution.py:285
  7.9 5.8 %collective-permute-start.1 = (f32[1,256]{1,0:T(1,128)S(1)}, f32[1,256]{1,0:T(1,128)S(1)}, u32[]{:S(2)}, u32[]{:S(2)}) collective-permute-start(f32[1,256]{1,0:T(1,128)S(1)} %param.1), channel_id=1, source_target_pairs={{1,5},{3,7},{5,1},{7,3},{9,13},{11,15},{13,9},{15,11},{17,21},{19,... | collective-permute-start | bytes 3080 | tf_op jit(solution)/shard_map/cond/branch_1_fun/ppermute | solution.py:285
  10.2 5.5 %collective-permute-start = (f32[1,256]{1,0:T(1,128)S(1)}, f32[1,256]{1,0:T(1,128)S(1)}, u32[]{:S(2)}, u32[]{:S(2)}) collective-permute-start(f32[1,256]{1,0:T(1,128)S(1)} %param.1), channel_id=1, source_target_pairs={{1,3},{3,5},{5,7},{7,1},{9,11},{11,13},{13,15},{15,9},{17,19},{19,... | collective-permute-start | bytes 3080 | tf_op jit(solution)/shard_map/cond/branch_1_fun/ppermute | solution.py:285
  15.7 28.8 %copy-start.1 = (bf16[4,512,256]{2,1,0:T(8,128)(2,1)S(1)}, bf16[4,512,256]{2,1,0:T(8,128)(2,1)}, u32[]{:S(2)}) copy-start(bf16[4,512,256]{2,1,0:T(8,128)(2,1)} %constant.20.clone.fo_ref) | copy-start | bytes 3145732
  15.7 28.8 %copy-start.3 = (bf16[4,256,256]{2,1,0:T(8,128)(2,1)S(1)}, bf16[4,256,256]{2,1,0:T(8,128)(2,1)}, u32[]{:S(2)}) copy-start(bf16[4,256,256]{2,1,0:T(8,128)(2,1)} %constant.21.clone.io_ref) | copy-start | bytes 1572868
  15.7 28.7 %copy-start.4 = (bf16[256,256]{1,0:T(8,128)(2,1)S(1)}, bf16[256,256]{1,0:T(8,128)(2,1)}, u32[]{:S(2)}) copy-start(bf16[256,256]{1,0:T(8,128)(2,1)} %constant.23.clone.ii_ref) | copy-start | bytes 393220
  15.7 28.7 %copy-start.5 = (bf16[256,256]{1,0:T(8,128)(2,1)S(1)}, bf16[256,256]{1,0:T(8,128)(2,1)}, u32[]{:S(2)}) copy-start(bf16[256,256]{1,0:T(8,128)(2,1)} %constant.22.clone.fi_ref) | copy-start | bytes 393220
  15.7 28.7 %copy-start.6 = (f32[64,128]{1,0:T(8,128)S(1)}, f32[64,128]{1,0:T(8,128)}, u32[]{:S(2)}) copy-start(f32[64,128]{1,0:T(8,128)} %constant.25.clone.sin_ref) | copy-start | bytes 98308
  15.8 28.7 %copy-start.7 = (f32[64,128]{1,0:T(8,128)S(1)}, f32[64,128]{1,0:T(8,128)}, u32[]{:S(2)}) copy-start(f32[64,128]{1,0:T(8,128)} %constant.24.clone.cos_ref) | copy-start | bytes 98308
  47.3 17.6 %copy-start.2 = (bf16[256,1024]{1,0:T(8,128)(2,1)S(1)}, bf16[256,1024]{1,0:T(8,128)(2,1)}, u32[]{:S(2)}) copy-start(bf16[256,1024]{1,0:T(8,128)(2,1)} %gate_ref.1) | copy-start | bytes 1572868
  47.3 17.6 %copy-start.8 = (f32[1024]{0:T(1024)S(1)}, f32[1024]{0:T(1024)}, u32[]{:S(2)}) copy-start(f32[1024]{0:T(1024)} %param.15) | copy-start | bytes 12292
  65.4 2.5 %collective-permute-start.3 = (f32[3,256]{1,0:T(4,128)S(1)}, f32[3,256]{1,0:T(4,128)S(1)}, u32[]{:S(2)}, u32[]{:S(2)}) collective-permute-start(f32[3,256]{1,0:T(4,128)S(1)} %get-tuple-element.18), channel_id=1, source_target_pairs={{0,2},{2,0},{4,6},{6,4},{1,3},{3,1},{5,7},{7,5},{8,10},{10,8},{12,... | collective-permute-start | bytes 9224 | tf_op jit(solution)/shard_map/ppermute | solution.py:315
  67.9 3.8 %collective-permute-start.4 = (f32[3,256]{1,0:T(4,128)S(1)}, f32[3,256]{1,0:T(4,128)S(1)}, u32[]{:S(2)}, u32[]{:S(2)}) collective-permute-start(f32[3,256]{1,0:T(4,128)S(1)} %add.23), channel_id=1, source_target_pairs={{0,6},{2,4},{4,2},{6,0},{1,7},{3,5},{5,3},{7,1},{8,14},{10,12},{12... | collective-permute-start | bytes 9224 | tf_op jit(solution)/shard_map/ppermute | solution.py:315

commit v9 on v8

--- a/solution.py
+++ b/solution.py
@@ -310,10 +310,10 @@
         out_specs=hbm,
         scratch_shapes=[tile_sems],
     )(mixed)
-    reach = 2
-    while reach <= chans:
+    reach = chans
+    while reach > 1:
         sums = sums + lax.ppermute(sums, "chan", [(i, i ^ (reach - 1)) for i in range(chans)])
-        reach *= 2
+        reach //= 2
     inner_total, out_total, sig_total = sums
     sig_total = jnp.where(is_last, sig_sq[0], sig_total)
     cosine = inner_total / jnp.sqrt((sig_total + EPSILON) * (out_total + EPSILON))

time: 72.6 us -> 72.5 us (level)
  starting transfers between devices: 14.4 us -> 13.1 us
  waiting for transfers between devices: 4.32 us -> 5.55 us
    ppermute x2, starting transfers between devices: 4.11 us -> 2.74 us  [local(): lax.ppermute(sums, 'chan', [(i, i ^ reach - 1) for i in range(chans)])]
    ppermute x2, waiting for transfers between devices: 1.41 us -> 2.64 us  [local(): lax.ppermute(sums, 'chan', [(i, i ^ reach - 1) for i in range(chans)])]
where the time goes in v9:
time: 72.5 us; the launch traced here: 72.2 us
  blocking collectives  46.3 us (64%)
  starting transfers between devices  13.1 us (18%)
  waiting for transfers between devices  5.55 us (8%)
  Pallas kernels  4.5 us (6%)
  other arithmetic  1.95 us (3%)
  between operations  0.77 us (1%)
    all_to_all x1, blocking collectives, local(): lax.all_to_all(packed, 'ctx', split_axis=0, concat_axis=0, tiled=True)  28.7 us
    all_to_all x1, blocking collectives, local(): lax.all_to_all(conv, 'ctx', split_axis=0, concat_axis=0, tiled=True)  17.6 us
    ppermute x3, starting transfers between devices, total_first(): lax.ppermute(part, ('chan', 'section'), [(i * sections + last, (i + hop)...  10.3 us
    ppermute x3, waiting for transfers between devices, total_first(): lax.ppermute(part, ('chan', 'section'), [(i * sections + last, (i + hop)...  2.91 us
    pallas_call x1, Pallas kernels, local(): call(conv_kernel, jax.ShapeDtypeStruct((count,) + packed_tail, bf16))  2.78 us
    ppermute x2, starting transfers between devices, local(): lax.ppermute(sums, 'chan', [(i, i ^ reach - 1) for i in range(chans)])  2.74 us
    ppermute x2, waiting for transfers between devices, local(): lax.ppermute(sums, 'chan', [(i, i ^ reach - 1) for i in range(chans)])  2.64 us
  transfers between devices with their start and end apart: 5, of which 4 were waited for; matrix products, arithmetic and copies ran while one was open for 0% of the time, Pallas kernels for 1%

profile of v9, /device:TPU:1, one launch (start us, length us, event | category | flops | bytes accessed | tf_op | source)
XLA Modules:
  0.0 72.2 jit_solution(17323606812101132323)
XLA Ops:
  0.6 0.0 copy-start
  0.6 1.4 %convert_element_type.6.fil_ref = bf16[256,1024]{1,0:T(8,128)(2,1)S(1)} convert(f32[256,1024]{1,0:T(8,128)} %param.14) | non-fusion elementwise | flops 262144 | bytes 1572864 | tf_op jit(solution)/shard_map/convert_element_type | solution.py:278
  2.0 0.0 copy-done
  2.0 0.4 shard_map.113
  2.4 13.3 %conditional.1 = (f32[1,256]{1,0:T(1,128)S(1)}) conditional(s32[]{:T(128)} %convert_element_type.7, f32[1,256]{1,0:T(1,128)S(1)} %get-tuple-element.14, f32[1,256]{1,0:T(1,128)S(1)} %get-tuple-element.14), branch_computations={%region_0.0_spmd, %region_1.0_spmd} | conditional | flops 768 | bytes 17536 | solution.py:293
  2.4 5.5 %collective-permute-start.2 = (f32[1,256]{1,0:T(1,128)S(1)}, f32[1,256]{1,0:T(1,128)S(1)}, u32[]{:S(2)}, u32[]{:S(2)}) collective-permute-start(f32[1,256]{1,0:T(1,128)S(1)} %param.1), channel_id=1, source_target_pairs={{1,7},{3,1},{5,3},{7,5},{9,15},{11,9},{13,11},{15,13},{17,23},{19,... | collective-permute-start | bytes 3080 | tf_op jit(solution)/shard_map/cond/branch_1_fun/ppermute | solution.py:285
  7.9 2.3 %collective-permute-start.1 = (f32[1,256]{1,0:T(1,128)S(1)}, f32[1,256]{1,0:T(1,128)S(1)}, u32[]{:S(2)}, u32[]{:S(2)}) collective-permute-start(f32[1,256]{1,0:T(1,128)S(1)} %param.1), channel_id=1, source_target_pairs={{1,5},{3,7},{5,1},{7,3},{9,13},{11,15},{13,9},{15,11},{17,21},{19,... | collective-permute-start | bytes 3080 | tf_op jit(solution)/shard_map/cond/branch_1_fun/ppermute | solution.py:285
  10.2 2.6 %collective-permute-start = (f32[1,256]{1,0:T(1,128)S(1)}, f32[1,256]{1,0:T(1,128)S(1)}, u32[]{:S(2)}, u32[]{:S(2)}) collective-permute-start(f32[1,256]{1,0:T(1,128)S(1)} %param.1), channel_id=1, source_target_pairs={{1,3},{3,5},{5,7},{7,1},{9,11},{11,13},{13,15},{15,9},{17,19},{19,... | collective-permute-start | bytes 3080 | tf_op jit(solution)/shard_map/cond/branch_1_fun/ppermute | solution.py:285
  12.8 0.0 collective-permute-done.2
  12.8 0.9 %collective-permute-done.1 = f32[1,256]{1,0:T(1,128)S(1)} collective-permute-done((f32[1,256]{1,0:T(1,128)S(1)}, f32[1,256]{1,0:T(1,128)S(1)}, u32[]{:S(2)}, u32[]{:S(2)}) %collective-permute-start.1) | collective-permute-done | bytes 1056 | tf_op jit(solution)/shard_map/cond/branch_1_fun/ppermute | solution.py:285
  13.7 2.0 %collective-permute-done = f32[1,256]{1,0:T(1,128)S(1)} collective-permute-done((f32[1,256]{1,0:T(1,128)S(1)}, f32[1,256]{1,0:T(1,128)S(1)}, u32[]{:S(2)}, u32[]{:S(2)}) %collective-permute-start) | collective-permute-done | bytes 1056 | tf_op jit(solution)/shard_map/cond/branch_1_fun/ppermute | solution.py:285
  15.7 0.0 copy-start.1
  15.7 0.0 copy-start.3
  15.7 0.0 copy-start.4
  15.7 0.0 copy-start.5
  15.7 0.0 copy-start.6
  15.8 0.0 copy-start.7
  15.8 28.7 %all_to_all.10.in_ref = bf16[32,2,4,16,128]{4,3,2,1,0:T(8,128)(2,1)S(1)} all-to-all(bf16[32,2,4,16,128]{4,3,2,1,0:T(8,128)(2,1)S(1)} %get-tuple-element.15), channel_id=1, replica_groups=mesh['ctx'=32,'chan'=4,'section'=2] {'ctx'}, dimensions={0} | all-to-all | bytes 2097152 | tf_op jit(solution)/shard_map/all_to_all | solution.py:295
  44.5 0.0 copy-done.1
  44.5 0.0 copy-done.3
  44.5 0.0 copy-done.4
  44.5 0.0 copy-done.5
  44.5 0.0 copy-done.6
  44.5 0.0 copy-done.7
  44.5 2.8 %shard_map.114 = bf16[32,4,16,128]{3,2,1,0:T(8,128)(2,1)S(1)} custom-call(bf16[32,2,4,16,128]{4,3,2,1,0:T(8,128)(2,1)S(1)} %all_to_all.10.in_ref, bf16[4,512,256]{2,1,0:T(8,128)(2,1)S(1)} %copy-done.1, bf16[4,256,256]{2,1,0:T(8,128)(2,1)S(1)} %copy-done.3, bf16[256,256]{1,0:T(8,128)(2,1)S(1)} %copy-done.5, bf16[256,256]{1,0:T(8,128)(2,1)S(1)} %copy-done.4, ...), custom_call_target="tpu_custom_call" | custom-call | tf_op jit(solution)/shard_map/pallas_call | solution.py:296
  47.3 0.0 copy-start.2
  47.3 0.0 copy-start.8
  47.3 17.6 %all_to_all.11.conv_ref = bf16[32,4,16,128]{3,2,1,0:T(8,128)(2,1)S(1)} all-to-all(bf16[32,4,16,128]{3,2,1,0:T(8,128)(2,1)S(1)} %shard_map.114), channel_id=1, replica_groups=mesh['ctx'=32,'chan'=4,'section'=2] {'ctx'}, dimensions={0} | all-to-all | bytes 1048576 | tf_op jit(solution)/shard_map/all_to_all | solution.py:299
  64.9 0.0 copy-done.2
  64.9 0.0 copy-done.8
  64.9 0.5 shard_map.115
  65.4 2.7 %collective-permute-start.3 = (f32[3,256]{1,0:T(4,128)S(1)}, f32[3,256]{1,0:T(4,128)S(1)}, u32[]{:S(2)}, u32[]{:S(2)}) collective-permute-start(f32[3,256]{1,0:T(4,128)S(1)} %get-tuple-element.18), channel_id=1, source_target_pairs={{0,6},{2,4},{4,2},{6,0},{1,7},{3,5},{5,3},{7,1},{8,14},{10,12},{12... | collective-permute-start | bytes 9224 | tf_op jit(solution)/shard_map/ppermute | solution.py:315
  68.1 1.0 %collective-permute-done.3 = f32[3,256]{1,0:T(4,128)S(1)} collective-permute-done((f32[3,256]{1,0:T(4,128)S(1)}, f32[3,256]{1,0:T(4,128)S(1)}, u32[]{:S(2)}, u32[]{:S(2)}) %collective-permute-start.3) | collective-permute-done | bytes 3104 | tf_op jit(solution)/shard_map/ppermute | solution.py:315
  69.2 0.0 collective-permute-start.4
  69.2 0.8 %shard_map.116 = bf16[256,1024]{1,0:T(8,128)(2,1)} custom-call(bf16[256,1024]{1,0:T(8,128)(2,1)S(1)} %get-tuple-element.17.in_ref), custom_call_target="tpu_custom_call" | custom-call | tf_op jit(solution)/shard_map/pallas_call | solution.py:306
  70.0 1.6 %collective-permute-done.4 = f32[3,256]{1,0:T(4,128)S(1)} collective-permute-done((f32[3,256]{1,0:T(4,128)S(1)}, f32[3,256]{1,0:T(4,128)S(1)}, u32[]{:S(2)}, u32[]{:S(2)}) %collective-permute-start.4) | collective-permute-done | bytes 3104 | tf_op jit(solution)/shard_map/ppermute | solution.py:315
  71.6 0.6 slice_multiply_fusion
  (3 shorter events, 0.0 us)
Async XLA Ops:
  0.6 1.4 %copy-start = (bf16[256,1024]{1,0:T(8,128)(2,1)S(1)}, bf16[256,1024]{1,0:T(8,128)(2,1)}, u32[]{:S(2)}) copy-start(bf16[256,1024]{1,0:T(8,128)(2,1)} %sig_ref.3) | copy-start | bytes 1572868
  2.4 10.4 %collective-permute-start.2 = (f32[1,256]{1,0:T(1,128)S(1)}, f32[1,256]{1,0:T(1,128)S(1)}, u32[]{:S(2)}, u32[]{:S(2)}) collective-permute-start(f32[1,256]{1,0:T(1,128)S(1)} %param.1), channel_id=1, source_target_pairs={{1,7},{3,1},{5,3},{7,5},{9,15},{11,9},{13,11},{15,13},{17,23},{19,... | collective-permute-start | bytes 3080 | tf_op jit(solution)/shard_map/cond/branch_1_fun/ppermute | solution.py:285
  7.9 5.8 %collective-permute-start.1 = (f32[1,256]{1,0:T(1,128)S(1)}, f32[1,256]{1,0:T(1,128)S(1)}, u32[]{:S(2)}, u32[]{:S(2)}) collective-permute-start(f32[1,256]{1,0:T(1,128)S(1)} %param.1), channel_id=1, source_target_pairs={{1,5},{3,7},{5,1},{7,3},{9,13},{11,15},{13,9},{15,11},{17,21},{19,... | collective-permute-start | bytes 3080 | tf_op jit(solution)/shard_map/cond/branch_1_fun/ppermute | solution.py:285
  10.2 5.5 %collective-permute-start = (f32[1,256]{1,0:T(1,128)S(1)}, f32[1,256]{1,0:T(1,128)S(1)}, u32[]{:S(2)}, u32[]{:S(2)}) collective-permute-start(f32[1,256]{1,0:T(1,128)S(1)} %param.1), channel_id=1, source_target_pairs={{1,3},{3,5},{5,7},{7,1},{9,11},{11,13},{13,15},{15,9},{17,19},{19,... | collective-permute-start | bytes 3080 | tf_op jit(solution)/shard_map/cond/branch_1_fun/ppermute | solution.py:285
  15.7 28.8 %copy-start.1 = (bf16[4,512,256]{2,1,0:T(8,128)(2,1)S(1)}, bf16[4,512,256]{2,1,0:T(8,128)(2,1)}, u32[]{:S(2)}) copy-start(bf16[4,512,256]{2,1,0:T(8,128)(2,1)} %constant.20.clone.fo_ref) | copy-start | bytes 3145732
  15.7 28.8 %copy-start.3 = (bf16[4,256,256]{2,1,0:T(8,128)(2,1)S(1)}, bf16[4,256,256]{2,1,0:T(8,128)(2,1)}, u32[]{:S(2)}) copy-start(bf16[4,256,256]{2,1,0:T(8,128)(2,1)} %constant.21.clone.io_ref) | copy-start | bytes 1572868
  15.7 28.7 %copy-start.4 = (bf16[256,256]{1,0:T(8,128)(2,1)S(1)}, bf16[256,256]{1,0:T(8,128)(2,1)}, u32[]{:S(2)}) copy-start(bf16[256,256]{1,0:T(8,128)(2,1)} %constant.23.clone.ii_ref) | copy-start | bytes 393220
  15.7 28.7 %copy-start.5 = (bf16[256,256]{1,0:T(8,128)(2,1)S(1)}, bf16[256,256]{1,0:T(8,128)(2,1)}, u32[]{:S(2)}) copy-start(bf16[256,256]{1,0:T(8,128)(2,1)} %constant.22.clone.fi_ref) | copy-start | bytes 393220
  15.7 28.7 %copy-start.6 = (f32[64,128]{1,0:T(8,128)S(1)}, f32[64,128]{1,0:T(8,128)}, u32[]{:S(2)}) copy-start(f32[64,128]{1,0:T(8,128)} %constant.25.clone.sin_ref) | copy-start | bytes 98308
  15.8 28.7 %copy-start.7 = (f32[64,128]{1,0:T(8,128)S(1)}, f32[64,128]{1,0:T(8,128)}, u32[]{:S(2)}) copy-start(f32[64,128]{1,0:T(8,128)} %constant.24.clone.cos_ref) | copy-start | bytes 98308
  47.3 17.6 %copy-start.2 = (bf16[256,1024]{1,0:T(8,128)(2,1)S(1)}, bf16[256,1024]{1,0:T(8,128)(2,1)}, u32[]{:S(2)}) copy-start(bf16[256,1024]{1,0:T(8,128)(2,1)} %gate_ref.1) | copy-start | bytes 1572868
  47.3 17.6 %copy-start.8 = (f32[1024]{0:T(1024)S(1)}, f32[1024]{0:T(1024)}, u32[]{:S(2)}) copy-start(f32[1024]{0:T(1024)} %param.15) | copy-start | bytes 12292
  65.4 3.8 %collective-permute-start.3 = (f32[3,256]{1,0:T(4,128)S(1)}, f32[3,256]{1,0:T(4,128)S(1)}, u32[]{:S(2)}, u32[]{:S(2)}) collective-permute-start(f32[3,256]{1,0:T(4,128)S(1)} %get-tuple-element.18), channel_id=1, source_target_pairs={{0,6},{2,4},{4,2},{6,0},{1,7},{3,5},{5,3},{7,1},{8,14},{10,12},{12... | collective-permute-start | bytes 9224 | tf_op jit(solution)/shard_map/ppermute | solution.py:315
  69.2 2.5 %collective-permute-start.4 = (f32[3,256]{1,0:T(4,128)S(1)}, f32[3,256]{1,0:T(4,128)S(1)}, u32[]{:S(2)}, u32[]{:S(2)}) collective-permute-start(f32[3,256]{1,0:T(4,128)S(1)} %add.23), channel_id=1, source_target_pairs={{0,2},{2,0},{4,6},{6,4},{1,3},{3,1},{5,7},{7,5},{8,10},{10,8},{12,... | collective-permute-start | bytes 9224 | tf_op jit(solution)/shard_map/ppermute | solution.py:315

commit v10 on v8

--- a/solution.py
+++ b/solution.py
@@ -241,7 +241,13 @@
 
 
 def deliver_kernel(in_ref, out_ref, sem_ref):
-    copies = tile_copies(in_ref, out_ref, sem_ref)
+    span = in_ref.shape[0] // TILES
+    copies = [
+        pltpu.make_async_copy(
+            in_ref.at[pl.ds(tile * span, span)], out_ref.at[pl.ds(tile * span, span)], sem_ref.at[tile]
+        )
+        for tile in range(TILES)
+    ]
     for copy in copies:
         copy.start()
     for copy in copies:

time: 72.6 us -> 72.6 us (level)
  no operation moved by 1% of the time
where the time goes in v10:
time: 72.6 us; the launch traced here: 72.3 us
  blocking collectives  46.3 us (64%)
  starting transfers between devices  14.4 us (20%)
  Pallas kernels  4.5 us (6%)
  waiting for transfers between devices  4.32 us (6%)
  other arithmetic  1.95 us (3%)
  between operations  0.77 us (1%)
    all_to_all x1, blocking collectives, local(): lax.all_to_all(packed, 'ctx', split_axis=0, concat_axis=0, tiled=True)  28.7 us
    all_to_all x1, blocking collectives, local(): lax.all_to_all(conv, 'ctx', split_axis=0, concat_axis=0, tiled=True)  17.6 us
    ppermute x3, starting transfers between devices, total_first(): lax.ppermute(part, ('chan', 'section'), [(i * sections + last, (i + hop)...  10.3 us
    ppermute x2, starting transfers between devices, local(): lax.ppermute(sums, 'chan', [(i, i ^ reach - 1) for i in range(chans)])  4.11 us
    ppermute x3, waiting for transfers between devices, total_first(): lax.ppermute(part, ('chan', 'section'), [(i * sections + last, (i + hop)...  2.91 us
    pallas_call x1, Pallas kernels, local(): call(conv_kernel, jax.ShapeDtypeStruct((count,) + packed_tail, bf16))  2.78 us
  transfers between devices with their start and end apart: 5, of which 4 were waited for; matrix products, arithmetic and copies ran while one was open for 0% of the time, Pallas kernels for 1%

profile of v10, /device:TPU:1, one launch (start us, length us, event | category | flops | bytes accessed | tf_op | source)
XLA Modules:
  0.0 72.3 jit_solution(9173155122237738466)
XLA Ops:
  0.6 0.0 copy-start
  0.6 1.4 %convert_element_type.6.fil_ref = bf16[256,1024]{1,0:T(8,128)(2,1)S(1)} convert(f32[256,1024]{1,0:T(8,128)} %param.14) | non-fusion elementwise | flops 262144 | bytes 1572864 | tf_op jit(solution)/shard_map/convert_element_type | solution.py:284
  2.0 0.0 copy-done
  2.0 0.4 shard_map.113
  2.4 13.3 %conditional.1 = (f32[1,256]{1,0:T(1,128)S(1)}) conditional(s32[]{:T(128)} %convert_element_type.7, f32[1,256]{1,0:T(1,128)S(1)} %get-tuple-element.14, f32[1,256]{1,0:T(1,128)S(1)} %get-tuple-element.14), branch_computations={%region_0.0_spmd, %region_1.0_spmd} | conditional | flops 768 | bytes 17536 | solution.py:299
  2.4 5.5 %collective-permute-start.2 = (f32[1,256]{1,0:T(1,128)S(1)}, f32[1,256]{1,0:T(1,128)S(1)}, u32[]{:S(2)}, u32[]{:S(2)}) collective-permute-start(f32[1,256]{1,0:T(1,128)S(1)} %param.1), channel_id=1, source_target_pairs={{1,7},{3,1},{5,3},{7,5},{9,15},{11,9},{13,11},{15,13},{17,23},{19,... | collective-permute-start | bytes 3080 | tf_op jit(solution)/shard_map/cond/branch_1_fun/ppermute | solution.py:291
  7.9 2.3 %collective-permute-start.1 = (f32[1,256]{1,0:T(1,128)S(1)}, f32[1,256]{1,0:T(1,128)S(1)}, u32[]{:S(2)}, u32[]{:S(2)}) collective-permute-start(f32[1,256]{1,0:T(1,128)S(1)} %param.1), channel_id=1, source_target_pairs={{1,5},{3,7},{5,1},{7,3},{9,13},{11,15},{13,9},{15,11},{17,21},{19,... | collective-permute-start | bytes 3080 | tf_op jit(solution)/shard_map/cond/branch_1_fun/ppermute | solution.py:291
  10.2 2.6 %collective-permute-start = (f32[1,256]{1,0:T(1,128)S(1)}, f32[1,256]{1,0:T(1,128)S(1)}, u32[]{:S(2)}, u32[]{:S(2)}) collective-permute-start(f32[1,256]{1,0:T(1,128)S(1)} %param.1), channel_id=1, source_target_pairs={{1,3},{3,5},{5,7},{7,1},{9,11},{11,13},{13,15},{15,9},{17,19},{19,... | collective-permute-start | bytes 3080 | tf_op jit(solution)/shard_map/cond/branch_1_fun/ppermute | solution.py:291
  12.8 0.0 collective-permute-done.2
  12.8 0.9 %collective-permute-done.1 = f32[1,256]{1,0:T(1,128)S(1)} collective-permute-done((f32[1,256]{1,0:T(1,128)S(1)}, f32[1,256]{1,0:T(1,128)S(1)}, u32[]{:S(2)}, u32[]{:S(2)}) %collective-permute-start.1) | collective-permute-done | bytes 1056 | tf_op jit(solution)/shard_map/cond/branch_1_fun/ppermute | solution.py:291
  13.7 2.0 %collective-permute-done = f32[1,256]{1,0:T(1,128)S(1)} collective-permute-done((f32[1,256]{1,0:T(1,128)S(1)}, f32[1,256]{1,0:T(1,128)S(1)}, u32[]{:S(2)}, u32[]{:S(2)}) %collective-permute-start) | collective-permute-done | bytes 1056 | tf_op jit(solution)/shard_map/cond/branch_1_fun/ppermute | solution.py:291
  15.7 0.0 copy-start.1
  15.7 0.0 copy-start.3
  15.7 0.0 copy-start.4
  15.7 0.0 copy-start.5
  15.7 0.0 copy-start.6
  15.8 0.0 copy-start.7
  15.8 28.7 %all_to_all.10.in_ref = bf16[32,2,4,16,128]{4,3,2,1,0:T(8,128)(2,1)S(1)} all-to-all(bf16[32,2,4,16,128]{4,3,2,1,0:T(8,128)(2,1)S(1)} %get-tuple-element.15), channel_id=1, replica_groups=mesh['ctx'=32,'chan'=4,'section'=2] {'ctx'}, dimensions={0} | all-to-all | bytes 2097152 | tf_op jit(solution)/shard_map/all_to_all | solution.py:301
  44.5 0.0 copy-done.1
  44.5 0.0 copy-done.3
  44.5 0.0 copy-done.4
  44.5 0.0 copy-done.5
  44.5 0.0 copy-done.6
  44.5 0.0 copy-done.7
  44.5 2.8 %shard_map.114 = bf16[32,4,16,128]{3,2,1,0:T(8,128)(2,1)S(1)} custom-call(bf16[32,2,4,16,128]{4,3,2,1,0:T(8,128)(2,1)S(1)} %all_to_all.10.in_ref, bf16[4,512,256]{2,1,0:T(8,128)(2,1)S(1)} %copy-done.1, bf16[4,256,256]{2,1,0:T(8,128)(2,1)S(1)} %copy-done.3, bf16[256,256]{1,0:T(8,128)(2,1)S(1)} %copy-done.5, bf16[256,256]{1,0:T(8,128)(2,1)S(1)} %copy-done.4, ...), custom_call_target="tpu_custom_call" | custom-call | tf_op jit(solution)/shard_map/pallas_call | solution.py:302
  47.3 0.0 copy-start.2
  47.3 0.0 copy-start.8
  47.3 17.6 %all_to_all.11.conv_ref = bf16[32,4,16,128]{3,2,1,0:T(8,128)(2,1)S(1)} all-to-all(bf16[32,4,16,128]{3,2,1,0:T(8,128)(2,1)S(1)} %shard_map.114), channel_id=1, replica_groups=mesh['ctx'=32,'chan'=4,'section'=2] {'ctx'}, dimensions={0} | all-to-all | bytes 1048576 | tf_op jit(solution)/shard_map/all_to_all | solution.py:305
  64.9 0.0 copy-done.2
  64.9 0.0 copy-done.8
  64.9 0.5 shard_map.115
  65.4 1.3 %collective-permute-start.3 = (f32[3,256]{1,0:T(4,128)S(1)}, f32[3,256]{1,0:T(4,128)S(1)}, u32[]{:S(2)}, u32[]{:S(2)}) collective-permute-start(f32[3,256]{1,0:T(4,128)S(1)} %get-tuple-element.18), channel_id=1, source_target_pairs={{0,2},{2,0},{4,6},{6,4},{1,3},{3,1},{5,7},{7,5},{8,10},{10,8},{12,... | collective-permute-start | bytes 9224 | tf_op jit(solution)/shard_map/ppermute | solution.py:321
  66.7 1.2 %collective-permute-done.3 = f32[3,256]{1,0:T(4,128)S(1)} collective-permute-done((f32[3,256]{1,0:T(4,128)S(1)}, f32[3,256]{1,0:T(4,128)S(1)}, u32[]{:S(2)}, u32[]{:S(2)}) %collective-permute-start.3) | collective-permute-done | bytes 3104 | tf_op jit(solution)/shard_map/ppermute | solution.py:321
  67.9 2.8 %collective-permute-start.4 = (f32[3,256]{1,0:T(4,128)S(1)}, f32[3,256]{1,0:T(4,128)S(1)}, u32[]{:S(2)}, u32[]{:S(2)}) collective-permute-start(f32[3,256]{1,0:T(4,128)S(1)} %add.23), channel_id=1, source_target_pairs={{0,6},{2,4},{4,2},{6,0},{1,7},{3,5},{5,3},{7,1},{8,14},{10,12},{12... | collective-permute-start | bytes 9224 | tf_op jit(solution)/shard_map/ppermute | solution.py:321
  70.7 0.8 %shard_map.116 = bf16[256,1024]{1,0:T(8,128)(2,1)} custom-call(bf16[256,1024]{1,0:T(8,128)(2,1)S(1)} %get-tuple-element.17.in_ref), custom_call_target="tpu_custom_call" | custom-call | tf_op jit(solution)/shard_map/pallas_call | solution.py:312
  71.6 0.2 collective-permute-done.4
  71.7 0.6 slice_multiply_fusion
  (3 shorter events, 0.0 us)
Async XLA Ops:
  0.6 1.4 %copy-start = (bf16[256,1024]{1,0:T(8,128)(2,1)S(1)}, bf16[256,1024]{1,0:T(8,128)(2,1)}, u32[]{:S(2)}) copy-start(bf16[256,1024]{1,0:T(8,128)(2,1)} %sig_ref.3) | copy-start | bytes 1572868
  2.4 10.4 %collective-permute-start.2 = (f32[1,256]{1,0:T(1,128)S(1)}, f32[1,256]{1,0:T(1,128)S(1)}, u32[]{:S(2)}, u32[]{:S(2)}) collective-permute-start(f32[1,256]{1,0:T(1,128)S(1)} %param.1), channel_id=1, source_target_pairs={{1,7},{3,1},{5,3},{7,5},{9,15},{11,9},{13,11},{15,13},{17,23},{19,... | collective-permute-start | bytes 3080 | tf_op jit(solution)/shard_map/cond/branch_1_fun/ppermute | solution.py:291
  7.9 5.8 %collective-permute-start.1 = (f32[1,256]{1,0:T(1,128)S(1)}, f32[1,256]{1,0:T(1,128)S(1)}, u32[]{:S(2)}, u32[]{:S(2)}) collective-permute-start(f32[1,256]{1,0:T(1,128)S(1)} %param.1), channel_id=1, source_target_pairs={{1,5},{3,7},{5,1},{7,3},{9,13},{11,15},{13,9},{15,11},{17,21},{19,... | collective-permute-start | bytes 3080 | tf_op jit(solution)/shard_map/cond/branch_1_fun/ppermute | solution.py:291
  10.2 5.5 %collective-permute-start = (f32[1,256]{1,0:T(1,128)S(1)}, f32[1,256]{1,0:T(1,128)S(1)}, u32[]{:S(2)}, u32[]{:S(2)}) collective-permute-start(f32[1,256]{1,0:T(1,128)S(1)} %param.1), channel_id=1, source_target_pairs={{1,3},{3,5},{5,7},{7,1},{9,11},{11,13},{13,15},{15,9},{17,19},{19,... | collective-permute-start | bytes 3080 | tf_op jit(solution)/shard_map/cond/branch_1_fun/ppermute | solution.py:291
  15.7 28.8 %copy-start.1 = (bf16[4,512,256]{2,1,0:T(8,128)(2,1)S(1)}, bf16[4,512,256]{2,1,0:T(8,128)(2,1)}, u32[]{:S(2)}) copy-start(bf16[4,512,256]{2,1,0:T(8,128)(2,1)} %constant.20.clone.fo_ref) | copy-start | bytes 3145732
  15.7 28.8 %copy-start.3 = (bf16[4,256,256]{2,1,0:T(8,128)(2,1)S(1)}, bf16[4,256,256]{2,1,0:T(8,128)(2,1)}, u32[]{:S(2)}) copy-start(bf16[4,256,256]{2,1,0:T(8,128)(2,1)} %constant.21.clone.io_ref) | copy-start | bytes 1572868
  15.7 28.7 %copy-start.4 = (bf16[256,256]{1,0:T(8,128)(2,1)S(1)}, bf16[256,256]{1,0:T(8,128)(2,1)}, u32[]{:S(2)}) copy-start(bf16[256,256]{1,0:T(8,128)(2,1)} %constant.23.clone.ii_ref) | copy-start | bytes 393220
  15.7 28.7 %copy-start.5 = (bf16[256,256]{1,0:T(8,128)(2,1)S(1)}, bf16[256,256]{1,0:T(8,128)(2,1)}, u32[]{:S(2)}) copy-start(bf16[256,256]{1,0:T(8,128)(2,1)} %constant.22.clone.fi_ref) | copy-start | bytes 393220
  15.7 28.7 %copy-start.6 = (f32[64,128]{1,0:T(8,128)S(1)}, f32[64,128]{1,0:T(8,128)}, u32[]{:S(2)}) copy-start(f32[64,128]{1,0:T(8,128)} %constant.25.clone.sin_ref) | copy-start | bytes 98308
  15.8 28.7 %copy-start.7 = (f32[64,128]{1,0:T(8,128)S(1)}, f32[64,128]{1,0:T(8,128)}, u32[]{:S(2)}) copy-start(f32[64,128]{1,0:T(8,128)} %constant.24.clone.cos_ref) | copy-start | bytes 98308
  47.3 17.6 %copy-start.2 = (bf16[256,1024]{1,0:T(8,128)(2,1)S(1)}, bf16[256,1024]{1,0:T(8,128)(2,1)}, u32[]{:S(2)}) copy-start(bf16[256,1024]{1,0:T(8,128)(2,1)} %gate_ref.1) | copy-start | bytes 1572868
  47.3 17.6 %copy-start.8 = (f32[1024]{0:T(1024)S(1)}, f32[1024]{0:T(1024)}, u32[]{:S(2)}) copy-start(f32[1024]{0:T(1024)} %param.15) | copy-start | bytes 12292
  65.4 2.5 %collective-permute-start.3 = (f32[3,256]{1,0:T(4,128)S(1)}, f32[3,256]{1,0:T(4,128)S(1)}, u32[]{:S(2)}, u32[]{:S(2)}) collective-permute-start(f32[3,256]{1,0:T(4,128)S(1)} %get-tuple-element.18), channel_id=1, source_target_pairs={{0,2},{2,0},{4,6},{6,4},{1,3},{3,1},{5,7},{7,5},{8,10},{10,8},{12,... | collective-permute-start | bytes 9224 | tf_op jit(solution)/shard_map/ppermute | solution.py:321
  67.9 3.8 %collective-permute-start.4 = (f32[3,256]{1,0:T(4,128)S(1)}, f32[3,256]{1,0:T(4,128)S(1)}, u32[]{:S(2)}, u32[]{:S(2)}) collective-permute-start(f32[3,256]{1,0:T(4,128)S(1)} %add.23), channel_id=1, source_target_pairs={{0,6},{2,4},{4,2},{6,0},{1,7},{3,5},{5,3},{7,1},{8,14},{10,12},{12... | collective-permute-start | bytes 9224 | tf_op jit(solution)/shard_map/ppermute | solution.py:321
